TPU v7x, 256 devices: a whole 4x4x8 slice. The times are simulated.
256 devices in a mesh: dp: 64 (over y_lo, x, z), mp: 4 (over y_hi, core).
Axes of the slice: x: 4, y: 4 (y_hi: 2, y_lo: 2; y = y_hi * 2 + y_lo), z: 8, core: 2. Of those that a mesh axis runs over, the one named last changes fastest.
Arguments:
- queries: bfloat16 [8192, 4096], P('dp', 'mp'), may hold values from -1 to 1
- passages: bfloat16 [8192, 4096], P('dp', 'mp'), may hold values from -1 to 1
- row_lse: float32 [8192], P('dp'), may hold values from 10 to 11
- row_weight: float32 [8192], P('dp'), may hold values from 0.5 to 2
- positive: int32 [8192], P('dp'), may hold values from 0 to 8191, as said below
Outputs:
- query_grad: bfloat16 [8192, 4096], P('dp', 'mp')
- passage_grad: bfloat16 [8192, 4096], P('dp', 'mp')
Inputs may be any that keep to these rules, and one draw needn't show every extreme that they name: Each passage is the positive of exactly one query.
All inputs are finite; a program needn't handle non-finite values.
Results may differ from a plain program's by a relative error of at most 0.005.
Values may be sent and summed in bfloat16 or wider, within the bound.
No kernel may reach another device: no remote copies, remote signals or barrier semaphores. Data moves between devices by JAX's collectives and lax.ppermute only.
A program may use at most 128 MiB of HBM per device.

v0:
```python
import jax
import jax.numpy as jnp
from jax import lax
from jax.sharding import PartitionSpec as P

inv_temp = 50.0


def loss_weights(scores, lse_rows, weight_rows, target_rows):
    columns = jnp.arange(scores.shape[1], dtype=jnp.int32)
    is_positive = (columns[None, :] == target_rows[:, None]).astype(jnp.float32)
    return (
        weight_rows[:, None] * (jnp.exp(inv_temp * scores - lse_rows[:, None]) - is_positive)
    ).astype(jnp.bfloat16)


def on_device(queries, passages, row_lse, row_weight, positive):
    all_passages, all_queries = (
        lax.all_gather(passages, "dp", axis=0, tiled=True),
        lax.all_gather(queries, "dp", axis=0, tiled=True),
    )
    partial_value = lax.dot_general(
        queries, all_passages, (((1,), (1,)), ((), ())), preferred_element_type=jnp.float32
    )
    scores = lax.psum(partial_value, "mp")
    grads = loss_weights(scores, row_lse, row_weight, positive)
    query_grad = (
        inv_temp * jnp.dot(grads, all_passages, preferred_element_type=jnp.float32)
    ).astype(jnp.bfloat16)
    column_grads = lax.all_to_all(grads, "dp", split_axis=1, concat_axis=0, tiled=True)
    passage_sum = lax.dot_general(
        column_grads, all_queries, (((0,), (0,)), ((), ())), preferred_element_type=jnp.float32
    )
    passage_grad = (inv_temp * passage_sum).astype(jnp.bfloat16)
    return (query_grad, passage_grad)


def solution(mesh):
    return jax.shard_map(
        on_device,
        mesh=mesh,
        in_specs=(P("dp", "mp"), P("dp", "mp"), P("dp"), P("dp"), P("dp")),
        out_specs=(P("dp", "mp"), P("dp", "mp")),
        check_vma=False,
    )
```

profile of v0, /device:TPU:16, one launch (start us, length us, event | category | flops | bytes accessed | tf_op | source)
XLA Modules:
  0.0 832.1 jit_solution(10328774560216886188)
XLA Ops:
  7.2 0.0 all-gather.3.cloned.1.call-start
  7.2 0.7 all-gather.3.cloned.1.call-update
  7.9 0.0 all-reduce.2.cloned.1.call-start
  7.9 337.2 %all-gather.3.cloned.1.call-done = bf16[8192,1024]{1,0:T(8,128)(2,1)} async-done(((bf16[128,1024]{1,0:T(8,128)(2,1)}), bf16[8192,1024]{1,0:T(8,128)(2,1)}) %all-gather.3.cloned.1.call-update) | async-done | bytes 16777232 | tf_op jit(solution)/shard_map/all_gather | solution.py:19
  345.1 13.4 %fusion.2 = f32[128,8192]{1,0:T(8,128)} fusion(bf16[128,1024]{1,0:T(8,128)(2,1)} %param.5, bf16[8192,1024]{1,0:T(8,128)(2,1)} %all-gather.3.cloned.1.call-done), kind=kOutput, calls=%fused_computation.7 | convolution fusion | flops 2147483648 | bytes 21233664 | tf_op jit(solution)/shard_map/dot_general | solution.py:22
  358.5 0.0 copy-start
  358.5 0.0 copy-start.1
  358.5 0.0 copy-start.2
  358.5 0.0 all-reduce.2.cloned.1.call-update
  358.5 0.0 all-gather.5.cloned.1.call-start
  358.6 0.7 all-gather.5.cloned.1.call-update
  359.3 91.3 %all-reduce.2.cloned.1.call-done = f32[128,8192]{1,0:T(8,128)} async-done(((f32[128,8192]{1,0:T(8,128)}), f32[128,8192]{1,0:T(8,128)}) %all-reduce.2.cloned.1.call-update) | async-done | bytes 4194320 | tf_op jit(solution)/shard_map/psum | solution.py:25
  450.6 0.0 copy-done
  450.6 0.0 copy-done.1
  450.6 0.0 copy-done.2
  450.6 4.9 copy_bitcast_fusion
  455.5 12.7 %all-to-all-start = ((bf16[128,64,128]{2,0,1:T(8,128)(2,1)}), bf16[128,64,128]{2,0,1:T(8,128)(2,1)S(1)}, u32[]{:S(2)}, u32[]{:S(2)}) async-start(bf16[128,64,128]{2,0,1:T(8,128)(2,1)} %copy_bitcast_fusion), calls=%async_computation | async-start | bytes 4194304 | tf_op jit(solution)/shard_map/all_to_all | solution.py:30
  468.2 10.7 %fusion = bf16[128,1024]{1,0:T(8,128)(2,1)} fusion(bf16[8192,1024]{1,0:T(8,128)(2,1)} %all-gather.3.cloned.1.call-done, f32[128,8192]{1,0:T(8,128)} %all-reduce.2.cloned.1.call-done, s32[128]{0:T(128)S(1)} %copy-done, f32[128]{0:T(128)S(1)} %copy-done.1, f32[128]{0:T(128)S(1)} %copy-done.2), kind=kOutput, calls=%fused_computation.5 | convolution fusion | flops 2155085824 | bytes 21235200 | tf_op jit(solution)/shard_map/dot_general | solution.py:28
  478.9 337.8 %all-gather.5.cloned.1.call-done = bf16[8192,1024]{1,0:T(8,128)(2,1)} async-done(((bf16[128,1024]{1,0:T(8,128)(2,1)}), bf16[8192,1024]{1,0:T(8,128)(2,1)}) %all-gather.5.cloned.1.call-update) | async-done | bytes 16777232 | tf_op jit(solution)/shard_map/all_gather | solution.py:20
  816.7 0.0 all-to-all-done
  816.7 8.8 %fusion.1 = bf16[128,1024]{1,0:T(8,128)(2,1)} fusion(bf16[8192,128]{1,0:T(8,128)(2,1)S(1)} %bitcast.14, bf16[8192,1024]{1,0:T(8,128)(2,1)} %all-gather.5.cloned.1.call-done), kind=kOutput, calls=%fused_computation.6 | convolution fusion | flops 2147745792 | bytes 19136512 | tf_op jit(solution)/shard_map/dot_general | solution.py:31
Async XLA Ops:
  7.2 338.0 %all-gather.3.cloned.1.call-start = ((), (), s32[]{:S(2)}) async-start(), calls=%async_computation.1 | async-start | bytes 17039360 | tf_op jit(solution)/shard_map/all_gather | solution.py:19
  7.9 442.7 %all-reduce.2.cloned.1.call-start = ((), (), s32[]{:S(2)}) async-start(), calls=%async_computation.2 | async-start | bytes 8388608 | tf_op jit(solution)/shard_map/psum | solution.py:25
  358.5 92.1 %copy-start = (s32[128]{0:T(128)S(1)}, s32[128]{0:T(128)}, u32[]{:S(2)}) copy-start(s32[128]{0:T(128)} %param.9) | copy-start | bytes 1540
  358.5 92.1 %copy-start.1 = (f32[128]{0:T(128)S(1)}, f32[128]{0:T(128)}, u32[]{:S(2)}) copy-start(f32[128]{0:T(128)} %param.7) | copy-start | bytes 1540
  358.5 92.1 %copy-start.2 = (f32[128]{0:T(128)S(1)}, f32[128]{0:T(128)}, u32[]{:S(2)}) copy-start(f32[128]{0:T(128)} %param.8) | copy-start | bytes 1540
  358.5 458.2 %all-gather.5.cloned.1.call-start = ((), (), s32[]{:S(2)}) async-start(), calls=%async_computation.3 | async-start | bytes 17039360 | tf_op jit(solution)/shard_map/all_gather | solution.py:20
  455.5 361.2 %all-to-all-start = ((bf16[128,64,128]{2,0,1:T(8,128)(2,1)}), bf16[128,64,128]{2,0,1:T(8,128)(2,1)S(1)}, u32[]{:S(2)}, u32[]{:S(2)}) async-start(bf16[128,64,128]{2,0,1:T(8,128)(2,1)} %copy_bitcast_fusion), calls=%async_computation | async-start | bytes 4194304 | tf_op jit(solution)/shard_map/all_to_all | solution.py:30
Sparse Core Ops, SparseCore 0:
  9.8 335.2 all-gather.2
  358.6 91.8 all-reduce.1
  452.5 364.1 all-gather.4
where the time goes:
time: 832 us
  waiting for transfers between devices  768 us (92%)
  matrix products  32.9 us (4%)
  between operations  13.8 us (2%)
  starting transfers between devices  12.9 us (2%)
    all_gather x1, waiting for transfers between devices, on_device(): lax.all_gather(queries, 'dp', axis=0, tiled=True)  338 us
    all_gather x1, waiting for transfers between devices, on_device(): lax.all_gather(passages, 'dp', axis=0, tiled=True)  337 us
    psum x1, waiting for transfers between devices, on_device(): scores = lax.psum(partial_value, 'mp')  91.3 us
  transfers between devices with their start and end apart: 4, of which 3 were waited for; matrix products, arithmetic and copies ran while one was open for 2% of the time, Pallas kernels for 0%

commit v1 on v0

v1 whole, which is shorter than its diff:
```python
import jax
import jax.numpy as jnp
from jax import lax
from jax.sharding import Mesh, PartitionSpec as P

inv_temp = 50.0
ROWS_SPEC = ("yl", "x", "z")
FEATURES_SPEC = ("yh", "c")
PLANE = ("yl", "x", "yh", "c")
bf16, f32 = jnp.bfloat16, jnp.float32
NEAR, FAR = (1, 3), (3, 1)


def flip(value, axis, bits):
    pairs = []
    for yl in range(2):
        for x in range(4):
            for yh in range(2):
                for core in range(2):
                    x_to, y_to = x, 2 * yh + yl
                    if axis == "x":
                        x_to ^= bits[core]
                    else:
                        y_to ^= bits[core]
                    target = (((y_to % 2) * 4 + x_to) * 2 + y_to // 2) * 2 + core
                    pairs.append((((yl * 4 + x) * 2 + yh) * 2 + core, target))
    return lax.ppermute(value, PLANE, pairs)


def shift(value, step):
    return lax.ppermute(value, "z", [(i, (i + step) % 8) for i in range(8)])


def gather_four(value, axis, core):
    rows = value.shape[0]
    near = flip(value, axis, NEAR)
    far = flip(jnp.concatenate([value, near]), axis, FAR)
    one = jnp.where(core == 0, near, far[:rows])
    three = jnp.where(core == 0, far[:rows], near)
    return [value, one, far[rows:], three]


def scatter_four(parts, axis, core):
    own, one, two, three = parts
    rows = own.shape[0]
    near = jnp.where(core == 0, one, three)
    far = jnp.where(core == 0, three, one)
    got = flip(jnp.concatenate([far, two]).astype(bf16), axis, FAR)
    last = flip((near + got[rows:]).astype(bf16), axis, NEAR)
    return own + got[:rows] + last


def gather_ring(value):
    half = value.shape[0] // 2
    blocks = [value] + [None] * 7
    up = down = value
    for step in range(1, 4):
        up, down = shift(up, 1), shift(down, -1)
        blocks[8 - step], blocks[step] = up, down
    blocks[4] = jnp.concatenate([shift(up[:half], 1), shift(down[half:], -1)])
    return blocks


def scatter_ring(parts):
    half = parts[0].shape[0] // 2
    up = shift(parts[4][:half].astype(bf16), 1)
    down = shift(parts[4][half:].astype(bf16), -1)
    up = jnp.concatenate([parts[3][:half] + up, parts[3][half:]]).astype(bf16)
    down = jnp.concatenate([parts[5][:half], parts[5][half:] + down]).astype(bf16)
    up, down = shift(up, 1), shift(down, -1)
    for step in (2, 1):
        up = shift((parts[step] + up).astype(bf16), 1)
        down = shift((parts[8 - step] + down).astype(bf16), -1)
    return parts[0] + up + down


def dot(a, b, contract):
    return lax.dot_general(a, b, (contract, ((), ())), preferred_element_type=f32)


def thirds(value):
    high = lax.reduce_precision(value, 8, 7)
    middle = lax.reduce_precision(value - high, 8, 7)
    return [high, middle, value - high - middle]


def on_device(queries, passages, row_lse, row_weight, positive):
    x, z, yl, yh, core = (lax.axis_index(a) for a in ("x", "z", "yl", "yh", "c"))
    rows, width = queries.shape
    half = rows // 2

    passage_own = lax.dynamic_slice_in_dim(passages, yh * half, half, 0)
    passage_away = lax.dynamic_slice_in_dim(passages, (1 - yh) * half, half, 0)
    passage_back = flip(passage_away, "y", (2, 2))

    target = [(positive // 128).astype(f32), (positive % 128).astype(f32)]
    stats = jnp.stack(thirds(row_lse) + thirds(row_weight) + target, axis=1).astype(bf16)
    loaded = jnp.concatenate([queries, jnp.pad(stats, ((0, 0), (0, 120)))], axis=1)

    first = gather_four(jnp.concatenate(gather_four(loaded[:half], "x", core)), "y", core)
    second = gather_four(jnp.concatenate(gather_four(loaded[half:], "y", core)), "x", core)
    ring = gather_ring(jnp.concatenate([passage_own, passage_back]))
    p_same = jnp.concatenate([b[:half] for b in ring])
    p_other = jnp.concatenate([b[half:] for b in ring])

    q_same = [jnp.concatenate(first[:2]), jnp.concatenate([b[:rows] for b in second])]
    q_other = [jnp.concatenate(first[2:]), jnp.concatenate([b[rows:] for b in second])]
    stats = [q[:, width:].astype(f32) for q in q_same]
    q_same = [q[:, :width] for q in q_same]
    q_other = [q[:, :width] for q in q_other]

    place = jnp.arange(8 * half, dtype=jnp.int32)
    owner = (yl * 4 + x) * 8 + (z + place // half) % 8
    column = owner * rows + yh * half + place % half
    grads = []
    for same, other, stat in zip(q_same, q_other, stats):
        partial_value = dot(same, p_same, ((1,), (1,))) + dot(other, p_other, ((1,), (1,)))
        scores = partial_value + lax.ppermute(partial_value, "c", [(0, 1), (1, 0)])
        lse = stat[:, 0:1] + stat[:, 1:2] + stat[:, 2:3]
        weight = stat[:, 3:4] + stat[:, 4:5] + stat[:, 5:6]
        target = (stat[:, 6:7] * 128 + stat[:, 7:8]).astype(jnp.int32)
        is_positive = (column[None, :] == target).astype(f32)
        grads.append((weight * (jnp.exp(inv_temp * scores - lse) - is_positive)).astype(bf16))

    v_same = dot(grads[0], q_same[0], ((0,), (0,))) + dot(grads[1], q_same[1], ((0,), (0,)))
    v_other = dot(grads[0], q_other[0], ((0,), (0,))) + dot(grads[1], q_other[1], ((0,), (0,)))
    parts = [
        jnp.concatenate([v_same[i * half : (i + 1) * half], v_other[i * half : (i + 1) * half]]) for i in range(8)
    ]
    passage_sum = (inv_temp * scatter_ring(parts)).astype(bf16)
    passage_own = passage_sum[:half]
    passage_back = flip(passage_sum[half:], "y", (2, 2))
    passage_grad = jnp.where(
        yh == 0,
        jnp.concatenate([passage_own, passage_back]),
        jnp.concatenate([passage_back, passage_own]),
    )

    block = 4 * half
    w_same = [dot(g, p_same, ((1,), (0,))) for g in grads]
    w_other = [dot(g, p_other, ((1,), (0,))) for g in grads]
    first = [w_same[0][:block], w_same[0][block:], w_other[0][:block], w_other[0][block:]]
    second = [
        jnp.concatenate([w_same[1][i * rows : (i + 1) * rows], w_other[1][i * rows : (i + 1) * rows]])
        for i in range(4)
    ]
    first = scatter_four(first, "y", core)
    second = scatter_four(second, "x", core)
    first = scatter_four([first[i * half : (i + 1) * half] for i in range(4)], "x", core)
    second = scatter_four([second[i * half : (i + 1) * half] for i in range(4)], "y", core)
    query_grad = (inv_temp * jnp.concatenate([first, second])).astype(bf16)
    return query_grad, passage_grad


def solution(mesh):
    split = Mesh(mesh.devices.reshape(2, 4, 8, 2, 2), ("yl", "x", "z", "yh", "c"))
    matrix, vector = P(ROWS_SPEC, FEATURES_SPEC), P(ROWS_SPEC)
    return jax.shard_map(
        on_device,
        mesh=split,
        in_specs=(matrix, matrix, vector, vector, vector),
        out_specs=(matrix, matrix),
        check_vma=False,
    )
```

time: 832 us -> 145 us (0.17)
  the two profiles are of different devices: /device:TPU:16 before, /device:TPU:2 now
where the time goes in v1:
time: 145 us
  starting transfers between devices  57.2 us (39%)
  waiting for transfers between devices  55 us (38%)
  other arithmetic  12.1 us (8%)
  matrix products  10.8 us (7%)
  local copies, waits for them, and re-layouts  8.6 us (6%)
    ppermute x16, starting transfers between devices, shift(): return lax.ppermute(value, 'z', [(i, (i + step) % 8) for i in range(8)])  32 us
    ppermute x18, waiting for transfers between devices, flip(): return lax.ppermute(value, PLANE, pairs)  28.6 us
    ppermute x16, waiting for transfers between devices, shift(): return lax.ppermute(value, 'z', [(i, (i + step) % 8) for i in range(8)])  25.6 us
    ppermute x18, starting transfers between devices, flip(): return lax.ppermute(value, PLANE, pairs)  24.7 us
    dot_general x12, matrix products, dot(): lax.dot_general(a, b, (contract, ((), ())), preferred_element_type=f32)  10.8 us
    unnamed x49, local copies, waits for them, and re-layouts  7.14 us
  transfers between devices with their start and end apart: 36, of which 15 were waited for; matrix products, arithmetic and copies ran while one was open for 13% of the time, Pallas kernels for 0%

profile of v1, /device:TPU:2, one launch (start us, length us, event | category | flops | bytes accessed | tf_op | source)
XLA Modules:
  0.0 145.1 jit_solution(10009747332405267131)
XLA Ops:
  1.6 3.3 %collective-permute-start.4 = (bf16[64,1024]{1,0:T(8,128)(2,1)S(1)}, bf16[64,1024]{1,0:T(8,128)(2,1)S(1)}, u32[]{:S(2)}, u32[]{:S(2)}) collective-permute-start(bf16[64,1024]{1,0:T(8,128)(2,1)S(1)} %get-tuple-element.79), channel_id=1, source_target_pairs={{0,2},{1,3},{2,0},{3,1},{32,34},{33,35},{34,32},{35,33},{64,66},{6... | collective-permute-start | bytes 393224 | tf_op jit(solution)/shard_map/ppermute | solution.py:27
  9.4 5.9 %collective-permute-start.5 = (bf16[128,1024]{1,0:T(8,128)(2,1)S(1)}, bf16[128,1024]{1,0:T(8,128)(2,1)S(1)}, u32[]{:S(2)}, u32[]{:S(2)}) collective-permute-start(bf16[128,1024]{1,0:T(8,128)(2,1)S(1)} %pad_maximum_fusion.11), channel_id=1, source_target_pairs={{0,28},{4,0},{8,4},{12,8},{16,12},{20,16},{24,20},{28,24},{1,29},{... | collective-permute-start | bytes 786440 | tf_op jit(solution)/shard_map/ppermute | solution.py:31
  15.4 2.2 %collective-permute-start.19 = (bf16[128,1152]{1,0:T(8,128)(2,1)S(1)}, bf16[128,1152]{1,0:T(8,128)(2,1)S(1)}, u32[]{:S(2)}, u32[]{:S(2)}) collective-permute-start(bf16[128,1152]{1,0:T(8,128)(2,1)S(1)} %pad_maximum_fusion.10), channel_id=1, source_target_pairs={{0,130},{1,129},{2,128},{3,131},{32,162},{33,161},{34,160},{35,163... | collective-permute-start | bytes 884744 | tf_op jit(solution)/shard_map/ppermute | solution.py:27
  17.7 1.6 %collective-permute-start.1 = (bf16[128,1152]{1,0:T(8,128)(2,1)S(1)}, bf16[128,1152]{1,0:T(8,128)(2,1)S(1)}, u32[]{:S(2)}, u32[]{:S(2)}) collective-permute-start(bf16[128,1152]{1,0:T(8,128)(2,1)S(1)} %pad_maximum_fusion.9), channel_id=1, source_target_pairs={{0,96},{1,33},{2,98},{3,35},{32,64},{33,1},{34,66},{35,3},{64,32},... | collective-permute-start | bytes 884744 | tf_op jit(solution)/shard_map/ppermute | solution.py:27
  19.2 2.1 %collective-permute-done.5 = bf16[128,1024]{1,0:T(8,128)(2,1)S(1)} collective-permute-done((bf16[128,1024]{1,0:T(8,128)(2,1)S(1)}, bf16[128,1024]{1,0:T(8,128)(2,1)S(1)}, u32[]{:S(2)}, u32[]{:S(2)}) %collective-permute-start.5) | collective-permute-done | bytes 262176 | tf_op jit(solution)/shard_map/ppermute | solution.py:31
  21.4 3.7 %collective-permute-start.6 = (bf16[128,1024]{1,0:T(8,128)(2,1)S(1)}, bf16[128,1024]{1,0:T(8,128)(2,1)S(1)}, u32[]{:S(2)}, u32[]{:S(2)}) collective-permute-start(bf16[128,1024]{1,0:T(8,128)(2,1)S(1)} %collective-permute-done.5), channel_id=1, source_target_pairs={{0,28},{4,0},{8,4},{12,8},{16,12},{20,16},{24,20},{28,24},{1,29},{... | collective-permute-start | bytes 786440 | tf_op jit(solution)/shard_map/ppermute | solution.py:31
  25.8 1.4 copy.34
  28.4 1.9 %collective-permute-start.20 = (bf16[256,1152]{1,0:T(8,128)(2,1)S(1)}, bf16[256,1152]{1,0:T(8,128)(2,1)S(1)}, u32[]{:S(2)}, u32[]{:S(2)}) collective-permute-start(bf16[256,1152]{1,0:T(8,128)(2,1)S(1)} %pad_maximum_fusion.8), channel_id=1, source_target_pairs={{0,32},{1,97},{2,34},{3,99},{32,0},{33,65},{34,2},{35,67},{64,96},... | collective-permute-start | bytes 1769480 | tf_op jit(solution)/shard_map/ppermute | solution.py:27
  30.5 3.5 %collective-permute-start.7 = (bf16[128,1024]{1,0:T(8,128)(2,1)S(1)}, bf16[128,1024]{1,0:T(8,128)(2,1)S(1)}, u32[]{:S(2)}, u32[]{:S(2)}) collective-permute-start(bf16[128,1024]{1,0:T(8,128)(2,1)S(1)} %collective-permute-done.6), channel_id=1, source_target_pairs={{0,28},{4,0},{8,4},{12,8},{16,12},{20,16},{24,20},{28,24},{1,29},{... | collective-permute-start | bytes 786440 | tf_op jit(solution)/shard_map/ppermute | solution.py:31
  34.1 1.3 copy.28
  35.4 2.9 %collective-permute-done.7 = bf16[128,1024]{1,0:T(8,128)(2,1)S(1)} collective-permute-done((bf16[128,1024]{1,0:T(8,128)(2,1)S(1)}, bf16[128,1024]{1,0:T(8,128)(2,1)S(1)}, u32[]{:S(2)}, u32[]{:S(2)}) %collective-permute-start.7) | collective-permute-done | bytes 262176 | tf_op jit(solution)/shard_map/ppermute | solution.py:31
  38.4 3.8 %collective-permute-start.12 = (bf16[64,1024]{1,0:T(8,128)(2,1)S(1)}, bf16[64,1024]{1,0:T(8,128)(2,1)S(1)}, u32[]{:S(2)}, u32[]{:S(2)}) collective-permute-start(bf16[64,1024]{1,0:T(8,128)(2,1)S(1)} %get-tuple-element.74), channel_id=1, source_target_pairs={{0,28},{4,0},{8,4},{12,8},{16,12},{20,16},{24,20},{28,24},{1,29},{... | collective-permute-start | bytes 393224 | tf_op jit(solution)/shard_map/ppermute | solution.py:31
  42.1 2.9 %collective-permute-done.10 = bf16[128,1024]{1,0:T(8,128)(2,1)S(1)} collective-permute-done((bf16[128,1024]{1,0:T(8,128)(2,1)S(1)}, bf16[128,1024]{1,0:T(8,128)(2,1)S(1)}, u32[]{:S(2)}, u32[]{:S(2)}) %collective-permute-start.10) | collective-permute-done | bytes 262176 | tf_op jit(solution)/shard_map/ppermute | solution.py:31
  45.5 1.3 collective-permute-start.3
  46.9 4.5 %collective-permute-done.11 = bf16[64,1024]{1,0:T(8,128)(2,1)S(1)} collective-permute-done((bf16[64,1024]{1,0:T(8,128)(2,1)S(1)}, bf16[64,1024]{1,0:T(8,128)(2,1)S(1)}, u32[]{:S(2)}, u32[]{:S(2)}) %collective-permute-start.11) | collective-permute-done | bytes 131104 | tf_op jit(solution)/shard_map/ppermute | solution.py:31
  51.5 10.1 %collective-permute-done.21 = bf16[512,1152]{1,0:T(8,128)(2,1)S(1)} collective-permute-done((bf16[512,1152]{1,0:T(8,128)(2,1)S(1)}, bf16[512,1152]{1,0:T(8,128)(2,1)S(1)}, u32[]{:S(2)}, u32[]{:S(2)}) %collective-permute-start.21) | collective-permute-done | bytes 1179680 | tf_op jit(solution)/shard_map/ppermute | solution.py:27
  63.0 1.7 %convolution_add_fusion.2 = f32[512,512]{1,0:T(8,128)} fusion(f32[512,512]{1,0:T(8,128)S(1)} %fusion.4, bf16[512,1024]{1,0:T(8,128)(2,1)S(1)} %get-tuple-element.66, bf16[512,1152]{1,0:T(8,128)(2,1)S(1)} %get-tuple-element.51), kind=kOutput, calls=%fused_computation.2 | convolution fusion | flops 537133056 | bytes 4194304 | tf_op jit(solution)/shard_map/dot_general | solution.py:78
  66.2 1.7 %convolution_add_fusion.3 = f32[512,512]{1,0:T(8,128)} fusion(f32[512,512]{1,0:T(8,128)S(1)} %fusion.11, bf16[512,1024]{1,0:T(8,128)(2,1)S(1)} %get-tuple-element.66, bf16[512,1152]{1,0:T(8,128)(2,1)S(1)} %get-tuple-element.36), kind=kOutput, calls=%fused_computation.3 | convolution fusion | flops 537133056 | bytes 4194304 | tf_op jit(solution)/shard_map/dot_general | solution.py:78
  71.0 2.6 %multiply_convert_fusion.1 = (bf16[512,512]{1,0:T(8,128)(2,1)S(1)}, bf16[512,512]{1,0:T(8,128)(2,1)S(1)}) fusion(f32[512,512]{1,0:T(8,128)} %convolution_add_fusion.3, f32[512,512]{1,0:T(8,128)} %collective-permute-done.13, s32[512]{0:T(512)S(1)} %fusion.43, f32[512]{0:T(512)S(1)} %get-tuple-element.3, f32[512]{0:T(512)S(1)} %get-tuple-element.2, ...), kind=kLoop, calls=%fused_computation.19 | loop fusion | flops 4194304 | bytes 5257216 | tf_op jit(solution)/shard_map/convert_element_type | solution.py:123
  81.2 3.5 %collective-permute-start.31 = (bf16[64,1024]{1,0:T(8,128)(2,1)S(1)}, bf16[64,1024]{1,0:T(8,128)(2,1)S(1)}, u32[]{:S(2)}, u32[]{:S(2)}) collective-permute-start(bf16[64,1024]{1,0:T(8,128)(2,1)S(1)} %get-tuple-element.46), channel_id=1, source_target_pairs={{0,28},{4,0},{8,4},{12,8},{16,12},{20,16},{24,20},{28,24},{1,29},{... | collective-permute-start | bytes 393224 | tf_op jit(solution)/shard_map/ppermute | solution.py:31
  88.2 3.8 %collective-permute-start.32 = (bf16[128,1024]{1,0:T(8,128)(2,1)S(1)}, bf16[128,1024]{1,0:T(8,128)(2,1)S(1)}, u32[]{:S(2)}, u32[]{:S(2)}) collective-permute-start(bf16[128,1024]{1,0:T(8,128)(2,1)S(1)} %pad_maximum_fusion.15), channel_id=1, source_target_pairs={{0,28},{4,0},{8,4},{12,8},{16,12},{20,16},{24,20},{28,24},{1,29},{... | collective-permute-start | bytes 786440 | tf_op jit(solution)/shard_map/ppermute | solution.py:31
  92.2 4.6 %collective-permute-done.28 = bf16[128,1024]{1,0:T(8,128)(2,1)S(1)} collective-permute-done((bf16[128,1024]{1,0:T(8,128)(2,1)S(1)}, bf16[128,1024]{1,0:T(8,128)(2,1)S(1)}, u32[]{:S(2)}, u32[]{:S(2)}) %collective-permute-start.28) | collective-permute-done | bytes 262176 | tf_op jit(solution)/shard_map/ppermute | solution.py:31
  97.3 3.8 %collective-permute-start.33 = (bf16[128,1024]{1,0:T(8,128)(2,1)S(1)}, bf16[128,1024]{1,0:T(8,128)(2,1)S(1)}, u32[]{:S(2)}, u32[]{:S(2)}) collective-permute-start(bf16[128,1024]{1,0:T(8,128)(2,1)S(1)} %fusion.20), channel_id=1, source_target_pairs={{0,28},{4,0},{8,4},{12,8},{16,12},{20,16},{24,20},{28,24},{1,29},{... | collective-permute-start | bytes 786440 | tf_op jit(solution)/shard_map/ppermute | solution.py:31
  101.2 4.2 %collective-permute-done.29 = bf16[128,1024]{1,0:T(8,128)(2,1)S(1)} collective-permute-done((bf16[128,1024]{1,0:T(8,128)(2,1)S(1)}, bf16[128,1024]{1,0:T(8,128)(2,1)S(1)}, u32[]{:S(2)}, u32[]{:S(2)}) %collective-permute-start.29) | collective-permute-done | bytes 262176 | tf_op jit(solution)/shard_map/ppermute | solution.py:31
  105.6 3.6 %collective-permute-start.34 = (bf16[128,1024]{1,0:T(8,128)(2,1)S(1)}, bf16[128,1024]{1,0:T(8,128)(2,1)S(1)}, u32[]{:S(2)}, u32[]{:S(2)}) collective-permute-start(bf16[128,1024]{1,0:T(8,128)(2,1)S(1)} %fusion.19), channel_id=1, source_target_pairs={{0,28},{4,0},{8,4},{12,8},{16,12},{20,16},{24,20},{28,24},{1,29},{... | collective-permute-start | bytes 786440 | tf_op jit(solution)/shard_map/ppermute | solution.py:31
  110.6 2.5 %collective-permute-done.30 = bf16[128,1024]{1,0:T(8,128)(2,1)S(1)} collective-permute-done((bf16[128,1024]{1,0:T(8,128)(2,1)S(1)}, bf16[128,1024]{1,0:T(8,128)(2,1)S(1)}, u32[]{:S(2)}, u32[]{:S(2)}) %collective-permute-start.30) | collective-permute-done | bytes 262176 | tf_op jit(solution)/shard_map/ppermute | solution.py:31
  113.3 3.0 %collective-permute-start.35 = (bf16[64,1024]{1,0:T(8,128)(2,1)S(1)}, bf16[64,1024]{1,0:T(8,128)(2,1)S(1)}, u32[]{:S(2)}, u32[]{:S(2)}) collective-permute-start(bf16[64,1024]{1,0:T(8,128)(2,1)S(1)} %get-tuple-element.65), channel_id=1, source_target_pairs={{0,2},{1,3},{2,0},{3,1},{32,34},{33,35},{34,32},{35,33},{64,66},{6... | collective-permute-start | bytes 393224 | tf_op jit(solution)/shard_map/ppermute | solution.py:27
  116.6 4.8 %collective-permute-start.24 = (bf16[256,1024]{1,0:T(8,128)(2,1)S(1)}, bf16[256,1024]{1,0:T(8,128)(2,1)S(1)}, u32[]{:S(2)}, u32[]{:S(2)}) collective-permute-start(bf16[256,1024]{1,0:T(8,128)(2,1)S(1)} %add_convert_fusion), channel_id=1, source_target_pairs={{0,32},{1,97},{2,34},{3,99},{32,0},{33,65},{34,2},{35,67},{64,96},... | collective-permute-start | bytes 1572872 | tf_op jit(solution)/shard_map/ppermute | solution.py:27
  121.8 9.4 %collective-permute-done.24 = bf16[256,1024]{1,0:T(8,128)(2,1)S(1)} collective-permute-done((bf16[256,1024]{1,0:T(8,128)(2,1)S(1)}, bf16[256,1024]{1,0:T(8,128)(2,1)S(1)}, u32[]{:S(2)}, u32[]{:S(2)}) %collective-permute-start.24) | collective-permute-done | bytes 524320 | tf_op jit(solution)/shard_map/ppermute | solution.py:27
  133.2 1.8 %collective-permute-start.17 = (bf16[64,1024]{1,0:T(8,128)(2,1)S(1)}, bf16[64,1024]{1,0:T(8,128)(2,1)S(1)}, u32[]{:S(2)}, u32[]{:S(2)}) collective-permute-start(bf16[64,1024]{1,0:T(8,128)(2,1)S(1)} %add_convert_fusion.3), channel_id=1, source_target_pairs={{0,32},{1,97},{2,34},{3,99},{32,0},{33,65},{34,2},{35,67},{64,96},... | collective-permute-start | bytes 393224 | tf_op jit(solution)/shard_map/ppermute | solution.py:27
  135.0 4.2 %collective-permute-done.25 = bf16[128,1024]{1,0:T(8,128)(2,1)S(1)} collective-permute-done((bf16[128,1024]{1,0:T(8,128)(2,1)S(1)}, bf16[128,1024]{1,0:T(8,128)(2,1)S(1)}, u32[]{:S(2)}, u32[]{:S(2)}) %collective-permute-start.25) | collective-permute-done | bytes 262176 | tf_op jit(solution)/shard_map/ppermute | solution.py:27
  139.4 4.9 %collective-permute-done.26 = bf16[64,1024]{1,0:T(8,128)(2,1)S(1)} collective-permute-done((bf16[64,1024]{1,0:T(8,128)(2,1)S(1)}, bf16[64,1024]{1,0:T(8,128)(2,1)S(1)}, u32[]{:S(2)}, u32[]{:S(2)}) %collective-permute-start.26) | collective-permute-done | bytes 131104 | tf_op jit(solution)/shard_map/ppermute | solution.py:27
  (166 shorter events, 31.1 us)
Async XLA Ops:
  1.6 7.7 %collective-permute-start.4 = (bf16[64,1024]{1,0:T(8,128)(2,1)S(1)}, bf16[64,1024]{1,0:T(8,128)(2,1)S(1)}, u32[]{:S(2)}, u32[]{:S(2)}) collective-permute-start(bf16[64,1024]{1,0:T(8,128)(2,1)S(1)} %get-tuple-element.79), channel_id=1, source_target_pairs={{0,2},{1,3},{2,0},{3,1},{32,34},{33,35},{34,32},{35,33},{64,66},{6... | collective-permute-start | bytes 393224 | tf_op jit(solution)/shard_map/ppermute | solution.py:27
  8.1 7.2 %collective-permute-start.18 = (bf16[64,1152]{1,0:T(8,128)(2,1)S(1)}, bf16[64,1152]{1,0:T(8,128)(2,1)S(1)}, u32[]{:S(2)}, u32[]{:S(2)}) collective-permute-start(bf16[64,1152]{1,0:T(8,128)(2,1)S(1)} %get-tuple-element.60), channel_id=1, source_target_pairs={{0,128},{1,131},{2,130},{3,129},{32,160},{33,163},{34,162},{35,161... | collective-permute-start | bytes 442376 | tf_op jit(solution)/shard_map/ppermute | solution.py:27
  8.8 8.8 %collective-permute-start = (bf16[64,1152]{1,0:T(8,128)(2,1)S(1)}, bf16[64,1152]{1,0:T(8,128)(2,1)S(1)}, u32[]{:S(2)}, u32[]{:S(2)}) collective-permute-start(bf16[64,1152]{1,0:T(8,128)(2,1)S(1)} %get-tuple-element.57), channel_id=1, source_target_pairs={{0,32},{1,97},{2,34},{3,99},{32,0},{33,65},{34,2},{35,67},{64,96},... | collective-permute-start | bytes 442376 | tf_op jit(solution)/shard_map/ppermute | solution.py:27
  9.4 12.0 %collective-permute-start.5 = (bf16[128,1024]{1,0:T(8,128)(2,1)S(1)}, bf16[128,1024]{1,0:T(8,128)(2,1)S(1)}, u32[]{:S(2)}, u32[]{:S(2)}) collective-permute-start(bf16[128,1024]{1,0:T(8,128)(2,1)S(1)} %pad_maximum_fusion.11), channel_id=1, source_target_pairs={{0,28},{4,0},{8,4},{12,8},{16,12},{20,16},{24,20},{28,24},{1,29},{... | collective-permute-start | bytes 786440 | tf_op jit(solution)/shard_map/ppermute | solution.py:31
  15.3 9.8 %collective-permute-start.8 = (bf16[128,1024]{1,0:T(8,128)(2,1)S(1)}, bf16[128,1024]{1,0:T(8,128)(2,1)S(1)}, u32[]{:S(2)}, u32[]{:S(2)}) collective-permute-start(bf16[128,1024]{1,0:T(8,128)(2,1)S(1)} %pad_maximum_fusion.11), channel_id=1, source_target_pairs={{0,4},{4,8},{8,12},{12,16},{16,20},{20,24},{24,28},{28,0},{1,5},{5... | collective-permute-start | bytes 786440 | tf_op jit(solution)/shard_map/ppermute | solution.py:31
  15.4 9.7 %collective-permute-start.19 = (bf16[128,1152]{1,0:T(8,128)(2,1)S(1)}, bf16[128,1152]{1,0:T(8,128)(2,1)S(1)}, u32[]{:S(2)}, u32[]{:S(2)}) collective-permute-start(bf16[128,1152]{1,0:T(8,128)(2,1)S(1)} %pad_maximum_fusion.10), channel_id=1, source_target_pairs={{0,130},{1,129},{2,128},{3,131},{32,162},{33,161},{34,160},{35,163... | collective-permute-start | bytes 884744 | tf_op jit(solution)/shard_map/ppermute | solution.py:27
  17.7 12.6 %collective-permute-start.1 = (bf16[128,1152]{1,0:T(8,128)(2,1)S(1)}, bf16[128,1152]{1,0:T(8,128)(2,1)S(1)}, u32[]{:S(2)}, u32[]{:S(2)}) collective-permute-start(bf16[128,1152]{1,0:T(8,128)(2,1)S(1)} %pad_maximum_fusion.9), channel_id=1, source_target_pairs={{0,96},{1,33},{2,98},{3,35},{32,64},{33,1},{34,66},{35,3},{64,32},... | collective-permute-start | bytes 884744 | tf_op jit(solution)/shard_map/ppermute | solution.py:27
  21.4 9.1 %collective-permute-start.6 = (bf16[128,1024]{1,0:T(8,128)(2,1)S(1)}, bf16[128,1024]{1,0:T(8,128)(2,1)S(1)}, u32[]{:S(2)}, u32[]{:S(2)}) collective-permute-start(bf16[128,1024]{1,0:T(8,128)(2,1)S(1)} %collective-permute-done.5), channel_id=1, source_target_pairs={{0,28},{4,0},{8,4},{12,8},{16,12},{20,16},{24,20},{28,24},{1,29},{... | collective-permute-start | bytes 786440 | tf_op jit(solution)/shard_map/ppermute | solution.py:31
  25.1 10.4 %collective-permute-start.9 = (bf16[128,1024]{1,0:T(8,128)(2,1)S(1)}, bf16[128,1024]{1,0:T(8,128)(2,1)S(1)}, u32[]{:S(2)}, u32[]{:S(2)}) collective-permute-start(bf16[128,1024]{1,0:T(8,128)(2,1)S(1)} %collective-permute-done.8), channel_id=1, source_target_pairs={{0,4},{4,8},{8,12},{12,16},{16,20},{20,24},{24,28},{28,0},{1,5},{5... | collective-permute-start | bytes 786440 | tf_op jit(solution)/shard_map/ppermute | solution.py:31
  28.4 16.8 %collective-permute-start.20 = (bf16[256,1152]{1,0:T(8,128)(2,1)S(1)}, bf16[256,1152]{1,0:T(8,128)(2,1)S(1)}, u32[]{:S(2)}, u32[]{:S(2)}) collective-permute-start(bf16[256,1152]{1,0:T(8,128)(2,1)S(1)} %pad_maximum_fusion.8), channel_id=1, source_target_pairs={{0,32},{1,97},{2,34},{3,99},{32,0},{33,65},{34,2},{35,67},{64,96},... | collective-permute-start | bytes 1769480 | tf_op jit(solution)/shard_map/ppermute | solution.py:27
  30.5 7.8 %collective-permute-start.7 = (bf16[128,1024]{1,0:T(8,128)(2,1)S(1)}, bf16[128,1024]{1,0:T(8,128)(2,1)S(1)}, u32[]{:S(2)}, u32[]{:S(2)}) collective-permute-start(bf16[128,1024]{1,0:T(8,128)(2,1)S(1)} %collective-permute-done.6), channel_id=1, source_target_pairs={{0,28},{4,0},{8,4},{12,8},{16,12},{20,16},{24,20},{28,24},{1,29},{... | collective-permute-start | bytes 786440 | tf_op jit(solution)/shard_map/ppermute | solution.py:31
  34.0 11.4 %collective-permute-start.2 = (bf16[256,1152]{1,0:T(8,128)(2,1)S(1)}, bf16[256,1152]{1,0:T(8,128)(2,1)S(1)}, u32[]{:S(2)}, u32[]{:S(2)}) collective-permute-start(bf16[256,1152]{1,0:T(8,128)(2,1)S(1)} %pad_maximum_fusion.7), channel_id=1, source_target_pairs={{0,128},{1,131},{2,130},{3,129},{32,160},{33,163},{34,162},{35,161... | collective-permute-start | bytes 1769480 | tf_op jit(solution)/shard_map/ppermute | solution.py:27
  35.4 9.7 %collective-permute-start.10 = (bf16[128,1024]{1,0:T(8,128)(2,1)S(1)}, bf16[128,1024]{1,0:T(8,128)(2,1)S(1)}, u32[]{:S(2)}, u32[]{:S(2)}) collective-permute-start(bf16[128,1024]{1,0:T(8,128)(2,1)S(1)} %collective-permute-done.9), channel_id=1, source_target_pairs={{0,4},{4,8},{8,12},{12,16},{16,20},{20,24},{24,28},{28,0},{1,5},{5... | collective-permute-start | bytes 786440 | tf_op jit(solution)/shard_map/ppermute | solution.py:31
  38.4 8.5 %collective-permute-start.12 = (bf16[64,1024]{1,0:T(8,128)(2,1)S(1)}, bf16[64,1024]{1,0:T(8,128)(2,1)S(1)}, u32[]{:S(2)}, u32[]{:S(2)}) collective-permute-start(bf16[64,1024]{1,0:T(8,128)(2,1)S(1)} %get-tuple-element.74), channel_id=1, source_target_pairs={{0,28},{4,0},{8,4},{12,8},{16,12},{20,16},{24,20},{28,24},{1,29},{... | collective-permute-start | bytes 393224 | tf_op jit(solution)/shard_map/ppermute | solution.py:31
  45.1 6.3 %collective-permute-start.11 = (bf16[64,1024]{1,0:T(8,128)(2,1)S(1)}, bf16[64,1024]{1,0:T(8,128)(2,1)S(1)}, u32[]{:S(2)}, u32[]{:S(2)}) collective-permute-start(bf16[64,1024]{1,0:T(8,128)(2,1)S(1)} %slice.414), channel_id=1, source_target_pairs={{0,4},{4,8},{8,12},{12,16},{16,20},{20,24},{24,28},{28,0},{1,5},{5... | collective-permute-start | bytes 393224 | tf_op jit(solution)/shard_map/ppermute | solution.py:31
  45.3 16.3 %collective-permute-start.21 = (bf16[512,1152]{1,0:T(8,128)(2,1)S(1)}, bf16[512,1152]{1,0:T(8,128)(2,1)S(1)}, u32[]{:S(2)}, u32[]{:S(2)}) collective-permute-start(bf16[512,1152]{1,0:T(8,128)(2,1)S(1)} %constant_dynamic-update-slice_fusion.15), channel_id=1, source_target_pairs={{0,96},{1,33},{2,98},{3,35},{32,64},{33,1},{34,66},{35,3},{64,32},... | collective-permute-start | bytes 3538952 | tf_op jit(solution)/shard_map/ppermute | solution.py:27
  45.5 19.3 %collective-permute-start.3 = (bf16[512,1152]{1,0:T(8,128)(2,1)S(1)}, bf16[512,1152]{1,0:T(8,128)(2,1)S(1)}, u32[]{:S(2)}, u32[]{:S(2)}) collective-permute-start(bf16[512,1152]{1,0:T(8,128)(2,1)S(1)} %constant_dynamic-update-slice_fusion), channel_id=1, source_target_pairs={{0,130},{1,129},{2,128},{3,131},{32,162},{33,161},{34,160},{35,163... | collective-permute-start | bytes 3538952 | tf_op jit(solution)/shard_map/ppermute | solution.py:27
  80.0 7.3 %collective-permute-start.27 = (bf16[64,1024]{1,0:T(8,128)(2,1)S(1)}, bf16[64,1024]{1,0:T(8,128)(2,1)S(1)}, u32[]{:S(2)}, u32[]{:S(2)}) collective-permute-start(bf16[64,1024]{1,0:T(8,128)(2,1)S(1)} %get-tuple-element.43), channel_id=1, source_target_pairs={{0,4},{4,8},{8,12},{12,16},{16,20},{20,24},{24,28},{28,0},{1,5},{5... | collective-permute-start | bytes 393224 | tf_op jit(solution)/shard_map/ppermute | solution.py:31
  81.2 6.8 %collective-permute-start.31 = (bf16[64,1024]{1,0:T(8,128)(2,1)S(1)}, bf16[64,1024]{1,0:T(8,128)(2,1)S(1)}, u32[]{:S(2)}, u32[]{:S(2)}) collective-permute-start(bf16[64,1024]{1,0:T(8,128)(2,1)S(1)} %get-tuple-element.46), channel_id=1, source_target_pairs={{0,28},{4,0},{8,4},{12,8},{16,12},{20,16},{24,20},{28,24},{1,29},{... | collective-permute-start | bytes 393224 | tf_op jit(solution)/shard_map/ppermute | solution.py:31
  85.1 24.2 %collective-permute-start.14 = (bf16[512,1024]{1,0:T(8,128)(2,1)S(1)}, bf16[512,1024]{1,0:T(8,128)(2,1)S(1)}, u32[]{:S(2)}, u32[]{:S(2)}) collective-permute-start(bf16[512,1024]{1,0:T(8,128)(2,1)S(1)} %pad_maximum_fusion.1), channel_id=1, source_target_pairs={{0,130},{1,129},{2,128},{3,131},{32,162},{33,161},{34,160},{35,163... | collective-permute-start | bytes 3145736 | tf_op jit(solution)/shard_map/ppermute | solution.py:27
  87.5 9.4 %collective-permute-start.28 = (bf16[128,1024]{1,0:T(8,128)(2,1)S(1)}, bf16[128,1024]{1,0:T(8,128)(2,1)S(1)}, u32[]{:S(2)}, u32[]{:S(2)}) collective-permute-start(bf16[128,1024]{1,0:T(8,128)(2,1)S(1)} %pad_maximum_fusion.14), channel_id=1, source_target_pairs={{0,4},{4,8},{8,12},{12,16},{16,20},{20,24},{24,28},{28,0},{1,5},{5... | collective-permute-start | bytes 786440 | tf_op jit(solution)/shard_map/ppermute | solution.py:31
  88.2 9.1 %collective-permute-start.32 = (bf16[128,1024]{1,0:T(8,128)(2,1)S(1)}, bf16[128,1024]{1,0:T(8,128)(2,1)S(1)}, u32[]{:S(2)}, u32[]{:S(2)}) collective-permute-start(bf16[128,1024]{1,0:T(8,128)(2,1)S(1)} %pad_maximum_fusion.15), channel_id=1, source_target_pairs={{0,28},{4,0},{8,4},{12,8},{16,12},{20,16},{24,20},{28,24},{1,29},{... | collective-permute-start | bytes 786440 | tf_op jit(solution)/shard_map/ppermute | solution.py:31
  96.9 8.5 %collective-permute-start.29 = (bf16[128,1024]{1,0:T(8,128)(2,1)S(1)}, bf16[128,1024]{1,0:T(8,128)(2,1)S(1)}, u32[]{:S(2)}, u32[]{:S(2)}) collective-permute-start(bf16[128,1024]{1,0:T(8,128)(2,1)S(1)} %fusion.18), channel_id=1, source_target_pairs={{0,4},{4,8},{8,12},{12,16},{16,20},{20,24},{24,28},{28,0},{1,5},{5... | collective-permute-start | bytes 786440 | tf_op jit(solution)/shard_map/ppermute | solution.py:31
  97.3 8.3 %collective-permute-start.33 = (bf16[128,1024]{1,0:T(8,128)(2,1)S(1)}, bf16[128,1024]{1,0:T(8,128)(2,1)S(1)}, u32[]{:S(2)}, u32[]{:S(2)}) collective-permute-start(bf16[128,1024]{1,0:T(8,128)(2,1)S(1)} %fusion.20), channel_id=1, source_target_pairs={{0,28},{4,0},{8,4},{12,8},{16,12},{20,16},{24,20},{28,24},{1,29},{... | collective-permute-start | bytes 786440 | tf_op jit(solution)/shard_map/ppermute | solution.py:31
  101.1 15.2 %collective-permute-start.23 = (bf16[512,1024]{1,0:T(8,128)(2,1)S(1)}, bf16[512,1024]{1,0:T(8,128)(2,1)S(1)}, u32[]{:S(2)}, u32[]{:S(2)}) collective-permute-start(bf16[512,1024]{1,0:T(8,128)(2,1)S(1)} %pad_maximum_fusion.4), channel_id=1, source_target_pairs={{0,96},{1,33},{2,98},{3,35},{32,64},{33,1},{34,66},{35,3},{64,32},... | collective-permute-start | bytes 3145736 | tf_op jit(solution)/shard_map/ppermute | solution.py:27
  105.5 7.7 %collective-permute-start.30 = (bf16[128,1024]{1,0:T(8,128)(2,1)S(1)}, bf16[128,1024]{1,0:T(8,128)(2,1)S(1)}, u32[]{:S(2)}, u32[]{:S(2)}) collective-permute-start(bf16[128,1024]{1,0:T(8,128)(2,1)S(1)} %fusion.17), channel_id=1, source_target_pairs={{0,4},{4,8},{8,12},{12,16},{16,20},{20,24},{24,28},{28,0},{1,5},{5... | collective-permute-start | bytes 786440 | tf_op jit(solution)/shard_map/ppermute | solution.py:31
  105.6 7.5 %collective-permute-start.34 = (bf16[128,1024]{1,0:T(8,128)(2,1)S(1)}, bf16[128,1024]{1,0:T(8,128)(2,1)S(1)}, u32[]{:S(2)}, u32[]{:S(2)}) collective-permute-start(bf16[128,1024]{1,0:T(8,128)(2,1)S(1)} %fusion.19), channel_id=1, source_target_pairs={{0,28},{4,0},{8,4},{12,8},{16,12},{20,16},{24,20},{28,24},{1,29},{... | collective-permute-start | bytes 786440 | tf_op jit(solution)/shard_map/ppermute | solution.py:31
  109.6 11.9 %collective-permute-start.15 = (bf16[256,1024]{1,0:T(8,128)(2,1)S(1)}, bf16[256,1024]{1,0:T(8,128)(2,1)S(1)}, u32[]{:S(2)}, u32[]{:S(2)}) collective-permute-start(bf16[256,1024]{1,0:T(8,128)(2,1)S(1)} %add_convert_fusion.1), channel_id=1, source_target_pairs={{0,128},{1,131},{2,130},{3,129},{32,160},{33,163},{34,162},{35,161... | collective-permute-start | bytes 1572872 | tf_op jit(solution)/shard_map/ppermute | solution.py:27
  113.3 19.1 %collective-permute-start.35 = (bf16[64,1024]{1,0:T(8,128)(2,1)S(1)}, bf16[64,1024]{1,0:T(8,128)(2,1)S(1)}, u32[]{:S(2)}, u32[]{:S(2)}) collective-permute-start(bf16[64,1024]{1,0:T(8,128)(2,1)S(1)} %get-tuple-element.65), channel_id=1, source_target_pairs={{0,2},{1,3},{2,0},{3,1},{32,34},{33,35},{34,32},{35,33},{64,66},{6... | collective-permute-start | bytes 393224 | tf_op jit(solution)/shard_map/ppermute | solution.py:27
  116.6 14.6 %collective-permute-start.24 = (bf16[256,1024]{1,0:T(8,128)(2,1)S(1)}, bf16[256,1024]{1,0:T(8,128)(2,1)S(1)}, u32[]{:S(2)}, u32[]{:S(2)}) collective-permute-start(bf16[256,1024]{1,0:T(8,128)(2,1)S(1)} %add_convert_fusion), channel_id=1, source_target_pairs={{0,32},{1,97},{2,34},{3,99},{32,0},{33,65},{34,2},{35,67},{64,96},... | collective-permute-start | bytes 1572872 | tf_op jit(solution)/shard_map/ppermute | solution.py:27
  121.7 11.4 %collective-permute-start.16 = (bf16[128,1024]{1,0:T(8,128)(2,1)S(1)}, bf16[128,1024]{1,0:T(8,128)(2,1)S(1)}, u32[]{:S(2)}, u32[]{:S(2)}) collective-permute-start(bf16[128,1024]{1,0:T(8,128)(2,1)S(1)} %pad_maximum_fusion.12), channel_id=1, source_target_pairs={{0,96},{1,33},{2,98},{3,35},{32,64},{33,1},{34,66},{35,3},{64,32},... | collective-permute-start | bytes 786440 | tf_op jit(solution)/shard_map/ppermute | solution.py:27
  131.5 7.7 %collective-permute-start.25 = (bf16[128,1024]{1,0:T(8,128)(2,1)S(1)}, bf16[128,1024]{1,0:T(8,128)(2,1)S(1)}, u32[]{:S(2)}, u32[]{:S(2)}) collective-permute-start(bf16[128,1024]{1,0:T(8,128)(2,1)S(1)} %pad_maximum_fusion.13), channel_id=1, source_target_pairs={{0,130},{1,129},{2,128},{3,131},{32,162},{33,161},{34,160},{35,163... | collective-permute-start | bytes 786440 | tf_op jit(solution)/shard_map/ppermute | solution.py:27
  (21 other events, 97.5 us)

commit v2 on v0

v2 whole, which is shorter than its diff:
```python
import jax
import jax.numpy as jnp
from jax import lax
from jax.experimental import pallas as pl
from jax.experimental.pallas import tpu as pltpu
from jax.sharding import Mesh, PartitionSpec as P

inv_temp = 50.0
ROWS_SPEC = ("yl", "x", "z")
FEATURES_SPEC = ("yh", "c")
PLANE = ("yl", "x", "yh", "c")
bf16, f32 = jnp.bfloat16, jnp.float32
NEAR, FAR = (1, 3), (3, 1)
HALF, WIDTH, LOADED = 64, 1024, 1152
BLOCK, COLUMNS = 256, 512
VMEM, SMEM = pltpu.VMEM, pltpu.SMEM


def flip(value, axis, bits):
    pairs = []
    for yl in range(2):
        for x in range(4):
            for yh in range(2):
                for core in range(2):
                    x_to, y_to = x, 2 * yh + yl
                    if axis == "x":
                        x_to ^= bits[core]
                    else:
                        y_to ^= bits[core]
                    target = (((y_to % 2) * 4 + x_to) * 2 + y_to // 2) * 2 + core
                    pairs.append((((yl * 4 + x) * 2 + yh) * 2 + core, target))
    return lax.ppermute(value, PLANE, pairs)


def shift(value, step):
    return lax.ppermute(value, "z", [(i, (i + step) % 8) for i in range(8)])


def together(*values):
    return lax.optimization_barrier(values)


def dot(a, b, contract):
    return lax.dot_general(a, b, (contract, ((), ())), preferred_element_type=f32)


def prepare(yh_ref, queries, passages, lse, weight, positive, top, low, own, away, need, ready):
    first = yh_ref[0] == 0
    need(1)
    away[...] = jnp.where(first, passages[HALF:, :], passages[0:HALF, :])
    ready(3)
    own[...] = jnp.where(first, passages[0:HALF, :], passages[HALF:, :])
    ready(2)
    need(2, 3, 4)
    rows = []
    for value in (lse[...], weight[...]):
        high = value.astype(bf16).astype(f32)
        middle = (value - high).astype(bf16).astype(f32)
        rows += [high, middle, value - high - middle]
    target = positive[...]
    rows += [(target // 128).astype(f32), (target % 128).astype(f32), jnp.zeros((120, 128), f32)]
    stats = jnp.concatenate(rows).T.astype(bf16)
    need(0)
    top[:, :WIDTH], top[:, WIDTH:] = queries[0:HALF, :], stats[0:HALF]
    low[:, :WIDTH], low[:, WIDTH:] = queries[HALF:, :], stats[HALF:]
    ready(0, 1)


def call(kernel, outs, args, flops=0):
    outs = [jax.ShapeDtypeStruct(*o) for o in outs]
    size = sum(a.size * a.dtype.itemsize for a in [*args, *outs])
    n, m = len(args) - 1, len(outs)

    def body(scalar, *refs):
        operands, results, refs = refs[:n], refs[n : n + m], refs[n + m :]
        here, made, sem_in, sem_out = refs[:n], refs[n : n + m], refs[-2], refs[-1]
        fetched = [pltpu.make_async_copy(operands[i], here[i], sem_in.at[i]) for i in range(n)]
        for copy in fetched:
            copy.start()
        sent = [pltpu.make_async_copy(made[i], results[i], sem_out.at[i]) for i in range(m)]

        def need(*places):
            for i in places:
                fetched[i].wait()

        def ready(*places):
            for i in places:
                sent[i].start()

        kernel(scalar, *here, *made, need=need, ready=ready)
        for copy in sent:
            copy.wait()

    return pl.pallas_call(
        body,
        out_shape=outs,
        in_specs=[pl.BlockSpec(memory_space=s) for s in [SMEM] + [pl.ANY] * n],
        out_specs=[pl.BlockSpec(memory_space=pl.ANY)] * m,
        scratch_shapes=[
            *[VMEM(a.shape, a.dtype) for a in [*args[1:], *outs]],
            pltpu.SemaphoreType.DMA((n,)),
            pltpu.SemaphoreType.DMA((m,)),
        ],
        compiler_params=pltpu.CompilerParams(vmem_limit_bytes=60 * 1024 * 1024),
        cost_estimate=pl.CostEstimate(flops=flops, bytes_accessed=size, transcendentals=0),
    )(*args)


def on_device(queries, passages, row_lse, row_weight, positive):
    x, z, yl, yh, core = (lax.axis_index(a) for a in ("x", "z", "yl", "yh", "c"))
    rows, half = 2 * HALF, HALF
    first_core = core == 0

    vectors = [value.reshape(1, rows) for value in (row_lse, row_weight, positive)]
    quarter = ((half, WIDTH), bf16)
    top, low, passage_own, passage_away = call(
        prepare,
        [((half, LOADED), bf16)] * 2 + [quarter] * 2,
        [yh.astype(jnp.int32).reshape(1), queries, passages, *vectors],
    )
    place = jnp.arange(COLUMNS, dtype=jnp.int32)
    owner = (yl * 4 + x) * 8 + (z + place // half) % 8
    column = (owner * rows + yh * half + place % half)[None, :]

    passage_back, top_near, low_near = together(
        flip(passage_away, "y", (2, 2)), flip(top, "x", NEAR), flip(low, "y", NEAR)
    )
    ring = [None] * 8
    ring[0], top, low = together(
        jnp.concatenate([passage_own, passage_back]),
        jnp.concatenate([top, top_near]),
        jnp.concatenate([low, low_near]),
    )
    ring[7], ring[1], top_far, low_far = together(
        shift(ring[0], 1), shift(ring[0], -1), flip(top, "x", FAR), flip(low, "y", FAR)
    )
    top, low = together(jnp.concatenate([top, top_far]), jnp.concatenate([low, low_far]))
    ring[6], ring[2], top_near, low_near = together(
        shift(ring[7], 1), shift(ring[1], -1), flip(top, "y", NEAR), flip(low, "x", NEAR)
    )
    top, low = together(jnp.concatenate([top, top_near]), jnp.concatenate([low, low_near]))
    top_far, low_far = flip(top, "y", FAR), flip(low, "x", FAR)
    ring[5], ring[3] = together(shift(ring[6], 1), shift(ring[2], -1))
    ring[4] = shift(ring[5], 1)

    p_same = jnp.concatenate([b[:half] for b in ring])
    p_other = jnp.concatenate([b[half:] for b in ring])

    def pick(own, near, far, opposite, axis):
        same = jnp.concatenate([own, jnp.where(first_core, near, far)], axis=axis)
        other = jnp.concatenate([opposite, jnp.where(first_core, far, near)], axis=axis)
        return same, other

    top_same, top_other = pick(top[:BLOCK], top[BLOCK:], top_far[:BLOCK], top_far[BLOCK:], 0)
    low_same, low_other = [], []
    for part in (low, low_far):
        part = part.reshape(2, 4, half, LOADED)
        same, other = pick(part[:, 0:1], part[:, 1:2], part[:, 2:3], part[:, 3:4], 1)
        low_same.append(same.reshape(BLOCK, LOADED))
        low_other.append(other.reshape(BLOCK, LOADED))
    q_same = [top_same, jnp.concatenate(low_same)]
    q_other = [top_other, jnp.concatenate(low_other)]
    stats = [q[:, WIDTH:].astype(f32) for q in q_same]
    q_same = [q[:, :WIDTH] for q in q_same]
    q_other = [q[:, :WIDTH] for q in q_other]

    def swapped(scores, shape, axis):
        scores = lax.ppermute(scores, "c", [(0, 1), (1, 0)]).reshape(shape)
        blocks = [lax.slice_in_dim(scores, i, i + 1, axis=axis) for i in (0, 2, 1, 3)]
        return jnp.concatenate(blocks, axis=axis).reshape(COLUMNS, COLUMNS)

    grads = []
    for same, other, stat, shape, axis in zip(
        q_same, q_other, stats, ((2, 4, half, COLUMNS), (4, rows, COLUMNS)), (1, 0)
    ):
        partial_value = dot(same, p_same, ((1,), (1,))) + dot(other, p_other, ((1,), (1,)))
        scores = partial_value + swapped(partial_value, shape, axis)
        lse = stat[:, 0:1] + stat[:, 1:2] + stat[:, 2:3]
        weight = stat[:, 3:4] + stat[:, 4:5] + stat[:, 5:6]
        target = (stat[:, 6:7] * 128 + stat[:, 7:8]).astype(jnp.int32)
        is_positive = (column == target).astype(f32)
        grads.append((weight * (jnp.exp(inv_temp * scores - lse) - is_positive)).astype(bf16))

    w_same = [dot(g, p_same, ((1,), (0,))) for g in grads]
    w_other = [dot(g, p_other, ((1,), (0,))) for g in grads]
    v_same = dot(grads[0], q_same[0], ((0,), (0,))) + dot(grads[1], q_same[1], ((0,), (0,)))
    v_other = dot(grads[0], q_other[0], ((0,), (0,))) + dot(grads[1], q_other[1], ((0,), (0,)))
    parts = [
        jnp.concatenate([v_same[i * half : (i + 1) * half], v_other[i * half : (i + 1) * half]]) for i in range(8)
    ]

    near, far = w_same[0][BLOCK:], w_other[0][BLOCK:]
    top_own, top_near = w_same[0][:BLOCK], jnp.where(first_core, near, far)
    top_send = jnp.concatenate([jnp.where(first_core, far, near), w_other[0][:BLOCK]]).astype(bf16)
    same, other = w_same[1].reshape(4, rows, WIDTH), w_other[1].reshape(4, rows, WIDTH)
    low_all = jnp.concatenate([same, other], axis=1)
    low_own, low_near, low_send = low_all[0], low_all[1], low_all[2:].reshape(2 * BLOCK, WIDTH).astype(bf16)
    top_got, low_got = flip(top_send, "y", FAR), flip(low_send, "x", FAR)
    up, down = together(shift(parts[4].astype(bf16), 1), shift(parts[5].astype(bf16), -1))
    up, down = together((parts[3] + up).astype(bf16), (parts[6] + down).astype(bf16))
    up, down, top_got, low_got = together(shift(up, 1), shift(down, -1), top_got, low_got)
    up, down, top_send, low_send = together(
        (parts[2] + up).astype(bf16),
        (parts[7] + down).astype(bf16),
        (top_near + top_got[BLOCK:]).astype(bf16),
        (low_near + low_got[BLOCK:]).astype(bf16),
    )
    up, down, top_last, low_last = together(
        shift(up, 1), shift(down, -1), flip(top_send, "y", NEAR), flip(low_send, "x", NEAR)
    )
    top = top_own + top_got[:BLOCK] + top_last
    low = low_own + low_got[:BLOCK] + low_last
    one, three = low[half:rows], low[rows + half :]
    low_near = jnp.where(first_core, one, three)
    low_send = jnp.concatenate([jnp.where(first_core, three, one), low[rows : rows + half]]).astype(bf16)
    up, top_send, low_send = together((parts[1] + up).astype(bf16), top[rows:].astype(bf16), low_send)
    up, top_got, low_got = together(shift(up, 1), flip(top_send, "x", FAR), flip(low_send, "y", FAR))
    passage_sum = (inv_temp * (parts[0] + up + down)).astype(bf16)
    passage_own = passage_sum[:half]
    passage_back = flip(passage_sum[half:], "y", (2, 2))
    top_last = flip((top[half:rows] + top_got[half:]).astype(bf16), "x", NEAR)
    low_last = flip((low_near + low_got[half:]).astype(bf16), "y", NEAR)
    passage_grad = jnp.where(
        yh == 0,
        jnp.concatenate([passage_own, passage_back]),
        jnp.concatenate([passage_back, passage_own]),
    )
    top = top[:half] + top_got[:half] + top_last
    low = low[:half] + low_got[:half] + low_last
    query_grad = (inv_temp * jnp.concatenate([top, low])).astype(bf16)
    return query_grad, passage_grad


def solution(mesh):
    split = Mesh(mesh.devices.reshape(2, 4, 8, 2, 2), ("yl", "x", "z", "yh", "c"))
    matrix, vector = P(ROWS_SPEC, FEATURES_SPEC), P(ROWS_SPEC)
    return jax.shard_map(
        on_device,
        mesh=split,
        in_specs=(matrix, matrix, vector, vector, vector),
        out_specs=(matrix, matrix),
        check_vma=False,
    )
```

time: 832 us -> 138 us (0.17)
  the two profiles are of different devices: /device:TPU:16 before, /device:TPU:1 now
where the time goes in v2:
time: 138 us
  waiting for transfers between devices  65.3 us (47%)
  starting transfers between devices  45.3 us (33%)
  other arithmetic  14.3 us (10%)
  matrix products  8.93 us (6%)
  Pallas kernels  1.97 us (1%)
    ppermute x14, waiting for transfers between devices, shift(): return lax.ppermute(value, 'z', [(i, (i + step) % 8) for i in range(8)])  40.7 us
    ppermute x18, waiting for transfers between devices, flip(): return lax.ppermute(value, PLANE, pairs)  23.9 us
    ppermute x14, starting transfers between devices, shift(): return lax.ppermute(value, 'z', [(i, (i + step) % 8) for i in range(8)])  18.8 us
    ppermute x18, starting transfers between devices, flip(): return lax.ppermute(value, PLANE, pairs)  18.4 us
    dot_general x12, matrix products, dot(): lax.dot_general(a, b, (contract, ((), ())), preferred_element_type=f32)  8.93 us
    ppermute x2, starting transfers between devices, swapped(): scores = lax.ppermute(scores, 'c', [(0, 1), (1, 0)]).reshape(shape)  8.11 us
  transfers between devices with their start and end apart: 34, of which 19 were waited for; matrix products, arithmetic and copies ran while one was open for 6% of the time, Pallas kernels for 0%

profile of v2, /device:TPU:1, one launch (start us, length us, event | category | flops | bytes accessed | tf_op | source)
XLA Modules:
  0.0 137.7 jit_solution(4386703826324110507)
XLA Ops:
  0.6 2.0 %shard_map.68 = (bf16[64,1152]{1,0:T(8,128)(2,1)}, bf16[64,1152]{1,0:T(8,128)(2,1)}, bf16[64,1024]{1,0:T(8,128)(2,1)}, bf16[64,1024]{1,0:T(8,128)(2,1)}) custom-call(s32[1]{0:T(128)} %bitcast.scalar, bf16[128,1024]{1,0:T(8,128)(2,1)} %refs_0_.1, bf16[128,1024]{1,0:T(8,128)(2,1)} %refs_1_.1, f32[1,128]{1,0:T(1,128)} %bitcast.98, f32[1,128]{1,0:T(1,128)} %bitcast.99, ...), custom_call_target="tpu_custom_call" | custom-call | bytes 1082884 | tf_op jit(solution)/shard_map/pallas_call | solution.py:94
  2.6 3.4 %collective-permute-start.1 = (bf16[64,1152]{1,0:T(8,128)(2,1)}, bf16[64,1152]{1,0:T(8,128)(2,1)S(1)}, u32[]{:S(2)}, u32[]{:S(2)}) collective-permute-start(bf16[64,1152]{1,0:T(8,128)(2,1)} %get-tuple-element.50), channel_id=1, source_target_pairs={{0,32},{1,97},{2,34},{3,99},{32,0},{33,65},{34,2},{35,67},{64,96},... | collective-permute-start | bytes 442376 | tf_op jit(solution)/shard_map/ppermute | solution.py:32
  6.0 2.7 %collective-permute-start.2 = (bf16[64,1152]{1,0:T(8,128)(2,1)}, bf16[64,1152]{1,0:T(8,128)(2,1)S(1)}, u32[]{:S(2)}, u32[]{:S(2)}) collective-permute-start(bf16[64,1152]{1,0:T(8,128)(2,1)} %get-tuple-element.51), channel_id=1, source_target_pairs={{0,128},{1,131},{2,130},{3,129},{32,160},{33,163},{34,162},{35,161... | collective-permute-start | bytes 442376 | tf_op jit(solution)/shard_map/ppermute | solution.py:32
  9.1 6.7 %collective-permute-done = bf16[64,1024]{1,0:T(8,128)(2,1)S(1)} collective-permute-done((bf16[64,1024]{1,0:T(8,128)(2,1)}, bf16[64,1024]{1,0:T(8,128)(2,1)S(1)}, u32[]{:S(2)}, u32[]{:S(2)}) %collective-permute-start) | collective-permute-done | bytes 131104 | tf_op jit(solution)/shard_map/ppermute | solution.py:32
  18.0 5.6 %collective-permute-start.4 = (bf16[128,1024]{1,0:T(8,128)(2,1)S(1)}, bf16[128,1024]{1,0:T(8,128)(2,1)S(1)}, u32[]{:S(2)}, u32[]{:S(2)}) collective-permute-start(bf16[128,1024]{1,0:T(8,128)(2,1)S(1)} %pad_maximum_fusion.26), channel_id=1, source_target_pairs={{0,28},{4,0},{8,4},{12,8},{16,12},{20,16},{24,20},{28,24},{1,29},{... | collective-permute-start | bytes 786440 | tf_op jit(solution)/shard_map/ppermute | solution.py:36
  23.6 3.3 %collective-permute-done.4 = bf16[128,1024]{1,0:T(8,128)(2,1)S(1)} collective-permute-done((bf16[128,1024]{1,0:T(8,128)(2,1)S(1)}, bf16[128,1024]{1,0:T(8,128)(2,1)S(1)}, u32[]{:S(2)}, u32[]{:S(2)}) %collective-permute-start.4) | collective-permute-done | bytes 262176 | tf_op jit(solution)/shard_map/ppermute | solution.py:36
  26.9 3.1 %collective-permute-done.3 = bf16[128,1024]{1,0:T(8,128)(2,1)S(1)} collective-permute-done((bf16[128,1024]{1,0:T(8,128)(2,1)S(1)}, bf16[128,1024]{1,0:T(8,128)(2,1)S(1)}, u32[]{:S(2)}, u32[]{:S(2)}) %collective-permute-start.3) | collective-permute-done | bytes 262176 | tf_op jit(solution)/shard_map/ppermute | solution.py:36
  30.2 1.3 collective-permute-start.9
  31.4 2.7 %collective-permute-start.8 = (bf16[128,1024]{1,0:T(8,128)(2,1)S(1)}, bf16[128,1024]{1,0:T(8,128)(2,1)S(1)}, u32[]{:S(2)}, u32[]{:S(2)}) collective-permute-start(bf16[128,1024]{1,0:T(8,128)(2,1)S(1)} %collective-permute-done.4), channel_id=1, source_target_pairs={{0,28},{4,0},{8,4},{12,8},{16,12},{20,16},{24,20},{28,24},{1,29},{... | collective-permute-start | bytes 786440 | tf_op jit(solution)/shard_map/ppermute | solution.py:36
  34.1 3.7 %collective-permute-done.7 = bf16[128,1024]{1,0:T(8,128)(2,1)S(1)} collective-permute-done((bf16[128,1024]{1,0:T(8,128)(2,1)S(1)}, bf16[128,1024]{1,0:T(8,128)(2,1)S(1)}, u32[]{:S(2)}, u32[]{:S(2)}) %collective-permute-start.7) | collective-permute-done | bytes 262176 | tf_op jit(solution)/shard_map/ppermute | solution.py:36
  37.9 2.3 %collective-permute-done.9 = bf16[256,1152]{1,0:T(8,128)(2,1)S(1)} collective-permute-done((bf16[256,1152]{1,0:T(8,128)(2,1)S(1)}, bf16[256,1152]{1,0:T(8,128)(2,1)S(1)}, u32[]{:S(2)}, u32[]{:S(2)}) %collective-permute-start.9) | collective-permute-done | bytes 589856 | tf_op jit(solution)/shard_map/ppermute | solution.py:32
  40.2 1.5 %collective-permute-done.10 = bf16[256,1152]{1,0:T(8,128)(2,1)S(1)} collective-permute-done((bf16[256,1152]{1,0:T(8,128)(2,1)S(1)}, bf16[256,1152]{1,0:T(8,128)(2,1)S(1)}, u32[]{:S(2)}, u32[]{:S(2)}) %collective-permute-start.10) | collective-permute-done | bytes 589856 | tf_op jit(solution)/shard_map/ppermute | solution.py:32
  41.8 1.5 %collective-permute-start.12 = (bf16[128,1024]{1,0:T(8,128)(2,1)S(1)}, bf16[128,1024]{1,0:T(8,128)(2,1)S(1)}, u32[]{:S(2)}, u32[]{:S(2)}) collective-permute-start(bf16[128,1024]{1,0:T(8,128)(2,1)S(1)} %collective-permute-done.7), channel_id=1, source_target_pairs={{0,4},{4,8},{8,12},{12,16},{16,20},{20,24},{24,28},{28,0},{1,5},{5... | collective-permute-start | bytes 786440 | tf_op jit(solution)/shard_map/ppermute | solution.py:36
  43.4 1.5 %collective-permute-start.11 = (bf16[512,1152]{1,0:T(8,128)(2,1)S(1)}, bf16[512,1152]{1,0:T(8,128)(2,1)S(1)}, u32[]{:S(2)}, u32[]{:S(2)}) collective-permute-start(bf16[512,1152]{1,0:T(8,128)(2,1)S(1)} %pad_maximum_fusion), channel_id=1, source_target_pairs={{0,130},{1,129},{2,128},{3,131},{32,162},{33,161},{34,160},{35,163... | collective-permute-start | bytes 3538952 | tf_op jit(solution)/shard_map/ppermute | solution.py:32
  44.9 1.2 collective-permute-start.16
  47.0 1.3 collective-permute-done.12
  48.9 7.4 %collective-permute-done.14 = bf16[128,1024]{1,0:T(8,128)(2,1)S(1)} collective-permute-done((bf16[128,1024]{1,0:T(8,128)(2,1)S(1)}, bf16[128,1024]{1,0:T(8,128)(2,1)S(1)}, u32[]{:S(2)}, u32[]{:S(2)}) %collective-permute-start.14) | collective-permute-done | bytes 262176 | tf_op jit(solution)/shard_map/ppermute | solution.py:36
  56.4 3.8 %collective-permute-done.16 = bf16[512,1152]{1,0:T(8,128)(2,1)S(1)} collective-permute-done((bf16[512,1152]{1,0:T(8,128)(2,1)S(1)}, bf16[512,1152]{1,0:T(8,128)(2,1)S(1)}, u32[]{:S(2)}, u32[]{:S(2)}) %collective-permute-start.16) | collective-permute-done | bytes 1179680 | tf_op jit(solution)/shard_map/ppermute | solution.py:32
  62.0 8.0 %collective-permute-start.15 = (f32[512,512]{1,0:T(8,128)S(1)}, f32[512,512]{1,0:T(8,128)S(1)}, u32[]{:S(2)}, u32[]{:S(2)}) collective-permute-start(f32[512,512]{1,0:T(8,128)S(1)} %convolution_add_fusion.3), channel_id=1, source_target_pairs={{0,1},{1,0},{2,3},{3,2},{4,5},{5,4},{6,7},{7,6},{8,9},{9,8},{10,11... | collective-permute-start | bytes 3145736 | tf_op jit(solution)/shard_map/ppermute | solution.py:168
  81.9 3.0 %collective-permute-start.19 = (bf16[128,1024]{1,0:T(8,128)(2,1)S(1)}, bf16[128,1024]{1,0:T(8,128)(2,1)S(1)}, u32[]{:S(2)}, u32[]{:S(2)}) collective-permute-start(bf16[128,1024]{1,0:T(8,128)(2,1)S(1)} %pad_maximum_fusion.28), channel_id=1, source_target_pairs={{0,28},{4,0},{8,4},{12,8},{16,12},{20,16},{24,20},{28,24},{1,29},{... | collective-permute-start | bytes 786440 | tf_op jit(solution)/shard_map/ppermute | solution.py:36
  86.1 5.3 %collective-permute-done.18 = bf16[128,1024]{1,0:T(8,128)(2,1)S(1)} collective-permute-done((bf16[128,1024]{1,0:T(8,128)(2,1)S(1)}, bf16[128,1024]{1,0:T(8,128)(2,1)S(1)}, u32[]{:S(2)}, u32[]{:S(2)}) %collective-permute-start.18) | collective-permute-done | bytes 262176 | tf_op jit(solution)/shard_map/ppermute | solution.py:36
  91.6 2.7 %collective-permute-start.21 = (bf16[128,1024]{1,0:T(8,128)(2,1)S(1)}, bf16[128,1024]{1,0:T(8,128)(2,1)S(1)}, u32[]{:S(2)}, u32[]{:S(2)}) collective-permute-start(bf16[128,1024]{1,0:T(8,128)(2,1)S(1)} %fusion.27), channel_id=1, source_target_pairs={{0,28},{4,0},{8,4},{12,8},{16,12},{20,16},{24,20},{28,24},{1,29},{... | collective-permute-start | bytes 786440 | tf_op jit(solution)/shard_map/ppermute | solution.py:36
  94.3 5.6 %collective-permute-done.20 = bf16[128,1024]{1,0:T(8,128)(2,1)S(1)} collective-permute-done((bf16[128,1024]{1,0:T(8,128)(2,1)S(1)}, bf16[128,1024]{1,0:T(8,128)(2,1)S(1)}, u32[]{:S(2)}, u32[]{:S(2)}) %collective-permute-start.20) | collective-permute-done | bytes 262176 | tf_op jit(solution)/shard_map/ppermute | solution.py:36
  100.5 2.0 %collective-permute-start.26 = (bf16[256,1024]{1,0:T(8,128)(2,1)S(1)}, bf16[256,1024]{1,0:T(8,128)(2,1)S(1)}, u32[]{:S(2)}, u32[]{:S(2)}) collective-permute-start(bf16[256,1024]{1,0:T(8,128)(2,1)S(1)} %add_convert_fusion), channel_id=1, source_target_pairs={{0,128},{1,131},{2,130},{3,129},{32,160},{33,163},{34,162},{35,161... | collective-permute-start | bytes 1572872 | tf_op jit(solution)/shard_map/ppermute | solution.py:32
  102.5 2.7 %collective-permute-start.25 = (bf16[128,1024]{1,0:T(8,128)(2,1)S(1)}, bf16[128,1024]{1,0:T(8,128)(2,1)S(1)}, u32[]{:S(2)}, u32[]{:S(2)}) collective-permute-start(bf16[128,1024]{1,0:T(8,128)(2,1)S(1)} %fusion.29), channel_id=1, source_target_pairs={{0,28},{4,0},{8,4},{12,8},{16,12},{20,16},{24,20},{28,24},{1,29},{... | collective-permute-start | bytes 786440 | tf_op jit(solution)/shard_map/ppermute | solution.py:36
  105.1 3.8 %collective-permute-done.24 = bf16[128,1024]{1,0:T(8,128)(2,1)S(1)} collective-permute-done((bf16[128,1024]{1,0:T(8,128)(2,1)S(1)}, bf16[128,1024]{1,0:T(8,128)(2,1)S(1)}, u32[]{:S(2)}, u32[]{:S(2)}) %collective-permute-start.24) | collective-permute-done | bytes 262176 | tf_op jit(solution)/shard_map/ppermute | solution.py:36
  108.9 1.2 collective-permute-done.26
  110.1 1.9 %collective-permute-done.27 = bf16[256,1024]{1,0:T(8,128)(2,1)S(1)} collective-permute-done((bf16[256,1024]{1,0:T(8,128)(2,1)S(1)}, bf16[256,1024]{1,0:T(8,128)(2,1)S(1)}, u32[]{:S(2)}, u32[]{:S(2)}) %collective-permute-start.27) | collective-permute-done | bytes 524320 | tf_op jit(solution)/shard_map/ppermute | solution.py:32
  114.6 6.4 %collective-permute-done.28 = bf16[128,1024]{1,0:T(8,128)(2,1)S(1)} collective-permute-done((bf16[128,1024]{1,0:T(8,128)(2,1)}, bf16[128,1024]{1,0:T(8,128)(2,1)S(1)}, u32[]{:S(2)}, u32[]{:S(2)}) %collective-permute-start.28) | collective-permute-done | bytes 262176 | tf_op jit(solution)/shard_map/ppermute | solution.py:36
  123.0 4.3 %collective-permute-start.31 = (bf16[64,1024]{1,0:T(8,128)(2,1)S(1)}, bf16[64,1024]{1,0:T(8,128)(2,1)S(1)}, u32[]{:S(2)}, u32[]{:S(2)}) collective-permute-start(bf16[64,1024]{1,0:T(8,128)(2,1)S(1)} %fusion.36), channel_id=1, source_target_pairs={{0,32},{1,97},{2,34},{3,99},{32,0},{33,65},{34,2},{35,67},{64,96},... | collective-permute-start | bytes 393224 | tf_op jit(solution)/shard_map/ppermute | solution.py:32
  127.9 1.7 %collective-permute-done.31 = bf16[64,1024]{1,0:T(8,128)(2,1)S(1)} collective-permute-done((bf16[64,1024]{1,0:T(8,128)(2,1)S(1)}, bf16[64,1024]{1,0:T(8,128)(2,1)S(1)}, u32[]{:S(2)}, u32[]{:S(2)}) %collective-permute-start.31) | collective-permute-done | bytes 131104 | tf_op jit(solution)/shard_map/ppermute | solution.py:32
  130.5 4.7 %collective-permute-done.32 = bf16[64,1024]{1,0:T(8,128)(2,1)S(1)} collective-permute-done((bf16[64,1024]{1,0:T(8,128)(2,1)S(1)}, bf16[64,1024]{1,0:T(8,128)(2,1)S(1)}, u32[]{:S(2)}, u32[]{:S(2)}) %collective-permute-start.32) | collective-permute-done | bytes 131104 | tf_op jit(solution)/shard_map/ppermute | solution.py:32
  (111 shorter events, 28.4 us)
Async XLA Ops:
  2.6 13.2 %collective-permute-start.1 = (bf16[64,1152]{1,0:T(8,128)(2,1)}, bf16[64,1152]{1,0:T(8,128)(2,1)S(1)}, u32[]{:S(2)}, u32[]{:S(2)}) collective-permute-start(bf16[64,1152]{1,0:T(8,128)(2,1)} %get-tuple-element.50), channel_id=1, source_target_pairs={{0,32},{1,97},{2,34},{3,99},{32,0},{33,65},{34,2},{35,67},{64,96},... | collective-permute-start | bytes 442376 | tf_op jit(solution)/shard_map/ppermute | solution.py:32
  6.0 9.8 %collective-permute-start.2 = (bf16[64,1152]{1,0:T(8,128)(2,1)}, bf16[64,1152]{1,0:T(8,128)(2,1)S(1)}, u32[]{:S(2)}, u32[]{:S(2)}) collective-permute-start(bf16[64,1152]{1,0:T(8,128)(2,1)} %get-tuple-element.51), channel_id=1, source_target_pairs={{0,128},{1,131},{2,130},{3,129},{32,160},{33,163},{34,162},{35,161... | collective-permute-start | bytes 442376 | tf_op jit(solution)/shard_map/ppermute | solution.py:32
  8.7 7.0 %collective-permute-start = (bf16[64,1024]{1,0:T(8,128)(2,1)}, bf16[64,1024]{1,0:T(8,128)(2,1)S(1)}, u32[]{:S(2)}, u32[]{:S(2)}) collective-permute-start(bf16[64,1024]{1,0:T(8,128)(2,1)} %get-tuple-element.49), channel_id=1, source_target_pairs={{0,2},{1,3},{2,0},{3,1},{32,34},{33,35},{34,32},{35,33},{64,66},{6... | collective-permute-start | bytes 393224 | tf_op jit(solution)/shard_map/ppermute | solution.py:32
  17.8 12.3 %collective-permute-start.5 = (bf16[128,1152]{1,0:T(8,128)(2,1)S(1)}, bf16[128,1152]{1,0:T(8,128)(2,1)S(1)}, u32[]{:S(2)}, u32[]{:S(2)}) collective-permute-start(bf16[128,1152]{1,0:T(8,128)(2,1)S(1)} %get-tuple-element.55), channel_id=1, source_target_pairs={{0,96},{1,33},{2,98},{3,35},{32,64},{33,1},{34,66},{35,3},{64,32},... | collective-permute-start | bytes 884744 | tf_op jit(solution)/shard_map/ppermute | solution.py:32
  18.0 12.0 %collective-permute-start.6 = (bf16[128,1152]{1,0:T(8,128)(2,1)S(1)}, bf16[128,1152]{1,0:T(8,128)(2,1)S(1)}, u32[]{:S(2)}, u32[]{:S(2)}) collective-permute-start(bf16[128,1152]{1,0:T(8,128)(2,1)S(1)} %get-tuple-element.57), channel_id=1, source_target_pairs={{0,130},{1,129},{2,128},{3,131},{32,162},{33,161},{34,160},{35,163... | collective-permute-start | bytes 884744 | tf_op jit(solution)/shard_map/ppermute | solution.py:32
  18.0 8.9 %collective-permute-start.4 = (bf16[128,1024]{1,0:T(8,128)(2,1)S(1)}, bf16[128,1024]{1,0:T(8,128)(2,1)S(1)}, u32[]{:S(2)}, u32[]{:S(2)}) collective-permute-start(bf16[128,1024]{1,0:T(8,128)(2,1)S(1)} %pad_maximum_fusion.26), channel_id=1, source_target_pairs={{0,28},{4,0},{8,4},{12,8},{16,12},{20,16},{24,20},{28,24},{1,29},{... | collective-permute-start | bytes 786440 | tf_op jit(solution)/shard_map/ppermute | solution.py:36
  23.6 6.4 %collective-permute-start.3 = (bf16[128,1024]{1,0:T(8,128)(2,1)S(1)}, bf16[128,1024]{1,0:T(8,128)(2,1)S(1)}, u32[]{:S(2)}, u32[]{:S(2)}) collective-permute-start(bf16[128,1024]{1,0:T(8,128)(2,1)S(1)} %pad_maximum_fusion.26), channel_id=1, source_target_pairs={{0,4},{4,8},{8,12},{12,16},{16,20},{20,24},{24,28},{28,0},{1,5},{5... | collective-permute-start | bytes 786440 | tf_op jit(solution)/shard_map/ppermute | solution.py:36
  30.2 10.0 %collective-permute-start.9 = (bf16[256,1152]{1,0:T(8,128)(2,1)S(1)}, bf16[256,1152]{1,0:T(8,128)(2,1)S(1)}, u32[]{:S(2)}, u32[]{:S(2)}) collective-permute-start(bf16[256,1152]{1,0:T(8,128)(2,1)S(1)} %pad_maximum_fusion.18), channel_id=1, source_target_pairs={{0,128},{1,131},{2,130},{3,129},{32,160},{33,163},{34,162},{35,161... | collective-permute-start | bytes 1769480 | tf_op jit(solution)/shard_map/ppermute | solution.py:32
  31.4 10.2 %collective-permute-start.10 = (bf16[256,1152]{1,0:T(8,128)(2,1)S(1)}, bf16[256,1152]{1,0:T(8,128)(2,1)S(1)}, u32[]{:S(2)}, u32[]{:S(2)}) collective-permute-start(bf16[256,1152]{1,0:T(8,128)(2,1)S(1)} %pad_maximum_fusion.19), channel_id=1, source_target_pairs={{0,32},{1,97},{2,34},{3,99},{32,0},{33,65},{34,2},{35,67},{64,96},... | collective-permute-start | bytes 1769480 | tf_op jit(solution)/shard_map/ppermute | solution.py:32
  31.4 6.4 %collective-permute-start.7 = (bf16[128,1024]{1,0:T(8,128)(2,1)S(1)}, bf16[128,1024]{1,0:T(8,128)(2,1)S(1)}, u32[]{:S(2)}, u32[]{:S(2)}) collective-permute-start(bf16[128,1024]{1,0:T(8,128)(2,1)S(1)} %collective-permute-done.3), channel_id=1, source_target_pairs={{0,4},{4,8},{8,12},{12,16},{16,20},{20,24},{24,28},{28,0},{1,5},{5... | collective-permute-start | bytes 786440 | tf_op jit(solution)/shard_map/ppermute | solution.py:36
  31.4 6.4 %collective-permute-start.8 = (bf16[128,1024]{1,0:T(8,128)(2,1)S(1)}, bf16[128,1024]{1,0:T(8,128)(2,1)S(1)}, u32[]{:S(2)}, u32[]{:S(2)}) collective-permute-start(bf16[128,1024]{1,0:T(8,128)(2,1)S(1)} %collective-permute-done.4), channel_id=1, source_target_pairs={{0,28},{4,0},{8,4},{12,8},{16,12},{20,16},{24,20},{28,24},{1,29},{... | collective-permute-start | bytes 786440 | tf_op jit(solution)/shard_map/ppermute | solution.py:36
  41.8 6.5 %collective-permute-start.12 = (bf16[128,1024]{1,0:T(8,128)(2,1)S(1)}, bf16[128,1024]{1,0:T(8,128)(2,1)S(1)}, u32[]{:S(2)}, u32[]{:S(2)}) collective-permute-start(bf16[128,1024]{1,0:T(8,128)(2,1)S(1)} %collective-permute-done.7), channel_id=1, source_target_pairs={{0,4},{4,8},{8,12},{12,16},{16,20},{20,24},{24,28},{28,0},{1,5},{5... | collective-permute-start | bytes 786440 | tf_op jit(solution)/shard_map/ppermute | solution.py:36
  43.4 16.9 %collective-permute-start.11 = (bf16[512,1152]{1,0:T(8,128)(2,1)S(1)}, bf16[512,1152]{1,0:T(8,128)(2,1)S(1)}, u32[]{:S(2)}, u32[]{:S(2)}) collective-permute-start(bf16[512,1152]{1,0:T(8,128)(2,1)S(1)} %pad_maximum_fusion), channel_id=1, source_target_pairs={{0,130},{1,129},{2,128},{3,131},{32,162},{33,161},{34,160},{35,163... | collective-permute-start | bytes 3538952 | tf_op jit(solution)/shard_map/ppermute | solution.py:32
  44.9 15.3 %collective-permute-start.16 = (bf16[512,1152]{1,0:T(8,128)(2,1)S(1)}, bf16[512,1152]{1,0:T(8,128)(2,1)S(1)}, u32[]{:S(2)}, u32[]{:S(2)}) collective-permute-start(bf16[512,1152]{1,0:T(8,128)(2,1)S(1)} %pad_maximum_fusion.1), channel_id=1, source_target_pairs={{0,96},{1,33},{2,98},{3,35},{32,64},{33,1},{34,66},{35,3},{64,32},... | collective-permute-start | bytes 3538952 | tf_op jit(solution)/shard_map/ppermute | solution.py:32
  48.3 7.9 %collective-permute-start.14 = (bf16[128,1024]{1,0:T(8,128)(2,1)S(1)}, bf16[128,1024]{1,0:T(8,128)(2,1)S(1)}, u32[]{:S(2)}, u32[]{:S(2)}) collective-permute-start(bf16[128,1024]{1,0:T(8,128)(2,1)S(1)} %collective-permute-done.12), channel_id=1, source_target_pairs={{0,4},{4,8},{8,12},{12,16},{16,20},{20,24},{24,28},{28,0},{1,5},{5... | collective-permute-start | bytes 786440 | tf_op jit(solution)/shard_map/ppermute | solution.py:36
  62.0 11.6 %collective-permute-start.15 = (f32[512,512]{1,0:T(8,128)S(1)}, f32[512,512]{1,0:T(8,128)S(1)}, u32[]{:S(2)}, u32[]{:S(2)}) collective-permute-start(f32[512,512]{1,0:T(8,128)S(1)} %convolution_add_fusion.3), channel_id=1, source_target_pairs={{0,1},{1,0},{2,3},{3,2},{4,5},{5,4},{6,7},{7,6},{8,9},{9,8},{10,11... | collective-permute-start | bytes 3145736 | tf_op jit(solution)/shard_map/ppermute | solution.py:168
  81.8 9.5 %collective-permute-start.18 = (bf16[128,1024]{1,0:T(8,128)(2,1)S(1)}, bf16[128,1024]{1,0:T(8,128)(2,1)S(1)}, u32[]{:S(2)}, u32[]{:S(2)}) collective-permute-start(bf16[128,1024]{1,0:T(8,128)(2,1)S(1)} %pad_maximum_fusion.27), channel_id=1, source_target_pairs={{0,4},{4,8},{8,12},{12,16},{16,20},{20,24},{24,28},{28,0},{1,5},{5... | collective-permute-start | bytes 786440 | tf_op jit(solution)/shard_map/ppermute | solution.py:36
  81.9 9.4 %collective-permute-start.19 = (bf16[128,1024]{1,0:T(8,128)(2,1)S(1)}, bf16[128,1024]{1,0:T(8,128)(2,1)S(1)}, u32[]{:S(2)}, u32[]{:S(2)}) collective-permute-start(bf16[128,1024]{1,0:T(8,128)(2,1)S(1)} %pad_maximum_fusion.28), channel_id=1, source_target_pairs={{0,28},{4,0},{8,4},{12,8},{16,12},{20,16},{24,20},{28,24},{1,29},{... | collective-permute-start | bytes 786440 | tf_op jit(solution)/shard_map/ppermute | solution.py:36
  85.2 14.7 %collective-permute-start.22 = (bf16[512,1024]{1,0:T(8,128)(2,1)S(1)}, bf16[512,1024]{1,0:T(8,128)(2,1)S(1)}, u32[]{:S(2)}, u32[]{:S(2)}) collective-permute-start(bf16[512,1024]{1,0:T(8,128)(2,1)S(1)} %pad_maximum_fusion.9), channel_id=1, source_target_pairs={{0,130},{1,129},{2,128},{3,131},{32,162},{33,161},{34,160},{35,163... | collective-permute-start | bytes 3145736 | tf_op jit(solution)/shard_map/ppermute | solution.py:32
  85.7 14.2 %collective-permute-start.23 = (bf16[512,1024]{1,0:T(8,128)(2,1)S(1)}, bf16[512,1024]{1,0:T(8,128)(2,1)S(1)}, u32[]{:S(2)}, u32[]{:S(2)}) collective-permute-start(bf16[512,1024]{1,0:T(8,128)(2,1)S(1)} %bitcast.96), channel_id=1, source_target_pairs={{0,96},{1,33},{2,98},{3,35},{32,64},{33,1},{34,66},{35,3},{64,32},... | collective-permute-start | bytes 3145736 | tf_op jit(solution)/shard_map/ppermute | solution.py:32
  91.5 8.4 %collective-permute-start.20 = (bf16[128,1024]{1,0:T(8,128)(2,1)S(1)}, bf16[128,1024]{1,0:T(8,128)(2,1)S(1)}, u32[]{:S(2)}, u32[]{:S(2)}) collective-permute-start(bf16[128,1024]{1,0:T(8,128)(2,1)S(1)} %fusion.26), channel_id=1, source_target_pairs={{0,4},{4,8},{8,12},{12,16},{16,20},{20,24},{24,28},{28,0},{1,5},{5... | collective-permute-start | bytes 786440 | tf_op jit(solution)/shard_map/ppermute | solution.py:36
  91.6 8.3 %collective-permute-start.21 = (bf16[128,1024]{1,0:T(8,128)(2,1)S(1)}, bf16[128,1024]{1,0:T(8,128)(2,1)S(1)}, u32[]{:S(2)}, u32[]{:S(2)}) collective-permute-start(bf16[128,1024]{1,0:T(8,128)(2,1)S(1)} %fusion.27), channel_id=1, source_target_pairs={{0,28},{4,0},{8,4},{12,8},{16,12},{20,16},{24,20},{28,24},{1,29},{... | collective-permute-start | bytes 786440 | tf_op jit(solution)/shard_map/ppermute | solution.py:36
  100.5 9.6 %collective-permute-start.26 = (bf16[256,1024]{1,0:T(8,128)(2,1)S(1)}, bf16[256,1024]{1,0:T(8,128)(2,1)S(1)}, u32[]{:S(2)}, u32[]{:S(2)}) collective-permute-start(bf16[256,1024]{1,0:T(8,128)(2,1)S(1)} %add_convert_fusion), channel_id=1, source_target_pairs={{0,128},{1,131},{2,130},{3,129},{32,160},{33,163},{34,162},{35,161... | collective-permute-start | bytes 1572872 | tf_op jit(solution)/shard_map/ppermute | solution.py:32
  102.5 9.5 %collective-permute-start.27 = (bf16[256,1024]{1,0:T(8,128)(2,1)S(1)}, bf16[256,1024]{1,0:T(8,128)(2,1)S(1)}, u32[]{:S(2)}, u32[]{:S(2)}) collective-permute-start(bf16[256,1024]{1,0:T(8,128)(2,1)S(1)} %fusion.5), channel_id=1, source_target_pairs={{0,32},{1,97},{2,34},{3,99},{32,0},{33,65},{34,2},{35,67},{64,96},... | collective-permute-start | bytes 1572872 | tf_op jit(solution)/shard_map/ppermute | solution.py:32
  102.5 6.4 %collective-permute-start.24 = (bf16[128,1024]{1,0:T(8,128)(2,1)S(1)}, bf16[128,1024]{1,0:T(8,128)(2,1)S(1)}, u32[]{:S(2)}, u32[]{:S(2)}) collective-permute-start(bf16[128,1024]{1,0:T(8,128)(2,1)S(1)} %fusion.28), channel_id=1, source_target_pairs={{0,4},{4,8},{8,12},{12,16},{16,20},{20,24},{24,28},{28,0},{1,5},{5... | collective-permute-start | bytes 786440 | tf_op jit(solution)/shard_map/ppermute | solution.py:36
  102.5 6.4 %collective-permute-start.25 = (bf16[128,1024]{1,0:T(8,128)(2,1)S(1)}, bf16[128,1024]{1,0:T(8,128)(2,1)S(1)}, u32[]{:S(2)}, u32[]{:S(2)}) collective-permute-start(bf16[128,1024]{1,0:T(8,128)(2,1)S(1)} %fusion.29), channel_id=1, source_target_pairs={{0,28},{4,0},{8,4},{12,8},{16,12},{20,16},{24,20},{28,24},{1,29},{... | collective-permute-start | bytes 786440 | tf_op jit(solution)/shard_map/ppermute | solution.py:36
  114.0 7.1 %collective-permute-start.28 = (bf16[128,1024]{1,0:T(8,128)(2,1)}, bf16[128,1024]{1,0:T(8,128)(2,1)S(1)}, u32[]{:S(2)}, u32[]{:S(2)}) collective-permute-start(bf16[128,1024]{1,0:T(8,128)(2,1)} %fusion.30), channel_id=1, source_target_pairs={{0,4},{4,8},{8,12},{12,16},{16,20},{20,24},{24,28},{28,0},{1,5},{5... | collective-permute-start | bytes 786440 | tf_op jit(solution)/shard_map/ppermute | solution.py:36
  114.0 7.1 %collective-permute-start.29 = (bf16[128,1024]{1,0:T(8,128)(2,1)S(1)}, bf16[128,1024]{1,0:T(8,128)(2,1)}, u32[]{:S(2)}, u32[]{:S(2)}) collective-permute-start(bf16[128,1024]{1,0:T(8,128)(2,1)S(1)} %slice.613), channel_id=1, source_target_pairs={{0,96},{1,33},{2,98},{3,35},{32,64},{33,1},{34,66},{35,3},{64,32},... | collective-permute-start | bytes 786440 | tf_op jit(solution)/shard_map/ppermute | solution.py:32
  114.0 7.1 %collective-permute-start.30 = (bf16[128,1024]{1,0:T(8,128)(2,1)}, bf16[128,1024]{1,0:T(8,128)(2,1)}, u32[]{:S(2)}, u32[]{:S(2)}) collective-permute-start(bf16[128,1024]{1,0:T(8,128)(2,1)} %pad_maximum_fusion.29), channel_id=1, source_target_pairs={{0,130},{1,129},{2,128},{3,131},{32,162},{33,161},{34,160},{35,163... | collective-permute-start | bytes 786440 | tf_op jit(solution)/shard_map/ppermute | solution.py:32
  123.0 6.6 %collective-permute-start.31 = (bf16[64,1024]{1,0:T(8,128)(2,1)S(1)}, bf16[64,1024]{1,0:T(8,128)(2,1)S(1)}, u32[]{:S(2)}, u32[]{:S(2)}) collective-permute-start(bf16[64,1024]{1,0:T(8,128)(2,1)S(1)} %fusion.36), channel_id=1, source_target_pairs={{0,32},{1,97},{2,34},{3,99},{32,0},{33,65},{34,2},{35,67},{64,96},... | collective-permute-start | bytes 393224 | tf_op jit(solution)/shard_map/ppermute | solution.py:32
  127.2 8.0 %collective-permute-start.32 = (bf16[64,1024]{1,0:T(8,128)(2,1)S(1)}, bf16[64,1024]{1,0:T(8,128)(2,1)S(1)}, u32[]{:S(2)}, u32[]{:S(2)}) collective-permute-start(bf16[64,1024]{1,0:T(8,128)(2,1)S(1)} %add_convert_fusion.1), channel_id=1, source_target_pairs={{0,128},{1,131},{2,130},{3,129},{32,160},{33,163},{34,162},{35,161... | collective-permute-start | bytes 393224 | tf_op jit(solution)/shard_map/ppermute | solution.py:32
  127.4 9.6 %collective-permute-start.33 = (bf16[64,1024]{1,0:T(8,128)(2,1)S(1)}, bf16[64,1024]{1,0:T(8,128)(2,1)S(1)}, u32[]{:S(2)}, u32[]{:S(2)}) collective-permute-start(bf16[64,1024]{1,0:T(8,128)(2,1)S(1)} %get-tuple-element.139), channel_id=1, source_target_pairs={{0,2},{1,3},{2,0},{3,1},{32,34},{33,35},{34,32},{35,33},{64,66},{6... | collective-permute-start | bytes 393224 | tf_op jit(solution)/shard_map/ppermute | solution.py:32
  (2 other events, 8.0 us)

commit v3 on v2

--- a/solution.py
+++ b/solution.py
@@ -1,5 +1,6 @@
 import jax
 import jax.numpy as jnp
+import numpy as np
 from jax import lax
 from jax.experimental import pallas as pl
 from jax.experimental.pallas import tpu as pltpu
@@ -11,6 +12,7 @@
 PLANE = ("yl", "x", "yh", "c")
 bf16, f32 = jnp.bfloat16, jnp.float32
 NEAR, FAR = (1, 3), (3, 1)
+AROUND = np.array([0, 1, 7, 6, 2, 3, 5, 4], np.int32)
 HALF, WIDTH, LOADED = 64, 1024, 1152
 BLOCK, COLUMNS = 256, 512
 VMEM, SMEM = pltpu.VMEM, pltpu.SMEM
@@ -30,6 +32,15 @@
                     target = (((y_to % 2) * 4 + x_to) * 2 + y_to // 2) * 2 + core
                     pairs.append((((yl * 4 + x) * 2 + yh) * 2 + core, target))
     return lax.ppermute(value, PLANE, pairs)
+
+
+def exchange(value, turn):
+    pairs = []
+    for z in range(8):
+        for core in range(2):
+            step = 1 if (turn + core + z) % 2 == 0 else -1
+            pairs.append((z * 2 + core, (z + step) % 8 * 2 + core))
+    return lax.ppermute(value, ("z", "c"), pairs)
 
 
 def shift(value, step):
@@ -119,30 +130,36 @@
         [yh.astype(jnp.int32).reshape(1), queries, passages, *vectors],
     )
     place = jnp.arange(COLUMNS, dtype=jnp.int32)
-    owner = (yl * 4 + x) * 8 + (z + place // half) % 8
+    owner = (yl * 4 + x) * 8 + (z + np.repeat(AROUND, half)) % 8
     column = (owner * rows + yh * half + place % half)[None, :]
 
-    passage_back, top_near, low_near = together(
-        flip(passage_away, "y", (2, 2)), flip(top, "x", NEAR), flip(low, "y", NEAR)
-    )
-    ring = [None] * 8
-    ring[0], top, low = together(
-        jnp.concatenate([passage_own, passage_back]),
-        jnp.concatenate([top, top_near]),
-        jnp.concatenate([low, low_near]),
-    )
-    ring[7], ring[1], top_far, low_far = together(
-        shift(ring[0], 1), shift(ring[0], -1), flip(top, "x", FAR), flip(low, "y", FAR)
-    )
-    top, low = together(jnp.concatenate([top, top_far]), jnp.concatenate([low, low_far]))
-    ring[6], ring[2], top_near, low_near = together(
-        shift(ring[7], 1), shift(ring[1], -1), flip(top, "y", NEAR), flip(low, "x", NEAR)
-    )
+    passage_back = flip(passage_away, "y", (2, 2))
+    top_near, low_near = together(flip(top, "x", NEAR), flip(low, "y", NEAR))
+    passage = jnp.concatenate([passage_own, passage_back])
+    top, low = together(jnp.concatenate([top, top_near]), jnp.concatenate([low, low_near]))
+    passage_near, top_far, low_far = together(exchange(passage, 0), flip(top, "x", FAR), flip(low, "y", FAR))
+    ring, top, low = together(
+        jnp.concatenate([passage, passage_near]),
+        jnp.concatenate([top, top_far]),
+        jnp.concatenate([low, low_far]),
+    )
+    got, top_near, low_near = together(exchange(ring, 1), flip(top, "y", NEAR), flip(low, "x", NEAR))
     top, low = together(jnp.concatenate([top, top_near]), jnp.concatenate([low, low_near]))
     top_far, low_far = flip(top, "y", FAR), flip(low, "x", FAR)
-    ring[5], ring[3] = together(shift(ring[6], 1), shift(ring[2], -1))
-    ring[4] = shift(ring[5], 1)
-
+    ring = [passage, passage_near, got[:rows], got[rows:]]
+    for turn in (0, 1):
+        got = exchange(got, turn)
+        ring += [got[:rows], got[rows:]]
+    plus = (z + core) % 2 == 0
+
+    def in_order(blocks):
+        blocks = list(blocks)
+        for i in (1, 3, 5):
+            one, two = blocks[i : i + 2]
+            blocks[i : i + 2] = jnp.where(plus, one, two), jnp.where(plus, two, one)
+        return blocks
+
+    ring = in_order(ring)
     p_same = jnp.concatenate([b[:half] for b in ring])
     p_other = jnp.concatenate([b[half:] for b in ring])
 
@@ -196,6 +213,7 @@
     low_all = jnp.concatenate([same, other], axis=1)
     low_own, low_near, low_send = low_all[0], low_all[1], low_all[2:].reshape(2 * BLOCK, WIDTH).astype(bf16)
     top_got, low_got = flip(top_send, "y", FAR), flip(low_send, "x", FAR)
+    parts = dict(zip(AROUND.tolist(), parts))
     up, down = together(shift(parts[4].astype(bf16), 1), shift(parts[5].astype(bf16), -1))
     up, down = together((parts[3] + up).astype(bf16), (parts[6] + down).astype(bf16))
     up, down, top_got, low_got = together(shift(up, 1), shift(down, -1), top_got, low_got)
@@ -225,9 +243,9 @@
         jnp.concatenate([passage_own, passage_back]),
         jnp.concatenate([passage_back, passage_own]),
     )
-    top = top[:half] + top_got[:half] + top_last
-    low = low[:half] + low_got[:half] + low_last
-    query_grad = (inv_temp * jnp.concatenate([top, low])).astype(bf16)
+    top = (inv_temp * (top[:half] + top_got[:half] + top_last)).astype(bf16)
+    low = (inv_temp * (low[:half] + low_got[:half] + low_last)).astype(bf16)
+    query_grad = jnp.concatenate([top, low])
     return query_grad, passage_grad
 
 

time: 138 us -> 130 us (0.942)
  the two profiles are of different devices: /device:TPU:1 before, /device:TPU:36 now
where the time goes in v3:
time: 130 us; the launch traced here: 129 us
  waiting for transfers between devices  55.9 us (43%)
  starting transfers between devices  45.8 us (35%)
  other arithmetic  13.8 us (11%)
  matrix products  8.91 us (7%)
  Pallas kernels  1.97 us (2%)
  local copies, waits for them, and re-layouts  1.38 us (1%)
    ppermute x18, starting transfers between devices, flip(): return lax.ppermute(value, PLANE, pairs)  27.4 us
    ppermute x4, waiting for transfers between devices, exchange(): return lax.ppermute(value, ('z', 'c'), pairs)  24.9 us
    ppermute x7, waiting for transfers between devices, shift(): return lax.ppermute(value, 'z', [(i, (i + step) % 8) for i in range(8)])  19.1 us
    ppermute x18, waiting for transfers between devices, flip(): return lax.ppermute(value, PLANE, pairs)  11.7 us
    ppermute x7, starting transfers between devices, shift(): return lax.ppermute(value, 'z', [(i, (i + step) % 8) for i in range(8)])  10.4 us
    dot_general x12, matrix products, dot(): lax.dot_general(a, b, (contract, ((), ())), preferred_element_type=f32)  8.91 us
    ppermute x4, starting transfers between devices, exchange(): return lax.ppermute(value, ('z', 'c'), pairs)  7.16 us
  transfers between devices with their start and end apart: 31, of which 18 were waited for; matrix products, arithmetic and copies ran while one was open for 9% of the time, Pallas kernels for 0%

profile of v3, /device:TPU:36, one launch (start us, length us, event | category | flops | bytes accessed | tf_op | source)
XLA Modules:
  0.0 128.9 jit_solution(4962713604525904722)
XLA Ops:
  0.6 2.0 %shard_map.77 = (bf16[64,1152]{1,0:T(8,128)(2,1)}, bf16[64,1152]{1,0:T(8,128)(2,1)}, bf16[64,1024]{1,0:T(8,128)(2,1)}, bf16[64,1024]{1,0:T(8,128)(2,1)}) custom-call(s32[1]{0:T(128)} %bitcast.scalar, bf16[128,1024]{1,0:T(8,128)(2,1)} %refs_0_.1, bf16[128,1024]{1,0:T(8,128)(2,1)} %refs_1_.1, f32[1,128]{1,0:T(1,128)} %bitcast.98, f32[1,128]{1,0:T(1,128)} %bitcast.99, ...), custom_call_target="tpu_custom_call" | custom-call | bytes 1082884 | tf_op jit(solution)/shard_map/pallas_call | solution.py:105
  2.6 1.3 collective-permute-start.2
  3.9 1.6 %collective-permute-start.3 = (bf16[64,1152]{1,0:T(8,128)(2,1)}, bf16[64,1152]{1,0:T(8,128)(2,1)S(1)}, u32[]{:S(2)}, u32[]{:S(2)}) collective-permute-start(bf16[64,1152]{1,0:T(8,128)(2,1)} %get-tuple-element.46), channel_id=1, source_target_pairs={{0,128},{1,131},{2,130},{3,129},{32,160},{33,163},{34,162},{35,161... | collective-permute-start | bytes 442376 | tf_op jit(solution)/shard_map/ppermute | solution.py:34
  5.5 2.9 %collective-permute-start = (bf16[64,1024]{1,0:T(8,128)(2,1)}, bf16[64,1024]{1,0:T(8,128)(2,1)S(1)}, u32[]{:S(2)}, u32[]{:S(2)}) collective-permute-start(bf16[64,1024]{1,0:T(8,128)(2,1)} %get-tuple-element.44), channel_id=1, source_target_pairs={{0,2},{1,3},{2,0},{3,1},{32,34},{33,35},{34,32},{35,33},{64,66},{6... | collective-permute-start | bytes 393224 | tf_op jit(solution)/shard_map/ppermute | solution.py:34
  8.4 2.0 %collective-permute-done.3 = bf16[64,1152]{1,0:T(8,128)(2,1)S(1)} collective-permute-done((bf16[64,1152]{1,0:T(8,128)(2,1)}, bf16[64,1152]{1,0:T(8,128)(2,1)S(1)}, u32[]{:S(2)}, u32[]{:S(2)}) %collective-permute-start.3) | collective-permute-done | bytes 147488 | tf_op jit(solution)/shard_map/ppermute | solution.py:34
  11.6 3.0 %collective-permute-start.5 = (bf16[128,1152]{1,0:T(8,128)(2,1)S(1)}, bf16[128,1152]{1,0:T(8,128)(2,1)S(1)}, u32[]{:S(2)}, u32[]{:S(2)}) collective-permute-start(bf16[128,1152]{1,0:T(8,128)(2,1)S(1)} %get-tuple-element.50), channel_id=1, source_target_pairs={{0,130},{1,129},{2,128},{3,131},{32,162},{33,161},{34,160},{35,163... | collective-permute-start | bytes 884744 | tf_op jit(solution)/shard_map/ppermute | solution.py:34
  15.8 6.3 %collective-permute-done.1 = bf16[128,1024]{1,0:T(8,128)(2,1)S(1)} collective-permute-done((bf16[128,1024]{1,0:T(8,128)(2,1)S(1)}, bf16[128,1024]{1,0:T(8,128)(2,1)S(1)}, u32[]{:S(2)}, u32[]{:S(2)}) %collective-permute-start.1) | collective-permute-done | bytes 262176 | tf_op jit(solution)/shard_map/ppermute | solution.py:43
  23.5 1.9 %collective-permute-start.6 = (bf16[256,1024]{1,0:T(8,128)(2,1)S(1)}, bf16[256,1024]{1,0:T(8,128)(2,1)}, u32[]{:S(2)}, u32[]{:S(2)}) collective-permute-start(bf16[256,1024]{1,0:T(8,128)(2,1)S(1)} %pad_maximum_fusion.24), channel_id=1, source_target_pairs={{0,28},{1,5},{4,8},{5,1},{8,4},{9,13},{12,16},{13,9},{16,12},{17,2... | collective-permute-start | bytes 1572872 | tf_op jit(solution)/shard_map/ppermute | solution.py:43
  25.5 7.3 %collective-permute-done.6 = bf16[256,1024]{1,0:T(8,128)(2,1)} collective-permute-done((bf16[256,1024]{1,0:T(8,128)(2,1)S(1)}, bf16[256,1024]{1,0:T(8,128)(2,1)}, u32[]{:S(2)}, u32[]{:S(2)}) %collective-permute-start.6) | collective-permute-done | bytes 524320 | tf_op jit(solution)/shard_map/ppermute | solution.py:43
  32.8 3.9 %collective-permute-start.10 = (bf16[256,1024]{1,0:T(8,128)(2,1)}, bf16[256,1024]{1,0:T(8,128)(2,1)S(1)}, u32[]{:S(2)}, u32[]{:S(2)}) collective-permute-start(bf16[256,1024]{1,0:T(8,128)(2,1)} %collective-permute-done.6), channel_id=1, source_target_pairs={{0,4},{1,29},{4,0},{5,9},{8,12},{9,5},{12,8},{13,17},{16,20},{17,1... | collective-permute-start | bytes 1572872 | tf_op jit(solution)/shard_map/ppermute | solution.py:43
  38.1 2.5 %collective-permute-start.13 = (bf16[512,1152]{1,0:T(8,128)(2,1)S(1)}, bf16[512,1152]{1,0:T(8,128)(2,1)S(1)}, u32[]{:S(2)}, u32[]{:S(2)}) collective-permute-start(bf16[512,1152]{1,0:T(8,128)(2,1)S(1)} %pad_maximum_fusion.1), channel_id=1, source_target_pairs={{0,96},{1,33},{2,98},{3,35},{32,64},{33,1},{34,66},{35,3},{64,32},... | collective-permute-start | bytes 3538952 | tf_op jit(solution)/shard_map/ppermute | solution.py:34
  40.6 3.5 %collective-permute-done.10 = bf16[256,1024]{1,0:T(8,128)(2,1)S(1)} collective-permute-done((bf16[256,1024]{1,0:T(8,128)(2,1)}, bf16[256,1024]{1,0:T(8,128)(2,1)S(1)}, u32[]{:S(2)}, u32[]{:S(2)}) %collective-permute-start.10) | collective-permute-done | bytes 524320 | tf_op jit(solution)/shard_map/ppermute | solution.py:43
  45.5 7.8 %collective-permute-done.11 = bf16[256,1024]{1,0:T(8,128)(2,1)S(1)} collective-permute-done((bf16[256,1024]{1,0:T(8,128)(2,1)S(1)}, bf16[256,1024]{1,0:T(8,128)(2,1)S(1)}, u32[]{:S(2)}, u32[]{:S(2)}) %collective-permute-start.11) | collective-permute-done | bytes 524320 | tf_op jit(solution)/shard_map/ppermute | solution.py:43
  68.6 1.2 collective-permute-start.15
  69.8 2.2 %collective-permute-start.16 = (bf16[128,1024]{1,0:T(8,128)(2,1)S(1)}, bf16[128,1024]{1,0:T(8,128)(2,1)S(1)}, u32[]{:S(2)}, u32[]{:S(2)}) collective-permute-start(bf16[128,1024]{1,0:T(8,128)(2,1)S(1)} %pad_maximum_fusion.29), channel_id=1, source_target_pairs={{0,28},{4,0},{8,4},{12,8},{16,12},{20,16},{24,20},{28,24},{1,29},{... | collective-permute-start | bytes 786440 | tf_op jit(solution)/shard_map/ppermute | solution.py:47
  73.6 2.6 %collective-permute-start.20 = (bf16[512,1024]{1,0:T(8,128)(2,1)S(1)}, bf16[512,1024]{1,0:T(8,128)(2,1)S(1)}, u32[]{:S(2)}, u32[]{:S(2)}) collective-permute-start(bf16[512,1024]{1,0:T(8,128)(2,1)S(1)} %bitcast.96), channel_id=1, source_target_pairs={{0,96},{1,33},{2,98},{3,35},{32,64},{33,1},{34,66},{35,3},{64,32},... | collective-permute-start | bytes 3145736 | tf_op jit(solution)/shard_map/ppermute | solution.py:34
  76.5 2.3 %collective-permute-done.15 = bf16[128,1024]{1,0:T(8,128)(2,1)S(1)} collective-permute-done((bf16[128,1024]{1,0:T(8,128)(2,1)S(1)}, bf16[128,1024]{1,0:T(8,128)(2,1)S(1)}, u32[]{:S(2)}, u32[]{:S(2)}) %collective-permute-start.15) | collective-permute-done | bytes 262176 | tf_op jit(solution)/shard_map/ppermute | solution.py:47
  79.9 3.2 %collective-permute-start.17 = (bf16[128,1024]{1,0:T(8,128)(2,1)S(1)}, bf16[128,1024]{1,0:T(8,128)(2,1)S(1)}, u32[]{:S(2)}, u32[]{:S(2)}) collective-permute-start(bf16[128,1024]{1,0:T(8,128)(2,1)S(1)} %fusion.26), channel_id=1, source_target_pairs={{0,4},{4,8},{8,12},{12,16},{16,20},{20,24},{24,28},{28,0},{1,5},{5... | collective-permute-start | bytes 786440 | tf_op jit(solution)/shard_map/ppermute | solution.py:47
  83.1 5.4 %collective-permute-done.17 = bf16[128,1024]{1,0:T(8,128)(2,1)S(1)} collective-permute-done((bf16[128,1024]{1,0:T(8,128)(2,1)S(1)}, bf16[128,1024]{1,0:T(8,128)(2,1)S(1)}, u32[]{:S(2)}, u32[]{:S(2)}) %collective-permute-start.17) | collective-permute-done | bytes 262176 | tf_op jit(solution)/shard_map/ppermute | solution.py:47
  88.5 2.9 %collective-permute-done.18 = bf16[128,1024]{1,0:T(8,128)(2,1)S(1)} collective-permute-done((bf16[128,1024]{1,0:T(8,128)(2,1)S(1)}, bf16[128,1024]{1,0:T(8,128)(2,1)S(1)}, u32[]{:S(2)}, u32[]{:S(2)}) %collective-permute-start.18) | collective-permute-done | bytes 262176 | tf_op jit(solution)/shard_map/ppermute | solution.py:47
  92.0 2.2 %collective-permute-start.23 = (bf16[256,1024]{1,0:T(8,128)(2,1)S(1)}, bf16[256,1024]{1,0:T(8,128)(2,1)S(1)}, u32[]{:S(2)}, u32[]{:S(2)}) collective-permute-start(bf16[256,1024]{1,0:T(8,128)(2,1)S(1)} %add_convert_fusion), channel_id=1, source_target_pairs={{0,128},{1,131},{2,130},{3,129},{32,160},{33,163},{34,162},{35,161... | collective-permute-start | bytes 1572872 | tf_op jit(solution)/shard_map/ppermute | solution.py:34
  95.1 1.7 %collective-permute-start.21 = (bf16[128,1024]{1,0:T(8,128)(2,1)S(1)}, bf16[128,1024]{1,0:T(8,128)(2,1)S(1)}, u32[]{:S(2)}, u32[]{:S(2)}) collective-permute-start(bf16[128,1024]{1,0:T(8,128)(2,1)S(1)} %fusion.28), channel_id=1, source_target_pairs={{0,4},{4,8},{8,12},{12,16},{16,20},{20,24},{24,28},{28,0},{1,5},{5... | collective-permute-start | bytes 786440 | tf_op jit(solution)/shard_map/ppermute | solution.py:47
  97.1 4.7 %collective-permute-done.21 = bf16[128,1024]{1,0:T(8,128)(2,1)S(1)} collective-permute-done((bf16[128,1024]{1,0:T(8,128)(2,1)S(1)}, bf16[128,1024]{1,0:T(8,128)(2,1)S(1)}, u32[]{:S(2)}, u32[]{:S(2)}) %collective-permute-start.21) | collective-permute-done | bytes 262176 | tf_op jit(solution)/shard_map/ppermute | solution.py:47
  101.9 1.5 %collective-permute-done.22 = bf16[128,1024]{1,0:T(8,128)(2,1)S(1)} collective-permute-done((bf16[128,1024]{1,0:T(8,128)(2,1)S(1)}, bf16[128,1024]{1,0:T(8,128)(2,1)S(1)}, u32[]{:S(2)}, u32[]{:S(2)}) %collective-permute-start.22) | collective-permute-done | bytes 262176 | tf_op jit(solution)/shard_map/ppermute | solution.py:47
  106.1 1.7 %collective-permute-start.25 = (bf16[128,1024]{1,0:T(8,128)(2,1)}, bf16[128,1024]{1,0:T(8,128)(2,1)S(1)}, u32[]{:S(2)}, u32[]{:S(2)}) collective-permute-start(bf16[128,1024]{1,0:T(8,128)(2,1)} %fusion.30), channel_id=1, source_target_pairs={{0,4},{4,8},{8,12},{12,16},{16,20},{20,24},{24,28},{28,0},{1,5},{5... | collective-permute-start | bytes 786440 | tf_op jit(solution)/shard_map/ppermute | solution.py:47
  107.8 2.5 %collective-permute-start.26 = (bf16[128,1024]{1,0:T(8,128)(2,1)}, bf16[128,1024]{1,0:T(8,128)(2,1)}, u32[]{:S(2)}, u32[]{:S(2)}) collective-permute-start(bf16[128,1024]{1,0:T(8,128)(2,1)} %slice.659), channel_id=1, source_target_pairs={{0,96},{1,33},{2,98},{3,35},{32,64},{33,1},{34,66},{35,3},{64,32},... | collective-permute-start | bytes 786440 | tf_op jit(solution)/shard_map/ppermute | solution.py:34
  111.4 1.3 collective-permute-done.25
  112.7 2.4 %collective-permute-done.26 = bf16[128,1024]{1,0:T(8,128)(2,1)} collective-permute-done((bf16[128,1024]{1,0:T(8,128)(2,1)}, bf16[128,1024]{1,0:T(8,128)(2,1)}, u32[]{:S(2)}, u32[]{:S(2)}) %collective-permute-start.26) | collective-permute-done | bytes 262176 | tf_op jit(solution)/shard_map/ppermute | solution.py:34
  115.0 3.8 %collective-permute-done.27 = bf16[128,1024]{1,0:T(8,128)(2,1)S(1)} collective-permute-done((bf16[128,1024]{1,0:T(8,128)(2,1)}, bf16[128,1024]{1,0:T(8,128)(2,1)S(1)}, u32[]{:S(2)}, u32[]{:S(2)}) %collective-permute-start.27) | collective-permute-done | bytes 262176 | tf_op jit(solution)/shard_map/ppermute | solution.py:34
  119.8 1.6 %collective-permute-start.28 = (bf16[64,1024]{1,0:T(8,128)(2,1)S(1)}, bf16[64,1024]{1,0:T(8,128)(2,1)S(1)}, u32[]{:S(2)}, u32[]{:S(2)}) collective-permute-start(bf16[64,1024]{1,0:T(8,128)(2,1)S(1)} %fusion.37), channel_id=1, source_target_pairs={{0,32},{1,97},{2,34},{3,99},{32,0},{33,65},{34,2},{35,67},{64,96},... | collective-permute-start | bytes 393224 | tf_op jit(solution)/shard_map/ppermute | solution.py:34
  121.6 1.5 %collective-permute-start.30 = (bf16[64,1024]{1,0:T(8,128)(2,1)S(1)}, bf16[64,1024]{1,0:T(8,128)(2,1)S(1)}, u32[]{:S(2)}, u32[]{:S(2)}) collective-permute-start(bf16[64,1024]{1,0:T(8,128)(2,1)S(1)} %get-tuple-element.141), channel_id=1, source_target_pairs={{0,2},{1,3},{2,0},{3,1},{32,34},{33,35},{34,32},{35,33},{64,66},{6... | collective-permute-start | bytes 393224 | tf_op jit(solution)/shard_map/ppermute | solution.py:34
  123.1 1.8 %collective-permute-done.28 = bf16[64,1024]{1,0:T(8,128)(2,1)S(1)} collective-permute-done((bf16[64,1024]{1,0:T(8,128)(2,1)S(1)}, bf16[64,1024]{1,0:T(8,128)(2,1)S(1)}, u32[]{:S(2)}, u32[]{:S(2)}) %collective-permute-start.28) | collective-permute-done | bytes 131104 | tf_op jit(solution)/shard_map/ppermute | solution.py:34
  (112 shorter events, 34.9 us)
Async XLA Ops:
  2.6 19.5 %copy-start = (bf16[64,1024]{1,0:T(8,128)(2,1)S(1)}, bf16[64,1024]{1,0:T(8,128)(2,1)}, u32[]{:S(2)}) copy-start(bf16[64,1024]{1,0:T(8,128)(2,1)} %get-tuple-element.43) | copy-start | bytes 393220
  2.6 5.8 %collective-permute-start.2 = (bf16[64,1152]{1,0:T(8,128)(2,1)}, bf16[64,1152]{1,0:T(8,128)(2,1)S(1)}, u32[]{:S(2)}, u32[]{:S(2)}) collective-permute-start(bf16[64,1152]{1,0:T(8,128)(2,1)} %get-tuple-element.45), channel_id=1, source_target_pairs={{0,32},{1,97},{2,34},{3,99},{32,0},{33,65},{34,2},{35,67},{64,96},... | collective-permute-start | bytes 442376 | tf_op jit(solution)/shard_map/ppermute | solution.py:34
  3.9 6.5 %collective-permute-start.3 = (bf16[64,1152]{1,0:T(8,128)(2,1)}, bf16[64,1152]{1,0:T(8,128)(2,1)S(1)}, u32[]{:S(2)}, u32[]{:S(2)}) collective-permute-start(bf16[64,1152]{1,0:T(8,128)(2,1)} %get-tuple-element.46), channel_id=1, source_target_pairs={{0,128},{1,131},{2,130},{3,129},{32,160},{33,163},{34,162},{35,161... | collective-permute-start | bytes 442376 | tf_op jit(solution)/shard_map/ppermute | solution.py:34
  5.5 9.1 %collective-permute-start = (bf16[64,1024]{1,0:T(8,128)(2,1)}, bf16[64,1024]{1,0:T(8,128)(2,1)S(1)}, u32[]{:S(2)}, u32[]{:S(2)}) collective-permute-start(bf16[64,1024]{1,0:T(8,128)(2,1)} %get-tuple-element.44), channel_id=1, source_target_pairs={{0,2},{1,3},{2,0},{3,1},{32,34},{33,35},{34,32},{35,33},{64,66},{6... | collective-permute-start | bytes 393224 | tf_op jit(solution)/shard_map/ppermute | solution.py:34
  11.5 10.5 %collective-permute-start.4 = (bf16[128,1152]{1,0:T(8,128)(2,1)S(1)}, bf16[128,1152]{1,0:T(8,128)(2,1)S(1)}, u32[]{:S(2)}, u32[]{:S(2)}) collective-permute-start(bf16[128,1152]{1,0:T(8,128)(2,1)S(1)} %get-tuple-element.49), channel_id=1, source_target_pairs={{0,96},{1,33},{2,98},{3,35},{32,64},{33,1},{34,66},{35,3},{64,32},... | collective-permute-start | bytes 884744 | tf_op jit(solution)/shard_map/ppermute | solution.py:34
  11.6 10.4 %collective-permute-start.5 = (bf16[128,1152]{1,0:T(8,128)(2,1)S(1)}, bf16[128,1152]{1,0:T(8,128)(2,1)S(1)}, u32[]{:S(2)}, u32[]{:S(2)}) collective-permute-start(bf16[128,1152]{1,0:T(8,128)(2,1)S(1)} %get-tuple-element.50), channel_id=1, source_target_pairs={{0,130},{1,129},{2,128},{3,131},{32,162},{33,161},{34,160},{35,163... | collective-permute-start | bytes 884744 | tf_op jit(solution)/shard_map/ppermute | solution.py:34
  15.6 6.5 %collective-permute-start.1 = (bf16[128,1024]{1,0:T(8,128)(2,1)S(1)}, bf16[128,1024]{1,0:T(8,128)(2,1)S(1)}, u32[]{:S(2)}, u32[]{:S(2)}) collective-permute-start(bf16[128,1024]{1,0:T(8,128)(2,1)S(1)} %pad_maximum_fusion.27), channel_id=1, source_target_pairs={{0,4},{1,29},{4,0},{5,9},{8,12},{9,5},{12,8},{13,17},{16,20},{17,1... | collective-permute-start | bytes 786440 | tf_op jit(solution)/shard_map/ppermute | solution.py:43
  22.2 10.6 %collective-permute-start.7 = (bf16[256,1152]{1,0:T(8,128)(2,1)S(1)}, bf16[256,1152]{1,0:T(8,128)(2,1)S(1)}, u32[]{:S(2)}, u32[]{:S(2)}) collective-permute-start(bf16[256,1152]{1,0:T(8,128)(2,1)S(1)} %pad_maximum_fusion.18), channel_id=1, source_target_pairs={{0,128},{1,131},{2,130},{3,129},{32,160},{33,163},{34,162},{35,161... | collective-permute-start | bytes 1769480 | tf_op jit(solution)/shard_map/ppermute | solution.py:34
  22.4 10.4 %collective-permute-start.8 = (bf16[256,1152]{1,0:T(8,128)(2,1)S(1)}, bf16[256,1152]{1,0:T(8,128)(2,1)S(1)}, u32[]{:S(2)}, u32[]{:S(2)}) collective-permute-start(bf16[256,1152]{1,0:T(8,128)(2,1)S(1)} %pad_maximum_fusion.19), channel_id=1, source_target_pairs={{0,32},{1,97},{2,34},{3,99},{32,0},{33,65},{34,2},{35,67},{64,96},... | collective-permute-start | bytes 1769480 | tf_op jit(solution)/shard_map/ppermute | solution.py:34
  23.5 9.3 %collective-permute-start.6 = (bf16[256,1024]{1,0:T(8,128)(2,1)S(1)}, bf16[256,1024]{1,0:T(8,128)(2,1)}, u32[]{:S(2)}, u32[]{:S(2)}) collective-permute-start(bf16[256,1024]{1,0:T(8,128)(2,1)S(1)} %pad_maximum_fusion.24), channel_id=1, source_target_pairs={{0,28},{1,5},{4,8},{5,1},{8,4},{9,13},{12,16},{13,9},{16,12},{17,2... | collective-permute-start | bytes 1572872 | tf_op jit(solution)/shard_map/ppermute | solution.py:43
  32.8 11.3 %collective-permute-start.10 = (bf16[256,1024]{1,0:T(8,128)(2,1)}, bf16[256,1024]{1,0:T(8,128)(2,1)S(1)}, u32[]{:S(2)}, u32[]{:S(2)}) collective-permute-start(bf16[256,1024]{1,0:T(8,128)(2,1)} %collective-permute-done.6), channel_id=1, source_target_pairs={{0,4},{1,29},{4,0},{5,9},{8,12},{9,5},{12,8},{13,17},{16,20},{17,1... | collective-permute-start | bytes 1572872 | tf_op jit(solution)/shard_map/ppermute | solution.py:43
  37.0 17.7 %collective-permute-start.9 = (bf16[512,1152]{1,0:T(8,128)(2,1)S(1)}, bf16[512,1152]{1,0:T(8,128)(2,1)S(1)}, u32[]{:S(2)}, u32[]{:S(2)}) collective-permute-start(bf16[512,1152]{1,0:T(8,128)(2,1)S(1)} %pad_maximum_fusion), channel_id=1, source_target_pairs={{0,130},{1,129},{2,128},{3,131},{32,162},{33,161},{34,160},{35,163... | collective-permute-start | bytes 3538952 | tf_op jit(solution)/shard_map/ppermute | solution.py:34
  38.1 18.4 %collective-permute-start.13 = (bf16[512,1152]{1,0:T(8,128)(2,1)S(1)}, bf16[512,1152]{1,0:T(8,128)(2,1)S(1)}, u32[]{:S(2)}, u32[]{:S(2)}) collective-permute-start(bf16[512,1152]{1,0:T(8,128)(2,1)S(1)} %pad_maximum_fusion.1), channel_id=1, source_target_pairs={{0,96},{1,33},{2,98},{3,35},{32,64},{33,1},{34,66},{35,3},{64,32},... | collective-permute-start | bytes 3538952 | tf_op jit(solution)/shard_map/ppermute | solution.py:34
  44.1 9.2 %collective-permute-start.11 = (bf16[256,1024]{1,0:T(8,128)(2,1)S(1)}, bf16[256,1024]{1,0:T(8,128)(2,1)S(1)}, u32[]{:S(2)}, u32[]{:S(2)}) collective-permute-start(bf16[256,1024]{1,0:T(8,128)(2,1)S(1)} %collective-permute-done.10), channel_id=1, source_target_pairs={{0,28},{1,5},{4,8},{5,1},{8,4},{9,13},{12,16},{13,9},{16,12},{17,2... | collective-permute-start | bytes 1572872 | tf_op jit(solution)/shard_map/ppermute | solution.py:43
  56.4 4.4 %collective-permute-start.12 = (f32[512,512]{1,0:T(8,128)S(1)}, f32[512,512]{1,0:T(8,128)S(1)}, u32[]{:S(2)}, u32[]{:S(2)}) collective-permute-start(f32[512,512]{1,0:T(8,128)S(1)} %convolution_add_fusion.3), channel_id=1, source_target_pairs={{0,1},{1,0},{2,3},{3,2},{4,5},{5,4},{6,7},{7,6},{8,9},{9,8},{10,11... | collective-permute-start | bytes 3145736 | tf_op jit(solution)/shard_map/ppermute | solution.py:185
  58.2 3.0 %collective-permute-start.14 = (f32[512,512]{1,0:T(8,128)S(1)}, f32[512,512]{1,0:T(8,128)S(1)}, u32[]{:S(2)}, u32[]{:S(2)}) collective-permute-start(f32[512,512]{1,0:T(8,128)S(1)} %convolution_add_fusion.2), channel_id=1, source_target_pairs={{0,1},{1,0},{2,3},{3,2},{4,5},{5,4},{6,7},{7,6},{8,9},{9,8},{10,11... | collective-permute-start | bytes 3145736 | tf_op jit(solution)/shard_map/ppermute | solution.py:185
  68.6 10.2 %collective-permute-start.15 = (bf16[128,1024]{1,0:T(8,128)(2,1)S(1)}, bf16[128,1024]{1,0:T(8,128)(2,1)S(1)}, u32[]{:S(2)}, u32[]{:S(2)}) collective-permute-start(bf16[128,1024]{1,0:T(8,128)(2,1)S(1)} %pad_maximum_fusion.28), channel_id=1, source_target_pairs={{0,4},{4,8},{8,12},{12,16},{16,20},{20,24},{24,28},{28,0},{1,5},{5... | collective-permute-start | bytes 786440 | tf_op jit(solution)/shard_map/ppermute | solution.py:47
  69.8 9.9 %collective-permute-start.16 = (bf16[128,1024]{1,0:T(8,128)(2,1)S(1)}, bf16[128,1024]{1,0:T(8,128)(2,1)S(1)}, u32[]{:S(2)}, u32[]{:S(2)}) collective-permute-start(bf16[128,1024]{1,0:T(8,128)(2,1)S(1)} %pad_maximum_fusion.29), channel_id=1, source_target_pairs={{0,28},{4,0},{8,4},{12,8},{16,12},{20,16},{24,20},{28,24},{1,29},{... | collective-permute-start | bytes 786440 | tf_op jit(solution)/shard_map/ppermute | solution.py:47
  72.3 19.1 %collective-permute-start.19 = (bf16[512,1024]{1,0:T(8,128)(2,1)S(1)}, bf16[512,1024]{1,0:T(8,128)(2,1)S(1)}, u32[]{:S(2)}, u32[]{:S(2)}) collective-permute-start(bf16[512,1024]{1,0:T(8,128)(2,1)S(1)} %pad_maximum_fusion.9), channel_id=1, source_target_pairs={{0,130},{1,129},{2,128},{3,131},{32,162},{33,161},{34,160},{35,163... | collective-permute-start | bytes 3145736 | tf_op jit(solution)/shard_map/ppermute | solution.py:34
  73.6 17.9 %collective-permute-start.20 = (bf16[512,1024]{1,0:T(8,128)(2,1)S(1)}, bf16[512,1024]{1,0:T(8,128)(2,1)S(1)}, u32[]{:S(2)}, u32[]{:S(2)}) collective-permute-start(bf16[512,1024]{1,0:T(8,128)(2,1)S(1)} %bitcast.96), channel_id=1, source_target_pairs={{0,96},{1,33},{2,98},{3,35},{32,64},{33,1},{34,66},{35,3},{64,32},... | collective-permute-start | bytes 3145736 | tf_op jit(solution)/shard_map/ppermute | solution.py:34
  79.9 8.6 %collective-permute-start.17 = (bf16[128,1024]{1,0:T(8,128)(2,1)S(1)}, bf16[128,1024]{1,0:T(8,128)(2,1)S(1)}, u32[]{:S(2)}, u32[]{:S(2)}) collective-permute-start(bf16[128,1024]{1,0:T(8,128)(2,1)S(1)} %fusion.26), channel_id=1, source_target_pairs={{0,4},{4,8},{8,12},{12,16},{16,20},{20,24},{24,28},{28,0},{1,5},{5... | collective-permute-start | bytes 786440 | tf_op jit(solution)/shard_map/ppermute | solution.py:47
  83.1 8.4 %collective-permute-start.18 = (bf16[128,1024]{1,0:T(8,128)(2,1)S(1)}, bf16[128,1024]{1,0:T(8,128)(2,1)S(1)}, u32[]{:S(2)}, u32[]{:S(2)}) collective-permute-start(bf16[128,1024]{1,0:T(8,128)(2,1)S(1)} %fusion.27), channel_id=1, source_target_pairs={{0,28},{4,0},{8,4},{12,8},{16,12},{20,16},{24,20},{28,24},{1,29},{... | collective-permute-start | bytes 786440 | tf_op jit(solution)/shard_map/ppermute | solution.py:47
  92.0 11.3 %collective-permute-start.23 = (bf16[256,1024]{1,0:T(8,128)(2,1)S(1)}, bf16[256,1024]{1,0:T(8,128)(2,1)S(1)}, u32[]{:S(2)}, u32[]{:S(2)}) collective-permute-start(bf16[256,1024]{1,0:T(8,128)(2,1)S(1)} %add_convert_fusion), channel_id=1, source_target_pairs={{0,128},{1,131},{2,130},{3,129},{32,160},{33,163},{34,162},{35,161... | collective-permute-start | bytes 1572872 | tf_op jit(solution)/shard_map/ppermute | solution.py:34
  94.2 9.2 %collective-permute-start.24 = (bf16[256,1024]{1,0:T(8,128)(2,1)S(1)}, bf16[256,1024]{1,0:T(8,128)(2,1)S(1)}, u32[]{:S(2)}, u32[]{:S(2)}) collective-permute-start(bf16[256,1024]{1,0:T(8,128)(2,1)S(1)} %fusion.5), channel_id=1, source_target_pairs={{0,32},{1,97},{2,34},{3,99},{32,0},{33,65},{34,2},{35,67},{64,96},... | collective-permute-start | bytes 1572872 | tf_op jit(solution)/shard_map/ppermute | solution.py:34
  95.1 6.8 %collective-permute-start.21 = (bf16[128,1024]{1,0:T(8,128)(2,1)S(1)}, bf16[128,1024]{1,0:T(8,128)(2,1)S(1)}, u32[]{:S(2)}, u32[]{:S(2)}) collective-permute-start(bf16[128,1024]{1,0:T(8,128)(2,1)S(1)} %fusion.28), channel_id=1, source_target_pairs={{0,4},{4,8},{8,12},{12,16},{16,20},{20,24},{24,28},{28,0},{1,5},{5... | collective-permute-start | bytes 786440 | tf_op jit(solution)/shard_map/ppermute | solution.py:47
  96.8 6.5 %collective-permute-start.22 = (bf16[128,1024]{1,0:T(8,128)(2,1)S(1)}, bf16[128,1024]{1,0:T(8,128)(2,1)S(1)}, u32[]{:S(2)}, u32[]{:S(2)}) collective-permute-start(bf16[128,1024]{1,0:T(8,128)(2,1)S(1)} %fusion.29), channel_id=1, source_target_pairs={{0,28},{4,0},{8,4},{12,8},{16,12},{20,16},{24,20},{28,24},{1,29},{... | collective-permute-start | bytes 786440 | tf_op jit(solution)/shard_map/ppermute | solution.py:47
  106.1 6.6 %collective-permute-start.25 = (bf16[128,1024]{1,0:T(8,128)(2,1)}, bf16[128,1024]{1,0:T(8,128)(2,1)S(1)}, u32[]{:S(2)}, u32[]{:S(2)}) collective-permute-start(bf16[128,1024]{1,0:T(8,128)(2,1)} %fusion.30), channel_id=1, source_target_pairs={{0,4},{4,8},{8,12},{12,16},{16,20},{20,24},{24,28},{28,0},{1,5},{5... | collective-permute-start | bytes 786440 | tf_op jit(solution)/shard_map/ppermute | solution.py:47
  107.8 7.2 %collective-permute-start.26 = (bf16[128,1024]{1,0:T(8,128)(2,1)}, bf16[128,1024]{1,0:T(8,128)(2,1)}, u32[]{:S(2)}, u32[]{:S(2)}) collective-permute-start(bf16[128,1024]{1,0:T(8,128)(2,1)} %slice.659), channel_id=1, source_target_pairs={{0,96},{1,33},{2,98},{3,35},{32,64},{33,1},{34,66},{35,3},{64,32},... | collective-permute-start | bytes 786440 | tf_op jit(solution)/shard_map/ppermute | solution.py:34
  110.4 8.5 %collective-permute-start.27 = (bf16[128,1024]{1,0:T(8,128)(2,1)}, bf16[128,1024]{1,0:T(8,128)(2,1)S(1)}, u32[]{:S(2)}, u32[]{:S(2)}) collective-permute-start(bf16[128,1024]{1,0:T(8,128)(2,1)} %pad_maximum_fusion.30), channel_id=1, source_target_pairs={{0,130},{1,129},{2,128},{3,131},{32,162},{33,161},{34,160},{35,163... | collective-permute-start | bytes 786440 | tf_op jit(solution)/shard_map/ppermute | solution.py:34
  119.8 5.1 %collective-permute-start.28 = (bf16[64,1024]{1,0:T(8,128)(2,1)S(1)}, bf16[64,1024]{1,0:T(8,128)(2,1)S(1)}, u32[]{:S(2)}, u32[]{:S(2)}) collective-permute-start(bf16[64,1024]{1,0:T(8,128)(2,1)S(1)} %fusion.37), channel_id=1, source_target_pairs={{0,32},{1,97},{2,34},{3,99},{32,0},{33,65},{34,2},{35,67},{64,96},... | collective-permute-start | bytes 393224 | tf_op jit(solution)/shard_map/ppermute | solution.py:34
  121.4 5.0 %collective-permute-start.29 = (bf16[64,1024]{1,0:T(8,128)(2,1)S(1)}, bf16[64,1024]{1,0:T(8,128)(2,1)S(1)}, u32[]{:S(2)}, u32[]{:S(2)}) collective-permute-start(bf16[64,1024]{1,0:T(8,128)(2,1)S(1)} %add_convert_fusion.1), channel_id=1, source_target_pairs={{0,128},{1,131},{2,130},{3,129},{32,160},{33,163},{34,162},{35,161... | collective-permute-start | bytes 393224 | tf_op jit(solution)/shard_map/ppermute | solution.py:34
  121.6 6.6 %collective-permute-start.30 = (bf16[64,1024]{1,0:T(8,128)(2,1)S(1)}, bf16[64,1024]{1,0:T(8,128)(2,1)S(1)}, u32[]{:S(2)}, u32[]{:S(2)}) collective-permute-start(bf16[64,1024]{1,0:T(8,128)(2,1)S(1)} %get-tuple-element.141), channel_id=1, source_target_pairs={{0,2},{1,3},{2,0},{3,1},{32,34},{33,35},{34,32},{35,33},{64,66},{6... | collective-permute-start | bytes 393224 | tf_op jit(solution)/shard_map/ppermute | solution.py:34
  (1 other events, 10.8 us)

commit v4 on v3

--- a/solution.py
+++ b/solution.py
@@ -120,6 +120,7 @@
 def on_device(queries, passages, row_lse, row_weight, positive):
     x, z, yl, yh, core = (lax.axis_index(a) for a in ("x", "z", "yl", "yh", "c"))
     rows, half = 2 * HALF, HALF
+    flops = 2 * BLOCK * COLUMNS * WIDTH
     first_core = core == 0
 
     vectors = [value.reshape(1, rows) for value in (row_lse, row_weight, positive)]
@@ -217,27 +218,26 @@
     up, down = together(shift(parts[4].astype(bf16), 1), shift(parts[5].astype(bf16), -1))
     up, down = together((parts[3] + up).astype(bf16), (parts[6] + down).astype(bf16))
     up, down, top_got, low_got = together(shift(up, 1), shift(down, -1), top_got, low_got)
-    up, down, top_send, low_send = together(
-        (parts[2] + up).astype(bf16),
-        (parts[7] + down).astype(bf16),
-        (top_near + top_got[BLOCK:]).astype(bf16),
-        (low_near + low_got[BLOCK:]).astype(bf16),
-    )
-    up, down, top_last, low_last = together(
-        shift(up, 1), shift(down, -1), flip(top_send, "y", NEAR), flip(low_send, "x", NEAR)
-    )
+    up, down = together((parts[2] + up).astype(bf16), (parts[7] + down).astype(bf16))
+    up, down = together(shift(up, 1), shift(down, -1))
+    top_send, low_send = together(
+        (top_near + top_got[BLOCK:]).astype(bf16), (low_near + low_got[BLOCK:]).astype(bf16)
+    )
+    top_last, low_last = together(flip(top_send, "y", NEAR), flip(low_send, "x", NEAR))
     top = top_own + top_got[:BLOCK] + top_last
     low = low_own + low_got[:BLOCK] + low_last
     one, three = low[half:rows], low[rows + half :]
     low_near = jnp.where(first_core, one, three)
     low_send = jnp.concatenate([jnp.where(first_core, three, one), low[rows : rows + half]]).astype(bf16)
-    up, top_send, low_send = together((parts[1] + up).astype(bf16), top[rows:].astype(bf16), low_send)
-    up, top_got, low_got = together(shift(up, 1), flip(top_send, "x", FAR), flip(low_send, "y", FAR))
+    up = shift((parts[1] + up).astype(bf16), 1)
+    top_send, low_send = together(top[rows:].astype(bf16), low_send)
+    top_got, low_got = together(flip(top_send, "x", FAR), flip(low_send, "y", FAR))
     passage_sum = (inv_temp * (parts[0] + up + down)).astype(bf16)
     passage_own = passage_sum[:half]
     passage_back = flip(passage_sum[half:], "y", (2, 2))
     top_last = flip((top[half:rows] + top_got[half:]).astype(bf16), "x", NEAR)
     low_last = flip((low_near + low_got[half:]).astype(bf16), "y", NEAR)
+    passage_back, top_last, low_last = together(passage_back, top_last, low_last)
     passage_grad = jnp.where(
         yh == 0,
         jnp.concatenate([passage_own, passage_back]),

time: 130 us -> 129 us (level)
  starting transfers between devices: 45.8 us -> 51 us
  other arithmetic: 13.8 us -> 10.5 us
  waiting for transfers between devices: 55.9 us -> 54.3 us
    ppermute x18, starting transfers between devices: 27.4 us -> 32.4 us  [flip(): return lax.ppermute(value, PLANE, pairs)]
  transfers between devices with their start and end apart: 31 -> 31, of which waited for: 18 -> 16; matrix products, arithmetic and copies ran while one was open for 9% -> 8% of each run, Pallas kernels for 0% -> 0%
where the time goes in v4:
time: 129 us
  waiting for transfers between devices  54.3 us (42%)
  starting transfers between devices  51 us (40%)
  other arithmetic  10.5 us (8%)
  matrix products  8.91 us (7%)
  Pallas kernels  1.97 us (2%)
    ppermute x18, starting transfers between devices, flip(): return lax.ppermute(value, PLANE, pairs)  32.4 us
    ppermute x4, waiting for transfers between devices, exchange(): return lax.ppermute(value, ('z', 'c'), pairs)  24.9 us
    ppermute x7, waiting for transfers between devices, shift(): return lax.ppermute(value, 'z', [(i, (i + step) % 8) for i in range(8)])  18.2 us
    ppermute x18, waiting for transfers between devices, flip(): return lax.ppermute(value, PLANE, pairs)  10.9 us
    ppermute x7, starting transfers between devices, shift(): return lax.ppermute(value, 'z', [(i, (i + step) % 8) for i in range(8)])  10.6 us
    dot_general x12, matrix products, dot(): lax.dot_general(a, b, (contract, ((), ())), preferred_element_type=f32)  8.91 us
    ppermute x4, starting transfers between devices, exchange(): return lax.ppermute(value, ('z', 'c'), pairs)  7.16 us
  transfers between devices with their start and end apart: 31, of which 16 were waited for; matrix products, arithmetic and copies ran while one was open for 8% of the time, Pallas kernels for 0%

profile of v4, /device:TPU:36, one launch (start us, length us, event | category | flops | bytes accessed | tf_op | source)
XLA Modules:
  0.0 128.6 jit_solution(15527673097854737696)
XLA Ops:
  0.6 2.0 %shard_map.77 = (bf16[64,1152]{1,0:T(8,128)(2,1)}, bf16[64,1152]{1,0:T(8,128)(2,1)}, bf16[64,1024]{1,0:T(8,128)(2,1)}, bf16[64,1024]{1,0:T(8,128)(2,1)}) custom-call(s32[1]{0:T(128)} %bitcast.scalar, bf16[128,1024]{1,0:T(8,128)(2,1)} %refs_0_.1, bf16[128,1024]{1,0:T(8,128)(2,1)} %refs_1_.1, f32[1,128]{1,0:T(1,128)} %bitcast.98, f32[1,128]{1,0:T(1,128)} %bitcast.99, ...), custom_call_target="tpu_custom_call" | custom-call | bytes 1082884 | tf_op jit(solution)/shard_map/pallas_call | solution.py:105
  2.6 1.3 collective-permute-start.2
  3.9 1.6 %collective-permute-start.3 = (bf16[64,1152]{1,0:T(8,128)(2,1)}, bf16[64,1152]{1,0:T(8,128)(2,1)S(1)}, u32[]{:S(2)}, u32[]{:S(2)}) collective-permute-start(bf16[64,1152]{1,0:T(8,128)(2,1)} %get-tuple-element.47), channel_id=1, source_target_pairs={{0,128},{1,131},{2,130},{3,129},{32,160},{33,163},{34,162},{35,161... | collective-permute-start | bytes 442376 | tf_op jit(solution)/shard_map/ppermute | solution.py:34
  5.5 2.9 %collective-permute-start = (bf16[64,1024]{1,0:T(8,128)(2,1)}, bf16[64,1024]{1,0:T(8,128)(2,1)S(1)}, u32[]{:S(2)}, u32[]{:S(2)}) collective-permute-start(bf16[64,1024]{1,0:T(8,128)(2,1)} %get-tuple-element.45), channel_id=1, source_target_pairs={{0,2},{1,3},{2,0},{3,1},{32,34},{33,35},{34,32},{35,33},{64,66},{6... | collective-permute-start | bytes 393224 | tf_op jit(solution)/shard_map/ppermute | solution.py:34
  8.4 2.0 %collective-permute-done.3 = bf16[64,1152]{1,0:T(8,128)(2,1)S(1)} collective-permute-done((bf16[64,1152]{1,0:T(8,128)(2,1)}, bf16[64,1152]{1,0:T(8,128)(2,1)S(1)}, u32[]{:S(2)}, u32[]{:S(2)}) %collective-permute-start.3) | collective-permute-done | bytes 147488 | tf_op jit(solution)/shard_map/ppermute | solution.py:34
  11.6 3.0 %collective-permute-start.5 = (bf16[128,1152]{1,0:T(8,128)(2,1)S(1)}, bf16[128,1152]{1,0:T(8,128)(2,1)S(1)}, u32[]{:S(2)}, u32[]{:S(2)}) collective-permute-start(bf16[128,1152]{1,0:T(8,128)(2,1)S(1)} %get-tuple-element.51), channel_id=1, source_target_pairs={{0,130},{1,129},{2,128},{3,131},{32,162},{33,161},{34,160},{35,163... | collective-permute-start | bytes 884744 | tf_op jit(solution)/shard_map/ppermute | solution.py:34
  15.8 6.3 %collective-permute-done.1 = bf16[128,1024]{1,0:T(8,128)(2,1)S(1)} collective-permute-done((bf16[128,1024]{1,0:T(8,128)(2,1)S(1)}, bf16[128,1024]{1,0:T(8,128)(2,1)S(1)}, u32[]{:S(2)}, u32[]{:S(2)}) %collective-permute-start.1) | collective-permute-done | bytes 262176 | tf_op jit(solution)/shard_map/ppermute | solution.py:43
  23.5 1.9 %collective-permute-start.6 = (bf16[256,1024]{1,0:T(8,128)(2,1)S(1)}, bf16[256,1024]{1,0:T(8,128)(2,1)}, u32[]{:S(2)}, u32[]{:S(2)}) collective-permute-start(bf16[256,1024]{1,0:T(8,128)(2,1)S(1)} %pad_maximum_fusion.24), channel_id=1, source_target_pairs={{0,28},{1,5},{4,8},{5,1},{8,4},{9,13},{12,16},{13,9},{16,12},{17,2... | collective-permute-start | bytes 1572872 | tf_op jit(solution)/shard_map/ppermute | solution.py:43
  25.5 7.3 %collective-permute-done.6 = bf16[256,1024]{1,0:T(8,128)(2,1)} collective-permute-done((bf16[256,1024]{1,0:T(8,128)(2,1)S(1)}, bf16[256,1024]{1,0:T(8,128)(2,1)}, u32[]{:S(2)}, u32[]{:S(2)}) %collective-permute-start.6) | collective-permute-done | bytes 524320 | tf_op jit(solution)/shard_map/ppermute | solution.py:43
  32.8 3.9 %collective-permute-start.10 = (bf16[256,1024]{1,0:T(8,128)(2,1)}, bf16[256,1024]{1,0:T(8,128)(2,1)S(1)}, u32[]{:S(2)}, u32[]{:S(2)}) collective-permute-start(bf16[256,1024]{1,0:T(8,128)(2,1)} %collective-permute-done.6), channel_id=1, source_target_pairs={{0,4},{1,29},{4,0},{5,9},{8,12},{9,5},{12,8},{13,17},{16,20},{17,1... | collective-permute-start | bytes 1572872 | tf_op jit(solution)/shard_map/ppermute | solution.py:43
  38.1 2.5 %collective-permute-start.13 = (bf16[512,1152]{1,0:T(8,128)(2,1)S(1)}, bf16[512,1152]{1,0:T(8,128)(2,1)S(1)}, u32[]{:S(2)}, u32[]{:S(2)}) collective-permute-start(bf16[512,1152]{1,0:T(8,128)(2,1)S(1)} %pad_maximum_fusion.1), channel_id=1, source_target_pairs={{0,96},{1,33},{2,98},{3,35},{32,64},{33,1},{34,66},{35,3},{64,32},... | collective-permute-start | bytes 3538952 | tf_op jit(solution)/shard_map/ppermute | solution.py:34
  40.6 3.5 %collective-permute-done.10 = bf16[256,1024]{1,0:T(8,128)(2,1)S(1)} collective-permute-done((bf16[256,1024]{1,0:T(8,128)(2,1)}, bf16[256,1024]{1,0:T(8,128)(2,1)S(1)}, u32[]{:S(2)}, u32[]{:S(2)}) %collective-permute-start.10) | collective-permute-done | bytes 524320 | tf_op jit(solution)/shard_map/ppermute | solution.py:43
  45.5 7.8 %collective-permute-done.11 = bf16[256,1024]{1,0:T(8,128)(2,1)S(1)} collective-permute-done((bf16[256,1024]{1,0:T(8,128)(2,1)S(1)}, bf16[256,1024]{1,0:T(8,128)(2,1)S(1)}, u32[]{:S(2)}, u32[]{:S(2)}) %collective-permute-start.11) | collective-permute-done | bytes 524320 | tf_op jit(solution)/shard_map/ppermute | solution.py:43
  68.6 1.2 collective-permute-start.15
  69.8 2.2 %collective-permute-start.16 = (bf16[128,1024]{1,0:T(8,128)(2,1)S(1)}, bf16[128,1024]{1,0:T(8,128)(2,1)S(1)}, u32[]{:S(2)}, u32[]{:S(2)}) collective-permute-start(bf16[128,1024]{1,0:T(8,128)(2,1)S(1)} %pad_maximum_fusion.29), channel_id=1, source_target_pairs={{0,28},{4,0},{8,4},{12,8},{16,12},{20,16},{24,20},{28,24},{1,29},{... | collective-permute-start | bytes 786440 | tf_op jit(solution)/shard_map/ppermute | solution.py:47
  73.6 2.6 %collective-permute-start.20 = (bf16[512,1024]{1,0:T(8,128)(2,1)S(1)}, bf16[512,1024]{1,0:T(8,128)(2,1)S(1)}, u32[]{:S(2)}, u32[]{:S(2)}) collective-permute-start(bf16[512,1024]{1,0:T(8,128)(2,1)S(1)} %bitcast.96), channel_id=1, source_target_pairs={{0,96},{1,33},{2,98},{3,35},{32,64},{33,1},{34,66},{35,3},{64,32},... | collective-permute-start | bytes 3145736 | tf_op jit(solution)/shard_map/ppermute | solution.py:34
  76.5 2.3 %collective-permute-done.15 = bf16[128,1024]{1,0:T(8,128)(2,1)S(1)} collective-permute-done((bf16[128,1024]{1,0:T(8,128)(2,1)S(1)}, bf16[128,1024]{1,0:T(8,128)(2,1)S(1)}, u32[]{:S(2)}, u32[]{:S(2)}) %collective-permute-start.15) | collective-permute-done | bytes 262176 | tf_op jit(solution)/shard_map/ppermute | solution.py:47
  79.9 3.2 %collective-permute-start.17 = (bf16[128,1024]{1,0:T(8,128)(2,1)S(1)}, bf16[128,1024]{1,0:T(8,128)(2,1)S(1)}, u32[]{:S(2)}, u32[]{:S(2)}) collective-permute-start(bf16[128,1024]{1,0:T(8,128)(2,1)S(1)} %fusion.26), channel_id=1, source_target_pairs={{0,4},{4,8},{8,12},{12,16},{16,20},{20,24},{24,28},{28,0},{1,5},{5... | collective-permute-start | bytes 786440 | tf_op jit(solution)/shard_map/ppermute | solution.py:47
  83.1 5.4 %collective-permute-done.17 = bf16[128,1024]{1,0:T(8,128)(2,1)S(1)} collective-permute-done((bf16[128,1024]{1,0:T(8,128)(2,1)S(1)}, bf16[128,1024]{1,0:T(8,128)(2,1)S(1)}, u32[]{:S(2)}, u32[]{:S(2)}) %collective-permute-start.17) | collective-permute-done | bytes 262176 | tf_op jit(solution)/shard_map/ppermute | solution.py:47
  88.5 2.9 %collective-permute-done.18 = bf16[128,1024]{1,0:T(8,128)(2,1)S(1)} collective-permute-done((bf16[128,1024]{1,0:T(8,128)(2,1)S(1)}, bf16[128,1024]{1,0:T(8,128)(2,1)S(1)}, u32[]{:S(2)}, u32[]{:S(2)}) %collective-permute-start.18) | collective-permute-done | bytes 262176 | tf_op jit(solution)/shard_map/ppermute | solution.py:47
  91.9 2.2 %collective-permute-start.21 = (bf16[256,1024]{1,0:T(8,128)(2,1)S(1)}, bf16[256,1024]{1,0:T(8,128)(2,1)S(1)}, u32[]{:S(2)}, u32[]{:S(2)}) collective-permute-start(bf16[256,1024]{1,0:T(8,128)(2,1)S(1)} %add_convert_fusion), channel_id=1, source_target_pairs={{0,128},{1,131},{2,130},{3,129},{32,160},{33,163},{34,162},{35,161... | collective-permute-start | bytes 1572872 | tf_op jit(solution)/shard_map/ppermute | solution.py:34
  95.1 1.8 %collective-permute-start.25 = (bf16[128,1024]{1,0:T(8,128)(2,1)S(1)}, bf16[128,1024]{1,0:T(8,128)(2,1)S(1)}, u32[]{:S(2)}, u32[]{:S(2)}) collective-permute-start(bf16[128,1024]{1,0:T(8,128)(2,1)S(1)} %fusion.32), channel_id=1, source_target_pairs={{0,4},{4,8},{8,12},{12,16},{16,20},{20,24},{24,28},{28,0},{1,5},{5... | collective-permute-start | bytes 786440 | tf_op jit(solution)/shard_map/ppermute | solution.py:47
  97.2 4.7 %collective-permute-done.25 = bf16[128,1024]{1,0:T(8,128)(2,1)S(1)} collective-permute-done((bf16[128,1024]{1,0:T(8,128)(2,1)S(1)}, bf16[128,1024]{1,0:T(8,128)(2,1)S(1)}, u32[]{:S(2)}, u32[]{:S(2)}) %collective-permute-start.25) | collective-permute-done | bytes 262176 | tf_op jit(solution)/shard_map/ppermute | solution.py:47
  101.9 1.5 %collective-permute-done.26 = bf16[128,1024]{1,0:T(8,128)(2,1)S(1)} collective-permute-done((bf16[128,1024]{1,0:T(8,128)(2,1)S(1)}, bf16[128,1024]{1,0:T(8,128)(2,1)S(1)}, u32[]{:S(2)}, u32[]{:S(2)}) %collective-permute-start.26) | collective-permute-done | bytes 262176 | tf_op jit(solution)/shard_map/ppermute | solution.py:47
  103.5 1.8 %collective-permute-start.27 = (bf16[128,1024]{1,0:T(8,128)(2,1)S(1)}, bf16[128,1024]{1,0:T(8,128)(2,1)S(1)}, u32[]{:S(2)}, u32[]{:S(2)}) collective-permute-start(bf16[128,1024]{1,0:T(8,128)(2,1)S(1)} %fusion.31), channel_id=1, source_target_pairs={{0,4},{4,8},{8,12},{12,16},{16,20},{20,24},{24,28},{28,0},{1,5},{5... | collective-permute-start | bytes 786440 | tf_op jit(solution)/shard_map/ppermute | solution.py:47
  105.9 1.9 %collective-permute-start.23 = (bf16[128,1024]{1,0:T(8,128)(2,1)S(1)}, bf16[128,1024]{1,0:T(8,128)(2,1)S(1)}, u32[]{:S(2)}, u32[]{:S(2)}) collective-permute-start(bf16[128,1024]{1,0:T(8,128)(2,1)S(1)} %slice.659), channel_id=1, source_target_pairs={{0,96},{1,33},{2,98},{3,35},{32,64},{33,1},{34,66},{35,3},{64,32},... | collective-permute-start | bytes 786440 | tf_op jit(solution)/shard_map/ppermute | solution.py:34
  107.7 1.8 %collective-permute-start.24 = (bf16[128,1024]{1,0:T(8,128)(2,1)S(1)}, bf16[128,1024]{1,0:T(8,128)(2,1)S(1)}, u32[]{:S(2)}, u32[]{:S(2)}) collective-permute-start(bf16[128,1024]{1,0:T(8,128)(2,1)S(1)} %pad_maximum_fusion.30), channel_id=1, source_target_pairs={{0,130},{1,129},{2,128},{3,131},{32,162},{33,161},{34,160},{35,163... | collective-permute-start | bytes 786440 | tf_op jit(solution)/shard_map/ppermute | solution.py:34
  110.1 4.6 %collective-permute-start.28 = (bf16[64,1024]{1,0:T(8,128)(2,1)S(1)}, bf16[64,1024]{1,0:T(8,128)(2,1)S(1)}, u32[]{:S(2)}, u32[]{:S(2)}) collective-permute-start(bf16[64,1024]{1,0:T(8,128)(2,1)S(1)} %get-tuple-element.143), channel_id=1, source_target_pairs={{0,2},{1,3},{2,0},{3,1},{32,34},{33,35},{34,32},{35,33},{64,66},{6... | collective-permute-start | bytes 393224 | tf_op jit(solution)/shard_map/ppermute | solution.py:34
  114.7 3.8 %collective-permute-done.24 = bf16[128,1024]{1,0:T(8,128)(2,1)S(1)} collective-permute-done((bf16[128,1024]{1,0:T(8,128)(2,1)S(1)}, bf16[128,1024]{1,0:T(8,128)(2,1)S(1)}, u32[]{:S(2)}, u32[]{:S(2)}) %collective-permute-start.24) | collective-permute-done | bytes 262176 | tf_op jit(solution)/shard_map/ppermute | solution.py:34
  118.6 3.4 %collective-permute-start.29 = (bf16[64,1024]{1,0:T(8,128)(2,1)S(1)}, bf16[64,1024]{1,0:T(8,128)(2,1)S(1)}, u32[]{:S(2)}, u32[]{:S(2)}) collective-permute-start(bf16[64,1024]{1,0:T(8,128)(2,1)S(1)} %fusion.37), channel_id=1, source_target_pairs={{0,32},{1,97},{2,34},{3,99},{32,0},{33,65},{34,2},{35,67},{64,96},... | collective-permute-start | bytes 393224 | tf_op jit(solution)/shard_map/ppermute | solution.py:34
  122.0 2.9 %collective-permute-done.29 = bf16[64,1024]{1,0:T(8,128)(2,1)S(1)} collective-permute-done((bf16[64,1024]{1,0:T(8,128)(2,1)S(1)}, bf16[64,1024]{1,0:T(8,128)(2,1)S(1)}, u32[]{:S(2)}, u32[]{:S(2)}) %collective-permute-start.29) | collective-permute-done | bytes 131104 | tf_op jit(solution)/shard_map/ppermute | solution.py:34
  124.9 2.0 %collective-permute-done.30 = bf16[64,1024]{1,0:T(8,128)(2,1)S(1)} collective-permute-done((bf16[64,1024]{1,0:T(8,128)(2,1)S(1)}, bf16[64,1024]{1,0:T(8,128)(2,1)S(1)}, u32[]{:S(2)}, u32[]{:S(2)}) %collective-permute-start.30) | collective-permute-done | bytes 131104 | tf_op jit(solution)/shard_map/ppermute | solution.py:34
  (112 shorter events, 28.9 us)
Async XLA Ops:
  2.6 19.5 %copy-start = (bf16[64,1024]{1,0:T(8,128)(2,1)S(1)}, bf16[64,1024]{1,0:T(8,128)(2,1)}, u32[]{:S(2)}) copy-start(bf16[64,1024]{1,0:T(8,128)(2,1)} %get-tuple-element.44) | copy-start | bytes 393220
  2.6 5.8 %collective-permute-start.2 = (bf16[64,1152]{1,0:T(8,128)(2,1)}, bf16[64,1152]{1,0:T(8,128)(2,1)S(1)}, u32[]{:S(2)}, u32[]{:S(2)}) collective-permute-start(bf16[64,1152]{1,0:T(8,128)(2,1)} %get-tuple-element.46), channel_id=1, source_target_pairs={{0,32},{1,97},{2,34},{3,99},{32,0},{33,65},{34,2},{35,67},{64,96},... | collective-permute-start | bytes 442376 | tf_op jit(solution)/shard_map/ppermute | solution.py:34
  3.9 6.5 %collective-permute-start.3 = (bf16[64,1152]{1,0:T(8,128)(2,1)}, bf16[64,1152]{1,0:T(8,128)(2,1)S(1)}, u32[]{:S(2)}, u32[]{:S(2)}) collective-permute-start(bf16[64,1152]{1,0:T(8,128)(2,1)} %get-tuple-element.47), channel_id=1, source_target_pairs={{0,128},{1,131},{2,130},{3,129},{32,160},{33,163},{34,162},{35,161... | collective-permute-start | bytes 442376 | tf_op jit(solution)/shard_map/ppermute | solution.py:34
  5.5 9.1 %collective-permute-start = (bf16[64,1024]{1,0:T(8,128)(2,1)}, bf16[64,1024]{1,0:T(8,128)(2,1)S(1)}, u32[]{:S(2)}, u32[]{:S(2)}) collective-permute-start(bf16[64,1024]{1,0:T(8,128)(2,1)} %get-tuple-element.45), channel_id=1, source_target_pairs={{0,2},{1,3},{2,0},{3,1},{32,34},{33,35},{34,32},{35,33},{64,66},{6... | collective-permute-start | bytes 393224 | tf_op jit(solution)/shard_map/ppermute | solution.py:34
  11.5 10.5 %collective-permute-start.4 = (bf16[128,1152]{1,0:T(8,128)(2,1)S(1)}, bf16[128,1152]{1,0:T(8,128)(2,1)S(1)}, u32[]{:S(2)}, u32[]{:S(2)}) collective-permute-start(bf16[128,1152]{1,0:T(8,128)(2,1)S(1)} %get-tuple-element.50), channel_id=1, source_target_pairs={{0,96},{1,33},{2,98},{3,35},{32,64},{33,1},{34,66},{35,3},{64,32},... | collective-permute-start | bytes 884744 | tf_op jit(solution)/shard_map/ppermute | solution.py:34
  11.6 10.4 %collective-permute-start.5 = (bf16[128,1152]{1,0:T(8,128)(2,1)S(1)}, bf16[128,1152]{1,0:T(8,128)(2,1)S(1)}, u32[]{:S(2)}, u32[]{:S(2)}) collective-permute-start(bf16[128,1152]{1,0:T(8,128)(2,1)S(1)} %get-tuple-element.51), channel_id=1, source_target_pairs={{0,130},{1,129},{2,128},{3,131},{32,162},{33,161},{34,160},{35,163... | collective-permute-start | bytes 884744 | tf_op jit(solution)/shard_map/ppermute | solution.py:34
  15.6 6.5 %collective-permute-start.1 = (bf16[128,1024]{1,0:T(8,128)(2,1)S(1)}, bf16[128,1024]{1,0:T(8,128)(2,1)S(1)}, u32[]{:S(2)}, u32[]{:S(2)}) collective-permute-start(bf16[128,1024]{1,0:T(8,128)(2,1)S(1)} %pad_maximum_fusion.27), channel_id=1, source_target_pairs={{0,4},{1,29},{4,0},{5,9},{8,12},{9,5},{12,8},{13,17},{16,20},{17,1... | collective-permute-start | bytes 786440 | tf_op jit(solution)/shard_map/ppermute | solution.py:43
  22.2 10.6 %collective-permute-start.7 = (bf16[256,1152]{1,0:T(8,128)(2,1)S(1)}, bf16[256,1152]{1,0:T(8,128)(2,1)S(1)}, u32[]{:S(2)}, u32[]{:S(2)}) collective-permute-start(bf16[256,1152]{1,0:T(8,128)(2,1)S(1)} %pad_maximum_fusion.18), channel_id=1, source_target_pairs={{0,128},{1,131},{2,130},{3,129},{32,160},{33,163},{34,162},{35,161... | collective-permute-start | bytes 1769480 | tf_op jit(solution)/shard_map/ppermute | solution.py:34
  22.4 10.4 %collective-permute-start.8 = (bf16[256,1152]{1,0:T(8,128)(2,1)S(1)}, bf16[256,1152]{1,0:T(8,128)(2,1)S(1)}, u32[]{:S(2)}, u32[]{:S(2)}) collective-permute-start(bf16[256,1152]{1,0:T(8,128)(2,1)S(1)} %pad_maximum_fusion.19), channel_id=1, source_target_pairs={{0,32},{1,97},{2,34},{3,99},{32,0},{33,65},{34,2},{35,67},{64,96},... | collective-permute-start | bytes 1769480 | tf_op jit(solution)/shard_map/ppermute | solution.py:34
  23.5 9.3 %collective-permute-start.6 = (bf16[256,1024]{1,0:T(8,128)(2,1)S(1)}, bf16[256,1024]{1,0:T(8,128)(2,1)}, u32[]{:S(2)}, u32[]{:S(2)}) collective-permute-start(bf16[256,1024]{1,0:T(8,128)(2,1)S(1)} %pad_maximum_fusion.24), channel_id=1, source_target_pairs={{0,28},{1,5},{4,8},{5,1},{8,4},{9,13},{12,16},{13,9},{16,12},{17,2... | collective-permute-start | bytes 1572872 | tf_op jit(solution)/shard_map/ppermute | solution.py:43
  32.8 11.3 %collective-permute-start.10 = (bf16[256,1024]{1,0:T(8,128)(2,1)}, bf16[256,1024]{1,0:T(8,128)(2,1)S(1)}, u32[]{:S(2)}, u32[]{:S(2)}) collective-permute-start(bf16[256,1024]{1,0:T(8,128)(2,1)} %collective-permute-done.6), channel_id=1, source_target_pairs={{0,4},{1,29},{4,0},{5,9},{8,12},{9,5},{12,8},{13,17},{16,20},{17,1... | collective-permute-start | bytes 1572872 | tf_op jit(solution)/shard_map/ppermute | solution.py:43
  37.0 17.7 %collective-permute-start.9 = (bf16[512,1152]{1,0:T(8,128)(2,1)S(1)}, bf16[512,1152]{1,0:T(8,128)(2,1)S(1)}, u32[]{:S(2)}, u32[]{:S(2)}) collective-permute-start(bf16[512,1152]{1,0:T(8,128)(2,1)S(1)} %pad_maximum_fusion), channel_id=1, source_target_pairs={{0,130},{1,129},{2,128},{3,131},{32,162},{33,161},{34,160},{35,163... | collective-permute-start | bytes 3538952 | tf_op jit(solution)/shard_map/ppermute | solution.py:34
  38.1 18.4 %collective-permute-start.13 = (bf16[512,1152]{1,0:T(8,128)(2,1)S(1)}, bf16[512,1152]{1,0:T(8,128)(2,1)S(1)}, u32[]{:S(2)}, u32[]{:S(2)}) collective-permute-start(bf16[512,1152]{1,0:T(8,128)(2,1)S(1)} %pad_maximum_fusion.1), channel_id=1, source_target_pairs={{0,96},{1,33},{2,98},{3,35},{32,64},{33,1},{34,66},{35,3},{64,32},... | collective-permute-start | bytes 3538952 | tf_op jit(solution)/shard_map/ppermute | solution.py:34
  44.1 9.2 %collective-permute-start.11 = (bf16[256,1024]{1,0:T(8,128)(2,1)S(1)}, bf16[256,1024]{1,0:T(8,128)(2,1)S(1)}, u32[]{:S(2)}, u32[]{:S(2)}) collective-permute-start(bf16[256,1024]{1,0:T(8,128)(2,1)S(1)} %collective-permute-done.10), channel_id=1, source_target_pairs={{0,28},{1,5},{4,8},{5,1},{8,4},{9,13},{12,16},{13,9},{16,12},{17,2... | collective-permute-start | bytes 1572872 | tf_op jit(solution)/shard_map/ppermute | solution.py:43
  56.4 4.4 %collective-permute-start.12 = (f32[512,512]{1,0:T(8,128)S(1)}, f32[512,512]{1,0:T(8,128)S(1)}, u32[]{:S(2)}, u32[]{:S(2)}) collective-permute-start(f32[512,512]{1,0:T(8,128)S(1)} %convolution_add_fusion.3), channel_id=1, source_target_pairs={{0,1},{1,0},{2,3},{3,2},{4,5},{5,4},{6,7},{7,6},{8,9},{9,8},{10,11... | collective-permute-start | bytes 3145736 | tf_op jit(solution)/shard_map/ppermute | solution.py:186
  58.2 3.0 %collective-permute-start.14 = (f32[512,512]{1,0:T(8,128)S(1)}, f32[512,512]{1,0:T(8,128)S(1)}, u32[]{:S(2)}, u32[]{:S(2)}) collective-permute-start(f32[512,512]{1,0:T(8,128)S(1)} %convolution_add_fusion.2), channel_id=1, source_target_pairs={{0,1},{1,0},{2,3},{3,2},{4,5},{5,4},{6,7},{7,6},{8,9},{9,8},{10,11... | collective-permute-start | bytes 3145736 | tf_op jit(solution)/shard_map/ppermute | solution.py:186
  68.6 10.2 %collective-permute-start.15 = (bf16[128,1024]{1,0:T(8,128)(2,1)S(1)}, bf16[128,1024]{1,0:T(8,128)(2,1)S(1)}, u32[]{:S(2)}, u32[]{:S(2)}) collective-permute-start(bf16[128,1024]{1,0:T(8,128)(2,1)S(1)} %pad_maximum_fusion.28), channel_id=1, source_target_pairs={{0,4},{4,8},{8,12},{12,16},{16,20},{20,24},{24,28},{28,0},{1,5},{5... | collective-permute-start | bytes 786440 | tf_op jit(solution)/shard_map/ppermute | solution.py:47
  69.8 9.9 %collective-permute-start.16 = (bf16[128,1024]{1,0:T(8,128)(2,1)S(1)}, bf16[128,1024]{1,0:T(8,128)(2,1)S(1)}, u32[]{:S(2)}, u32[]{:S(2)}) collective-permute-start(bf16[128,1024]{1,0:T(8,128)(2,1)S(1)} %pad_maximum_fusion.29), channel_id=1, source_target_pairs={{0,28},{4,0},{8,4},{12,8},{16,12},{20,16},{24,20},{28,24},{1,29},{... | collective-permute-start | bytes 786440 | tf_op jit(solution)/shard_map/ppermute | solution.py:47
  72.3 19.1 %collective-permute-start.19 = (bf16[512,1024]{1,0:T(8,128)(2,1)S(1)}, bf16[512,1024]{1,0:T(8,128)(2,1)S(1)}, u32[]{:S(2)}, u32[]{:S(2)}) collective-permute-start(bf16[512,1024]{1,0:T(8,128)(2,1)S(1)} %pad_maximum_fusion.9), channel_id=1, source_target_pairs={{0,130},{1,129},{2,128},{3,131},{32,162},{33,161},{34,160},{35,163... | collective-permute-start | bytes 3145736 | tf_op jit(solution)/shard_map/ppermute | solution.py:34
  73.6 17.9 %collective-permute-start.20 = (bf16[512,1024]{1,0:T(8,128)(2,1)S(1)}, bf16[512,1024]{1,0:T(8,128)(2,1)S(1)}, u32[]{:S(2)}, u32[]{:S(2)}) collective-permute-start(bf16[512,1024]{1,0:T(8,128)(2,1)S(1)} %bitcast.96), channel_id=1, source_target_pairs={{0,96},{1,33},{2,98},{3,35},{32,64},{33,1},{34,66},{35,3},{64,32},... | collective-permute-start | bytes 3145736 | tf_op jit(solution)/shard_map/ppermute | solution.py:34
  79.9 8.6 %collective-permute-start.17 = (bf16[128,1024]{1,0:T(8,128)(2,1)S(1)}, bf16[128,1024]{1,0:T(8,128)(2,1)S(1)}, u32[]{:S(2)}, u32[]{:S(2)}) collective-permute-start(bf16[128,1024]{1,0:T(8,128)(2,1)S(1)} %fusion.26), channel_id=1, source_target_pairs={{0,4},{4,8},{8,12},{12,16},{16,20},{20,24},{24,28},{28,0},{1,5},{5... | collective-permute-start | bytes 786440 | tf_op jit(solution)/shard_map/ppermute | solution.py:47
  83.1 8.4 %collective-permute-start.18 = (bf16[128,1024]{1,0:T(8,128)(2,1)S(1)}, bf16[128,1024]{1,0:T(8,128)(2,1)S(1)}, u32[]{:S(2)}, u32[]{:S(2)}) collective-permute-start(bf16[128,1024]{1,0:T(8,128)(2,1)S(1)} %fusion.27), channel_id=1, source_target_pairs={{0,28},{4,0},{8,4},{12,8},{16,12},{20,16},{24,20},{28,24},{1,29},{... | collective-permute-start | bytes 786440 | tf_op jit(solution)/shard_map/ppermute | solution.py:47
  91.9 13.4 %collective-permute-start.21 = (bf16[256,1024]{1,0:T(8,128)(2,1)S(1)}, bf16[256,1024]{1,0:T(8,128)(2,1)S(1)}, u32[]{:S(2)}, u32[]{:S(2)}) collective-permute-start(bf16[256,1024]{1,0:T(8,128)(2,1)S(1)} %add_convert_fusion), channel_id=1, source_target_pairs={{0,128},{1,131},{2,130},{3,129},{32,160},{33,163},{34,162},{35,161... | collective-permute-start | bytes 1572872 | tf_op jit(solution)/shard_map/ppermute | solution.py:34
  94.1 11.2 %collective-permute-start.22 = (bf16[256,1024]{1,0:T(8,128)(2,1)S(1)}, bf16[256,1024]{1,0:T(8,128)(2,1)S(1)}, u32[]{:S(2)}, u32[]{:S(2)}) collective-permute-start(bf16[256,1024]{1,0:T(8,128)(2,1)S(1)} %fusion.5), channel_id=1, source_target_pairs={{0,32},{1,97},{2,34},{3,99},{32,0},{33,65},{34,2},{35,67},{64,96},... | collective-permute-start | bytes 1572872 | tf_op jit(solution)/shard_map/ppermute | solution.py:34
  95.1 6.8 %collective-permute-start.25 = (bf16[128,1024]{1,0:T(8,128)(2,1)S(1)}, bf16[128,1024]{1,0:T(8,128)(2,1)S(1)}, u32[]{:S(2)}, u32[]{:S(2)}) collective-permute-start(bf16[128,1024]{1,0:T(8,128)(2,1)S(1)} %fusion.32), channel_id=1, source_target_pairs={{0,4},{4,8},{8,12},{12,16},{16,20},{20,24},{24,28},{28,0},{1,5},{5... | collective-permute-start | bytes 786440 | tf_op jit(solution)/shard_map/ppermute | solution.py:47
  96.9 6.5 %collective-permute-start.26 = (bf16[128,1024]{1,0:T(8,128)(2,1)S(1)}, bf16[128,1024]{1,0:T(8,128)(2,1)S(1)}, u32[]{:S(2)}, u32[]{:S(2)}) collective-permute-start(bf16[128,1024]{1,0:T(8,128)(2,1)S(1)} %fusion.33), channel_id=1, source_target_pairs={{0,28},{4,0},{8,4},{12,8},{16,12},{20,16},{24,20},{28,24},{1,29},{... | collective-permute-start | bytes 786440 | tf_op jit(solution)/shard_map/ppermute | solution.py:47
  103.5 6.4 %collective-permute-start.27 = (bf16[128,1024]{1,0:T(8,128)(2,1)S(1)}, bf16[128,1024]{1,0:T(8,128)(2,1)S(1)}, u32[]{:S(2)}, u32[]{:S(2)}) collective-permute-start(bf16[128,1024]{1,0:T(8,128)(2,1)S(1)} %fusion.31), channel_id=1, source_target_pairs={{0,4},{4,8},{8,12},{12,16},{16,20},{20,24},{24,28},{28,0},{1,5},{5... | collective-permute-start | bytes 786440 | tf_op jit(solution)/shard_map/ppermute | solution.py:47
  105.9 8.8 %collective-permute-start.23 = (bf16[128,1024]{1,0:T(8,128)(2,1)S(1)}, bf16[128,1024]{1,0:T(8,128)(2,1)S(1)}, u32[]{:S(2)}, u32[]{:S(2)}) collective-permute-start(bf16[128,1024]{1,0:T(8,128)(2,1)S(1)} %slice.659), channel_id=1, source_target_pairs={{0,96},{1,33},{2,98},{3,35},{32,64},{33,1},{34,66},{35,3},{64,32},... | collective-permute-start | bytes 786440 | tf_op jit(solution)/shard_map/ppermute | solution.py:34
  107.7 10.8 %collective-permute-start.24 = (bf16[128,1024]{1,0:T(8,128)(2,1)S(1)}, bf16[128,1024]{1,0:T(8,128)(2,1)S(1)}, u32[]{:S(2)}, u32[]{:S(2)}) collective-permute-start(bf16[128,1024]{1,0:T(8,128)(2,1)S(1)} %pad_maximum_fusion.30), channel_id=1, source_target_pairs={{0,130},{1,129},{2,128},{3,131},{32,162},{33,161},{34,160},{35,163... | collective-permute-start | bytes 786440 | tf_op jit(solution)/shard_map/ppermute | solution.py:34
  110.1 11.9 %collective-permute-start.28 = (bf16[64,1024]{1,0:T(8,128)(2,1)S(1)}, bf16[64,1024]{1,0:T(8,128)(2,1)S(1)}, u32[]{:S(2)}, u32[]{:S(2)}) collective-permute-start(bf16[64,1024]{1,0:T(8,128)(2,1)S(1)} %get-tuple-element.143), channel_id=1, source_target_pairs={{0,2},{1,3},{2,0},{3,1},{32,34},{33,35},{34,32},{35,33},{64,66},{6... | collective-permute-start | bytes 393224 | tf_op jit(solution)/shard_map/ppermute | solution.py:34
  118.6 6.3 %collective-permute-start.29 = (bf16[64,1024]{1,0:T(8,128)(2,1)S(1)}, bf16[64,1024]{1,0:T(8,128)(2,1)S(1)}, u32[]{:S(2)}, u32[]{:S(2)}) collective-permute-start(bf16[64,1024]{1,0:T(8,128)(2,1)S(1)} %fusion.37), channel_id=1, source_target_pairs={{0,32},{1,97},{2,34},{3,99},{32,0},{33,65},{34,2},{35,67},{64,96},... | collective-permute-start | bytes 393224 | tf_op jit(solution)/shard_map/ppermute | solution.py:34
  122.0 5.0 %collective-permute-start.30 = (bf16[64,1024]{1,0:T(8,128)(2,1)S(1)}, bf16[64,1024]{1,0:T(8,128)(2,1)S(1)}, u32[]{:S(2)}, u32[]{:S(2)}) collective-permute-start(bf16[64,1024]{1,0:T(8,128)(2,1)S(1)} %add_convert_fusion.1), channel_id=1, source_target_pairs={{0,128},{1,131},{2,130},{3,129},{32,160},{33,163},{34,162},{35,161... | collective-permute-start | bytes 393224 | tf_op jit(solution)/shard_map/ppermute | solution.py:34
  (1 other events, 10.8 us)

commit v5 on v4

--- a/solution.py
+++ b/solution.py
@@ -144,7 +144,8 @@
         jnp.concatenate([top, top_far]),
         jnp.concatenate([low, low_far]),
     )
-    got, top_near, low_near = together(exchange(ring, 1), flip(top, "y", NEAR), flip(low, "x", NEAR))
+    got = exchange(ring, 1)
+    top_near, low_near = together(flip(top, "y", NEAR), flip(low, "x", NEAR))
     top, low = together(jnp.concatenate([top, top_near]), jnp.concatenate([low, low_near]))
     top_far, low_far = flip(top, "y", FAR), flip(low, "x", FAR)
     ring = [passage, passage_near, got[:rows], got[rows:]]
@@ -237,7 +238,7 @@
     passage_back = flip(passage_sum[half:], "y", (2, 2))
     top_last = flip((top[half:rows] + top_got[half:]).astype(bf16), "x", NEAR)
     low_last = flip((low_near + low_got[half:]).astype(bf16), "y", NEAR)
-    passage_back, top_last, low_last = together(passage_back, top_last, low_last)
+    top_last, low_last = together(top_last, low_last)
     passage_grad = jnp.where(
         yh == 0,
         jnp.concatenate([passage_own, passage_back]),

time: 129 us -> 128 us (level)
  waiting for transfers between devices: 54.3 us -> 52.6 us
  starting transfers between devices: 51 us -> 52.4 us
    ppermute x18, waiting for transfers between devices: 10.9 us -> 9.35 us  [flip(): return lax.ppermute(value, PLANE, pairs)]
  transfers between devices with their start and end apart: 31 -> 31, of which waited for: 16 -> 16; matrix products, arithmetic and copies ran while one was open for 8% -> 9% of each run, Pallas kernels for 0% -> 0%
where the time goes in v5:
time: 128 us
  waiting for transfers between devices  52.6 us (41%)
  starting transfers between devices  52.4 us (41%)
  other arithmetic  10.5 us (8%)
  matrix products  8.91 us (7%)
  Pallas kernels  1.97 us (2%)
    ppermute x18, starting transfers between devices, flip(): return lax.ppermute(value, PLANE, pairs)  33.6 us
    ppermute x4, waiting for transfers between devices, exchange(): return lax.ppermute(value, ('z', 'c'), pairs)  24.9 us
    ppermute x7, waiting for transfers between devices, shift(): return lax.ppermute(value, 'z', [(i, (i + step) % 8) for i in range(8)])  18 us
    ppermute x7, starting transfers between devices, shift(): return lax.ppermute(value, 'z', [(i, (i + step) % 8) for i in range(8)])  10.8 us
    ppermute x18, waiting for transfers between devices, flip(): return lax.ppermute(value, PLANE, pairs)  9.35 us
    dot_general x12, matrix products, dot(): lax.dot_general(a, b, (contract, ((), ())), preferred_element_type=f32)  8.91 us
    ppermute x4, starting transfers between devices, exchange(): return lax.ppermute(value, ('z', 'c'), pairs)  7.16 us
  transfers between devices with their start and end apart: 31, of which 16 were waited for; matrix products, arithmetic and copies ran while one was open for 9% of the time, Pallas kernels for 0%

profile of v5, /device:TPU:36, one launch (start us, length us, event | category | flops | bytes accessed | tf_op | source)
XLA Modules:
  0.0 128.3 jit_solution(7858662304919082477)
XLA Ops:
  0.6 2.0 %shard_map.77 = (bf16[64,1152]{1,0:T(8,128)(2,1)}, bf16[64,1152]{1,0:T(8,128)(2,1)}, bf16[64,1024]{1,0:T(8,128)(2,1)}, bf16[64,1024]{1,0:T(8,128)(2,1)}) custom-call(s32[1]{0:T(128)} %bitcast.scalar, bf16[128,1024]{1,0:T(8,128)(2,1)} %refs_0_.1, bf16[128,1024]{1,0:T(8,128)(2,1)} %refs_1_.1, f32[1,128]{1,0:T(1,128)} %bitcast.98, f32[1,128]{1,0:T(1,128)} %bitcast.99, ...), custom_call_target="tpu_custom_call" | custom-call | bytes 1082884 | tf_op jit(solution)/shard_map/pallas_call | solution.py:105
  2.6 1.3 %collective-permute-start.2 = (bf16[64,1152]{1,0:T(8,128)(2,1)}, bf16[64,1152]{1,0:T(8,128)(2,1)S(1)}, u32[]{:S(2)}, u32[]{:S(2)}) collective-permute-start(bf16[64,1152]{1,0:T(8,128)(2,1)} %get-tuple-element.44), channel_id=1, source_target_pairs={{0,32},{1,97},{2,34},{3,99},{32,0},{33,65},{34,2},{35,67},{64,96},... | collective-permute-start | bytes 442376 | tf_op jit(solution)/shard_map/ppermute | solution.py:34
  3.9 1.6 %collective-permute-start.3 = (bf16[64,1152]{1,0:T(8,128)(2,1)}, bf16[64,1152]{1,0:T(8,128)(2,1)S(1)}, u32[]{:S(2)}, u32[]{:S(2)}) collective-permute-start(bf16[64,1152]{1,0:T(8,128)(2,1)} %get-tuple-element.45), channel_id=1, source_target_pairs={{0,128},{1,131},{2,130},{3,129},{32,160},{33,163},{34,162},{35,161... | collective-permute-start | bytes 442376 | tf_op jit(solution)/shard_map/ppermute | solution.py:34
  5.5 2.9 %collective-permute-start = (bf16[64,1024]{1,0:T(8,128)(2,1)}, bf16[64,1024]{1,0:T(8,128)(2,1)S(1)}, u32[]{:S(2)}, u32[]{:S(2)}) collective-permute-start(bf16[64,1024]{1,0:T(8,128)(2,1)} %get-tuple-element.43), channel_id=1, source_target_pairs={{0,2},{1,3},{2,0},{3,1},{32,34},{33,35},{34,32},{35,33},{64,66},{6... | collective-permute-start | bytes 393224 | tf_op jit(solution)/shard_map/ppermute | solution.py:34
  8.4 2.0 %collective-permute-done.3 = bf16[64,1152]{1,0:T(8,128)(2,1)S(1)} collective-permute-done((bf16[64,1152]{1,0:T(8,128)(2,1)}, bf16[64,1152]{1,0:T(8,128)(2,1)S(1)}, u32[]{:S(2)}, u32[]{:S(2)}) %collective-permute-start.3) | collective-permute-done | bytes 147488 | tf_op jit(solution)/shard_map/ppermute | solution.py:34
  11.6 3.0 %collective-permute-start.5 = (bf16[128,1152]{1,0:T(8,128)(2,1)S(1)}, bf16[128,1152]{1,0:T(8,128)(2,1)S(1)}, u32[]{:S(2)}, u32[]{:S(2)}) collective-permute-start(bf16[128,1152]{1,0:T(8,128)(2,1)S(1)} %get-tuple-element.49), channel_id=1, source_target_pairs={{0,130},{1,129},{2,128},{3,131},{32,162},{33,161},{34,160},{35,163... | collective-permute-start | bytes 884744 | tf_op jit(solution)/shard_map/ppermute | solution.py:34
  15.8 6.3 %collective-permute-done.1 = bf16[128,1024]{1,0:T(8,128)(2,1)S(1)} collective-permute-done((bf16[128,1024]{1,0:T(8,128)(2,1)S(1)}, bf16[128,1024]{1,0:T(8,128)(2,1)S(1)}, u32[]{:S(2)}, u32[]{:S(2)}) %collective-permute-start.1) | collective-permute-done | bytes 262176 | tf_op jit(solution)/shard_map/ppermute | solution.py:43
  23.5 1.9 %collective-permute-start.9 = (bf16[256,1024]{1,0:T(8,128)(2,1)S(1)}, bf16[256,1024]{1,0:T(8,128)(2,1)}, u32[]{:S(2)}, u32[]{:S(2)}) collective-permute-start(bf16[256,1024]{1,0:T(8,128)(2,1)S(1)} %pad_maximum_fusion.24), channel_id=1, source_target_pairs={{0,28},{1,5},{4,8},{5,1},{8,4},{9,13},{12,16},{13,9},{16,12},{17,2... | collective-permute-start | bytes 1572872 | tf_op jit(solution)/shard_map/ppermute | solution.py:43
  25.5 7.3 %collective-permute-done.9 = bf16[256,1024]{1,0:T(8,128)(2,1)} collective-permute-done((bf16[256,1024]{1,0:T(8,128)(2,1)S(1)}, bf16[256,1024]{1,0:T(8,128)(2,1)}, u32[]{:S(2)}, u32[]{:S(2)}) %collective-permute-start.9) | collective-permute-done | bytes 524320 | tf_op jit(solution)/shard_map/ppermute | solution.py:43
  32.8 3.9 %collective-permute-start.10 = (bf16[256,1024]{1,0:T(8,128)(2,1)}, bf16[256,1024]{1,0:T(8,128)(2,1)S(1)}, u32[]{:S(2)}, u32[]{:S(2)}) collective-permute-start(bf16[256,1024]{1,0:T(8,128)(2,1)} %collective-permute-done.9), channel_id=1, source_target_pairs={{0,4},{1,29},{4,0},{5,9},{8,12},{9,5},{12,8},{13,17},{16,20},{17,1... | collective-permute-start | bytes 1572872 | tf_op jit(solution)/shard_map/ppermute | solution.py:43
  38.1 2.5 %collective-permute-start.13 = (bf16[512,1152]{1,0:T(8,128)(2,1)S(1)}, bf16[512,1152]{1,0:T(8,128)(2,1)S(1)}, u32[]{:S(2)}, u32[]{:S(2)}) collective-permute-start(bf16[512,1152]{1,0:T(8,128)(2,1)S(1)} %pad_maximum_fusion.1), channel_id=1, source_target_pairs={{0,96},{1,33},{2,98},{3,35},{32,64},{33,1},{34,66},{35,3},{64,32},... | collective-permute-start | bytes 3538952 | tf_op jit(solution)/shard_map/ppermute | solution.py:34
  40.6 3.5 %collective-permute-done.10 = bf16[256,1024]{1,0:T(8,128)(2,1)S(1)} collective-permute-done((bf16[256,1024]{1,0:T(8,128)(2,1)}, bf16[256,1024]{1,0:T(8,128)(2,1)S(1)}, u32[]{:S(2)}, u32[]{:S(2)}) %collective-permute-start.10) | collective-permute-done | bytes 524320 | tf_op jit(solution)/shard_map/ppermute | solution.py:43
  45.5 7.8 %collective-permute-done.11 = bf16[256,1024]{1,0:T(8,128)(2,1)S(1)} collective-permute-done((bf16[256,1024]{1,0:T(8,128)(2,1)S(1)}, bf16[256,1024]{1,0:T(8,128)(2,1)S(1)}, u32[]{:S(2)}, u32[]{:S(2)}) %collective-permute-start.11) | collective-permute-done | bytes 524320 | tf_op jit(solution)/shard_map/ppermute | solution.py:43
  68.6 1.2 collective-permute-start.15
  69.8 2.2 %collective-permute-start.16 = (bf16[128,1024]{1,0:T(8,128)(2,1)S(1)}, bf16[128,1024]{1,0:T(8,128)(2,1)S(1)}, u32[]{:S(2)}, u32[]{:S(2)}) collective-permute-start(bf16[128,1024]{1,0:T(8,128)(2,1)S(1)} %pad_maximum_fusion.29), channel_id=1, source_target_pairs={{0,28},{4,0},{8,4},{12,8},{16,12},{20,16},{24,20},{28,24},{1,29},{... | collective-permute-start | bytes 786440 | tf_op jit(solution)/shard_map/ppermute | solution.py:47
  73.6 2.7 %collective-permute-start.20 = (bf16[512,1024]{1,0:T(8,128)(2,1)S(1)}, bf16[512,1024]{1,0:T(8,128)(2,1)S(1)}, u32[]{:S(2)}, u32[]{:S(2)}) collective-permute-start(bf16[512,1024]{1,0:T(8,128)(2,1)S(1)} %bitcast.96), channel_id=1, source_target_pairs={{0,96},{1,33},{2,98},{3,35},{32,64},{33,1},{34,66},{35,3},{64,32},... | collective-permute-start | bytes 3145736 | tf_op jit(solution)/shard_map/ppermute | solution.py:34
  76.6 2.2 %collective-permute-done.15 = bf16[128,1024]{1,0:T(8,128)(2,1)S(1)} collective-permute-done((bf16[128,1024]{1,0:T(8,128)(2,1)S(1)}, bf16[128,1024]{1,0:T(8,128)(2,1)S(1)}, u32[]{:S(2)}, u32[]{:S(2)}) %collective-permute-start.15) | collective-permute-done | bytes 262176 | tf_op jit(solution)/shard_map/ppermute | solution.py:47
  79.9 3.2 %collective-permute-start.17 = (bf16[128,1024]{1,0:T(8,128)(2,1)S(1)}, bf16[128,1024]{1,0:T(8,128)(2,1)S(1)}, u32[]{:S(2)}, u32[]{:S(2)}) collective-permute-start(bf16[128,1024]{1,0:T(8,128)(2,1)S(1)} %fusion.26), channel_id=1, source_target_pairs={{0,4},{4,8},{8,12},{12,16},{16,20},{20,24},{24,28},{28,0},{1,5},{5... | collective-permute-start | bytes 786440 | tf_op jit(solution)/shard_map/ppermute | solution.py:47
  83.1 5.4 %collective-permute-done.17 = bf16[128,1024]{1,0:T(8,128)(2,1)S(1)} collective-permute-done((bf16[128,1024]{1,0:T(8,128)(2,1)S(1)}, bf16[128,1024]{1,0:T(8,128)(2,1)S(1)}, u32[]{:S(2)}, u32[]{:S(2)}) %collective-permute-start.17) | collective-permute-done | bytes 262176 | tf_op jit(solution)/shard_map/ppermute | solution.py:47
  88.5 2.9 %collective-permute-done.18 = bf16[128,1024]{1,0:T(8,128)(2,1)S(1)} collective-permute-done((bf16[128,1024]{1,0:T(8,128)(2,1)S(1)}, bf16[128,1024]{1,0:T(8,128)(2,1)S(1)}, u32[]{:S(2)}, u32[]{:S(2)}) %collective-permute-start.18) | collective-permute-done | bytes 262176 | tf_op jit(solution)/shard_map/ppermute | solution.py:47
  91.9 2.2 %collective-permute-start.21 = (bf16[256,1024]{1,0:T(8,128)(2,1)S(1)}, bf16[256,1024]{1,0:T(8,128)(2,1)S(1)}, u32[]{:S(2)}, u32[]{:S(2)}) collective-permute-start(bf16[256,1024]{1,0:T(8,128)(2,1)S(1)} %add_convert_fusion), channel_id=1, source_target_pairs={{0,128},{1,131},{2,130},{3,129},{32,160},{33,163},{34,162},{35,161... | collective-permute-start | bytes 1572872 | tf_op jit(solution)/shard_map/ppermute | solution.py:34
  95.1 1.8 %collective-permute-start.27 = (bf16[128,1024]{1,0:T(8,128)(2,1)S(1)}, bf16[128,1024]{1,0:T(8,128)(2,1)S(1)}, u32[]{:S(2)}, u32[]{:S(2)}) collective-permute-start(bf16[128,1024]{1,0:T(8,128)(2,1)S(1)} %fusion.32), channel_id=1, source_target_pairs={{0,4},{4,8},{8,12},{12,16},{16,20},{20,24},{24,28},{28,0},{1,5},{5... | collective-permute-start | bytes 786440 | tf_op jit(solution)/shard_map/ppermute | solution.py:47
  97.2 4.8 %collective-permute-done.27 = bf16[128,1024]{1,0:T(8,128)(2,1)S(1)} collective-permute-done((bf16[128,1024]{1,0:T(8,128)(2,1)S(1)}, bf16[128,1024]{1,0:T(8,128)(2,1)S(1)}, u32[]{:S(2)}, u32[]{:S(2)}) %collective-permute-start.27) | collective-permute-done | bytes 262176 | tf_op jit(solution)/shard_map/ppermute | solution.py:47
  102.0 1.5 %collective-permute-done.28 = bf16[128,1024]{1,0:T(8,128)(2,1)S(1)} collective-permute-done((bf16[128,1024]{1,0:T(8,128)(2,1)S(1)}, bf16[128,1024]{1,0:T(8,128)(2,1)S(1)}, u32[]{:S(2)}, u32[]{:S(2)}) %collective-permute-start.28) | collective-permute-done | bytes 262176 | tf_op jit(solution)/shard_map/ppermute | solution.py:47
  103.5 2.1 %collective-permute-start.29 = (bf16[128,1024]{1,0:T(8,128)(2,1)S(1)}, bf16[128,1024]{1,0:T(8,128)(2,1)S(1)}, u32[]{:S(2)}, u32[]{:S(2)}) collective-permute-start(bf16[128,1024]{1,0:T(8,128)(2,1)S(1)} %fusion.31), channel_id=1, source_target_pairs={{0,4},{4,8},{8,12},{12,16},{16,20},{20,24},{24,28},{28,0},{1,5},{5... | collective-permute-start | bytes 786440 | tf_op jit(solution)/shard_map/ppermute | solution.py:47
  106.2 1.8 %collective-permute-start.23 = (bf16[128,1024]{1,0:T(8,128)(2,1)S(1)}, bf16[128,1024]{1,0:T(8,128)(2,1)S(1)}, u32[]{:S(2)}, u32[]{:S(2)}) collective-permute-start(bf16[128,1024]{1,0:T(8,128)(2,1)S(1)} %slice.661), channel_id=1, source_target_pairs={{0,96},{1,33},{2,98},{3,35},{32,64},{33,1},{34,66},{35,3},{64,32},... | collective-permute-start | bytes 786440 | tf_op jit(solution)/shard_map/ppermute | solution.py:34
  108.0 1.7 %collective-permute-start.24 = (bf16[128,1024]{1,0:T(8,128)(2,1)S(1)}, bf16[128,1024]{1,0:T(8,128)(2,1)S(1)}, u32[]{:S(2)}, u32[]{:S(2)}) collective-permute-start(bf16[128,1024]{1,0:T(8,128)(2,1)S(1)} %pad_maximum_fusion.30), channel_id=1, source_target_pairs={{0,130},{1,129},{2,128},{3,131},{32,162},{33,161},{34,160},{35,163... | collective-permute-start | bytes 786440 | tf_op jit(solution)/shard_map/ppermute | solution.py:34
  110.1 5.2 %collective-permute-start.30 = (bf16[64,1024]{1,0:T(8,128)(2,1)S(1)}, bf16[64,1024]{1,0:T(8,128)(2,1)S(1)}, u32[]{:S(2)}, u32[]{:S(2)}) collective-permute-start(bf16[64,1024]{1,0:T(8,128)(2,1)S(1)} %get-tuple-element.139), channel_id=1, source_target_pairs={{0,2},{1,3},{2,0},{3,1},{32,34},{33,35},{34,32},{35,33},{64,66},{6... | collective-permute-start | bytes 393224 | tf_op jit(solution)/shard_map/ppermute | solution.py:34
  115.3 3.1 %collective-permute-done.24 = bf16[128,1024]{1,0:T(8,128)(2,1)S(1)} collective-permute-done((bf16[128,1024]{1,0:T(8,128)(2,1)S(1)}, bf16[128,1024]{1,0:T(8,128)(2,1)S(1)}, u32[]{:S(2)}, u32[]{:S(2)}) %collective-permute-start.24) | collective-permute-done | bytes 262176 | tf_op jit(solution)/shard_map/ppermute | solution.py:34
  118.4 4.1 %collective-permute-start.25 = (bf16[64,1024]{1,0:T(8,128)(2,1)S(1)}, bf16[64,1024]{1,0:T(8,128)(2,1)S(1)}, u32[]{:S(2)}, u32[]{:S(2)}) collective-permute-start(bf16[64,1024]{1,0:T(8,128)(2,1)S(1)} %fusion.37), channel_id=1, source_target_pairs={{0,32},{1,97},{2,34},{3,99},{32,0},{33,65},{34,2},{35,67},{64,96},... | collective-permute-start | bytes 393224 | tf_op jit(solution)/shard_map/ppermute | solution.py:34
  123.3 2.2 %collective-permute-done.25 = bf16[64,1024]{1,0:T(8,128)(2,1)S(1)} collective-permute-done((bf16[64,1024]{1,0:T(8,128)(2,1)S(1)}, bf16[64,1024]{1,0:T(8,128)(2,1)S(1)}, u32[]{:S(2)}, u32[]{:S(2)}) %collective-permute-start.25) | collective-permute-done | bytes 131104 | tf_op jit(solution)/shard_map/ppermute | solution.py:34
  125.5 2.0 %collective-permute-done.26 = bf16[64,1024]{1,0:T(8,128)(2,1)S(1)} collective-permute-done((bf16[64,1024]{1,0:T(8,128)(2,1)S(1)}, bf16[64,1024]{1,0:T(8,128)(2,1)S(1)}, u32[]{:S(2)}, u32[]{:S(2)}) %collective-permute-start.26) | collective-permute-done | bytes 131104 | tf_op jit(solution)/shard_map/ppermute | solution.py:34
  (112 shorter events, 28.7 us)
Async XLA Ops:
  2.6 19.5 %copy-start = (bf16[64,1024]{1,0:T(8,128)(2,1)S(1)}, bf16[64,1024]{1,0:T(8,128)(2,1)}, u32[]{:S(2)}) copy-start(bf16[64,1024]{1,0:T(8,128)(2,1)} %get-tuple-element.42) | copy-start | bytes 393220
  2.6 5.8 %collective-permute-start.2 = (bf16[64,1152]{1,0:T(8,128)(2,1)}, bf16[64,1152]{1,0:T(8,128)(2,1)S(1)}, u32[]{:S(2)}, u32[]{:S(2)}) collective-permute-start(bf16[64,1152]{1,0:T(8,128)(2,1)} %get-tuple-element.44), channel_id=1, source_target_pairs={{0,32},{1,97},{2,34},{3,99},{32,0},{33,65},{34,2},{35,67},{64,96},... | collective-permute-start | bytes 442376 | tf_op jit(solution)/shard_map/ppermute | solution.py:34
  3.9 6.5 %collective-permute-start.3 = (bf16[64,1152]{1,0:T(8,128)(2,1)}, bf16[64,1152]{1,0:T(8,128)(2,1)S(1)}, u32[]{:S(2)}, u32[]{:S(2)}) collective-permute-start(bf16[64,1152]{1,0:T(8,128)(2,1)} %get-tuple-element.45), channel_id=1, source_target_pairs={{0,128},{1,131},{2,130},{3,129},{32,160},{33,163},{34,162},{35,161... | collective-permute-start | bytes 442376 | tf_op jit(solution)/shard_map/ppermute | solution.py:34
  5.5 9.1 %collective-permute-start = (bf16[64,1024]{1,0:T(8,128)(2,1)}, bf16[64,1024]{1,0:T(8,128)(2,1)S(1)}, u32[]{:S(2)}, u32[]{:S(2)}) collective-permute-start(bf16[64,1024]{1,0:T(8,128)(2,1)} %get-tuple-element.43), channel_id=1, source_target_pairs={{0,2},{1,3},{2,0},{3,1},{32,34},{33,35},{34,32},{35,33},{64,66},{6... | collective-permute-start | bytes 393224 | tf_op jit(solution)/shard_map/ppermute | solution.py:34
  11.5 10.5 %collective-permute-start.4 = (bf16[128,1152]{1,0:T(8,128)(2,1)S(1)}, bf16[128,1152]{1,0:T(8,128)(2,1)S(1)}, u32[]{:S(2)}, u32[]{:S(2)}) collective-permute-start(bf16[128,1152]{1,0:T(8,128)(2,1)S(1)} %get-tuple-element.48), channel_id=1, source_target_pairs={{0,96},{1,33},{2,98},{3,35},{32,64},{33,1},{34,66},{35,3},{64,32},... | collective-permute-start | bytes 884744 | tf_op jit(solution)/shard_map/ppermute | solution.py:34
  11.6 10.4 %collective-permute-start.5 = (bf16[128,1152]{1,0:T(8,128)(2,1)S(1)}, bf16[128,1152]{1,0:T(8,128)(2,1)S(1)}, u32[]{:S(2)}, u32[]{:S(2)}) collective-permute-start(bf16[128,1152]{1,0:T(8,128)(2,1)S(1)} %get-tuple-element.49), channel_id=1, source_target_pairs={{0,130},{1,129},{2,128},{3,131},{32,162},{33,161},{34,160},{35,163... | collective-permute-start | bytes 884744 | tf_op jit(solution)/shard_map/ppermute | solution.py:34
  15.6 6.5 %collective-permute-start.1 = (bf16[128,1024]{1,0:T(8,128)(2,1)S(1)}, bf16[128,1024]{1,0:T(8,128)(2,1)S(1)}, u32[]{:S(2)}, u32[]{:S(2)}) collective-permute-start(bf16[128,1024]{1,0:T(8,128)(2,1)S(1)} %pad_maximum_fusion.27), channel_id=1, source_target_pairs={{0,4},{1,29},{4,0},{5,9},{8,12},{9,5},{12,8},{13,17},{16,20},{17,1... | collective-permute-start | bytes 786440 | tf_op jit(solution)/shard_map/ppermute | solution.py:43
  22.2 14.6 %collective-permute-start.6 = (bf16[256,1152]{1,0:T(8,128)(2,1)S(1)}, bf16[256,1152]{1,0:T(8,128)(2,1)S(1)}, u32[]{:S(2)}, u32[]{:S(2)}) collective-permute-start(bf16[256,1152]{1,0:T(8,128)(2,1)S(1)} %pad_maximum_fusion.18), channel_id=1, source_target_pairs={{0,128},{1,131},{2,130},{3,129},{32,160},{33,163},{34,162},{35,161... | collective-permute-start | bytes 1769480 | tf_op jit(solution)/shard_map/ppermute | solution.py:34
  22.4 14.4 %collective-permute-start.7 = (bf16[256,1152]{1,0:T(8,128)(2,1)S(1)}, bf16[256,1152]{1,0:T(8,128)(2,1)S(1)}, u32[]{:S(2)}, u32[]{:S(2)}) collective-permute-start(bf16[256,1152]{1,0:T(8,128)(2,1)S(1)} %pad_maximum_fusion.19), channel_id=1, source_target_pairs={{0,32},{1,97},{2,34},{3,99},{32,0},{33,65},{34,2},{35,67},{64,96},... | collective-permute-start | bytes 1769480 | tf_op jit(solution)/shard_map/ppermute | solution.py:34
  23.5 9.3 %collective-permute-start.9 = (bf16[256,1024]{1,0:T(8,128)(2,1)S(1)}, bf16[256,1024]{1,0:T(8,128)(2,1)}, u32[]{:S(2)}, u32[]{:S(2)}) collective-permute-start(bf16[256,1024]{1,0:T(8,128)(2,1)S(1)} %pad_maximum_fusion.24), channel_id=1, source_target_pairs={{0,28},{1,5},{4,8},{5,1},{8,4},{9,13},{12,16},{13,9},{16,12},{17,2... | collective-permute-start | bytes 1572872 | tf_op jit(solution)/shard_map/ppermute | solution.py:43
  32.8 11.3 %collective-permute-start.10 = (bf16[256,1024]{1,0:T(8,128)(2,1)}, bf16[256,1024]{1,0:T(8,128)(2,1)S(1)}, u32[]{:S(2)}, u32[]{:S(2)}) collective-permute-start(bf16[256,1024]{1,0:T(8,128)(2,1)} %collective-permute-done.9), channel_id=1, source_target_pairs={{0,4},{1,29},{4,0},{5,9},{8,12},{9,5},{12,8},{13,17},{16,20},{17,1... | collective-permute-start | bytes 1572872 | tf_op jit(solution)/shard_map/ppermute | solution.py:43
  37.0 17.7 %collective-permute-start.8 = (bf16[512,1152]{1,0:T(8,128)(2,1)S(1)}, bf16[512,1152]{1,0:T(8,128)(2,1)S(1)}, u32[]{:S(2)}, u32[]{:S(2)}) collective-permute-start(bf16[512,1152]{1,0:T(8,128)(2,1)S(1)} %pad_maximum_fusion), channel_id=1, source_target_pairs={{0,130},{1,129},{2,128},{3,131},{32,162},{33,161},{34,160},{35,163... | collective-permute-start | bytes 3538952 | tf_op jit(solution)/shard_map/ppermute | solution.py:34
  38.1 18.4 %collective-permute-start.13 = (bf16[512,1152]{1,0:T(8,128)(2,1)S(1)}, bf16[512,1152]{1,0:T(8,128)(2,1)S(1)}, u32[]{:S(2)}, u32[]{:S(2)}) collective-permute-start(bf16[512,1152]{1,0:T(8,128)(2,1)S(1)} %pad_maximum_fusion.1), channel_id=1, source_target_pairs={{0,96},{1,33},{2,98},{3,35},{32,64},{33,1},{34,66},{35,3},{64,32},... | collective-permute-start | bytes 3538952 | tf_op jit(solution)/shard_map/ppermute | solution.py:34
  44.1 9.2 %collective-permute-start.11 = (bf16[256,1024]{1,0:T(8,128)(2,1)S(1)}, bf16[256,1024]{1,0:T(8,128)(2,1)S(1)}, u32[]{:S(2)}, u32[]{:S(2)}) collective-permute-start(bf16[256,1024]{1,0:T(8,128)(2,1)S(1)} %collective-permute-done.10), channel_id=1, source_target_pairs={{0,28},{1,5},{4,8},{5,1},{8,4},{9,13},{12,16},{13,9},{16,12},{17,2... | collective-permute-start | bytes 1572872 | tf_op jit(solution)/shard_map/ppermute | solution.py:43
  56.4 4.4 %collective-permute-start.12 = (f32[512,512]{1,0:T(8,128)S(1)}, f32[512,512]{1,0:T(8,128)S(1)}, u32[]{:S(2)}, u32[]{:S(2)}) collective-permute-start(f32[512,512]{1,0:T(8,128)S(1)} %convolution_add_fusion.3), channel_id=1, source_target_pairs={{0,1},{1,0},{2,3},{3,2},{4,5},{5,4},{6,7},{7,6},{8,9},{9,8},{10,11... | collective-permute-start | bytes 3145736 | tf_op jit(solution)/shard_map/ppermute | solution.py:187
  58.2 3.0 %collective-permute-start.14 = (f32[512,512]{1,0:T(8,128)S(1)}, f32[512,512]{1,0:T(8,128)S(1)}, u32[]{:S(2)}, u32[]{:S(2)}) collective-permute-start(f32[512,512]{1,0:T(8,128)S(1)} %convolution_add_fusion.2), channel_id=1, source_target_pairs={{0,1},{1,0},{2,3},{3,2},{4,5},{5,4},{6,7},{7,6},{8,9},{9,8},{10,11... | collective-permute-start | bytes 3145736 | tf_op jit(solution)/shard_map/ppermute | solution.py:187
  68.6 10.2 %collective-permute-start.15 = (bf16[128,1024]{1,0:T(8,128)(2,1)S(1)}, bf16[128,1024]{1,0:T(8,128)(2,1)S(1)}, u32[]{:S(2)}, u32[]{:S(2)}) collective-permute-start(bf16[128,1024]{1,0:T(8,128)(2,1)S(1)} %pad_maximum_fusion.28), channel_id=1, source_target_pairs={{0,4},{4,8},{8,12},{12,16},{16,20},{20,24},{24,28},{28,0},{1,5},{5... | collective-permute-start | bytes 786440 | tf_op jit(solution)/shard_map/ppermute | solution.py:47
  69.8 9.9 %collective-permute-start.16 = (bf16[128,1024]{1,0:T(8,128)(2,1)S(1)}, bf16[128,1024]{1,0:T(8,128)(2,1)S(1)}, u32[]{:S(2)}, u32[]{:S(2)}) collective-permute-start(bf16[128,1024]{1,0:T(8,128)(2,1)S(1)} %pad_maximum_fusion.29), channel_id=1, source_target_pairs={{0,28},{4,0},{8,4},{12,8},{16,12},{20,16},{24,20},{28,24},{1,29},{... | collective-permute-start | bytes 786440 | tf_op jit(solution)/shard_map/ppermute | solution.py:47
  72.3 19.1 %collective-permute-start.19 = (bf16[512,1024]{1,0:T(8,128)(2,1)S(1)}, bf16[512,1024]{1,0:T(8,128)(2,1)S(1)}, u32[]{:S(2)}, u32[]{:S(2)}) collective-permute-start(bf16[512,1024]{1,0:T(8,128)(2,1)S(1)} %pad_maximum_fusion.9), channel_id=1, source_target_pairs={{0,130},{1,129},{2,128},{3,131},{32,162},{33,161},{34,160},{35,163... | collective-permute-start | bytes 3145736 | tf_op jit(solution)/shard_map/ppermute | solution.py:34
  73.6 17.9 %collective-permute-start.20 = (bf16[512,1024]{1,0:T(8,128)(2,1)S(1)}, bf16[512,1024]{1,0:T(8,128)(2,1)S(1)}, u32[]{:S(2)}, u32[]{:S(2)}) collective-permute-start(bf16[512,1024]{1,0:T(8,128)(2,1)S(1)} %bitcast.96), channel_id=1, source_target_pairs={{0,96},{1,33},{2,98},{3,35},{32,64},{33,1},{34,66},{35,3},{64,32},... | collective-permute-start | bytes 3145736 | tf_op jit(solution)/shard_map/ppermute | solution.py:34
  79.9 8.6 %collective-permute-start.17 = (bf16[128,1024]{1,0:T(8,128)(2,1)S(1)}, bf16[128,1024]{1,0:T(8,128)(2,1)S(1)}, u32[]{:S(2)}, u32[]{:S(2)}) collective-permute-start(bf16[128,1024]{1,0:T(8,128)(2,1)S(1)} %fusion.26), channel_id=1, source_target_pairs={{0,4},{4,8},{8,12},{12,16},{16,20},{20,24},{24,28},{28,0},{1,5},{5... | collective-permute-start | bytes 786440 | tf_op jit(solution)/shard_map/ppermute | solution.py:47
  83.1 8.4 %collective-permute-start.18 = (bf16[128,1024]{1,0:T(8,128)(2,1)S(1)}, bf16[128,1024]{1,0:T(8,128)(2,1)S(1)}, u32[]{:S(2)}, u32[]{:S(2)}) collective-permute-start(bf16[128,1024]{1,0:T(8,128)(2,1)S(1)} %fusion.27), channel_id=1, source_target_pairs={{0,28},{4,0},{8,4},{12,8},{16,12},{20,16},{24,20},{28,24},{1,29},{... | collective-permute-start | bytes 786440 | tf_op jit(solution)/shard_map/ppermute | solution.py:47
  91.9 13.7 %collective-permute-start.21 = (bf16[256,1024]{1,0:T(8,128)(2,1)S(1)}, bf16[256,1024]{1,0:T(8,128)(2,1)S(1)}, u32[]{:S(2)}, u32[]{:S(2)}) collective-permute-start(bf16[256,1024]{1,0:T(8,128)(2,1)S(1)} %add_convert_fusion), channel_id=1, source_target_pairs={{0,128},{1,131},{2,130},{3,129},{32,160},{33,163},{34,162},{35,161... | collective-permute-start | bytes 1572872 | tf_op jit(solution)/shard_map/ppermute | solution.py:34
  94.1 11.5 %collective-permute-start.22 = (bf16[256,1024]{1,0:T(8,128)(2,1)S(1)}, bf16[256,1024]{1,0:T(8,128)(2,1)S(1)}, u32[]{:S(2)}, u32[]{:S(2)}) collective-permute-start(bf16[256,1024]{1,0:T(8,128)(2,1)S(1)} %fusion.5), channel_id=1, source_target_pairs={{0,32},{1,97},{2,34},{3,99},{32,0},{33,65},{34,2},{35,67},{64,96},... | collective-permute-start | bytes 1572872 | tf_op jit(solution)/shard_map/ppermute | solution.py:34
  95.1 6.9 %collective-permute-start.27 = (bf16[128,1024]{1,0:T(8,128)(2,1)S(1)}, bf16[128,1024]{1,0:T(8,128)(2,1)S(1)}, u32[]{:S(2)}, u32[]{:S(2)}) collective-permute-start(bf16[128,1024]{1,0:T(8,128)(2,1)S(1)} %fusion.32), channel_id=1, source_target_pairs={{0,4},{4,8},{8,12},{12,16},{16,20},{20,24},{24,28},{28,0},{1,5},{5... | collective-permute-start | bytes 786440 | tf_op jit(solution)/shard_map/ppermute | solution.py:47
  96.9 6.5 %collective-permute-start.28 = (bf16[128,1024]{1,0:T(8,128)(2,1)S(1)}, bf16[128,1024]{1,0:T(8,128)(2,1)S(1)}, u32[]{:S(2)}, u32[]{:S(2)}) collective-permute-start(bf16[128,1024]{1,0:T(8,128)(2,1)S(1)} %fusion.33), channel_id=1, source_target_pairs={{0,28},{4,0},{8,4},{12,8},{16,12},{20,16},{24,20},{28,24},{1,29},{... | collective-permute-start | bytes 786440 | tf_op jit(solution)/shard_map/ppermute | solution.py:47
  103.5 6.4 %collective-permute-start.29 = (bf16[128,1024]{1,0:T(8,128)(2,1)S(1)}, bf16[128,1024]{1,0:T(8,128)(2,1)S(1)}, u32[]{:S(2)}, u32[]{:S(2)}) collective-permute-start(bf16[128,1024]{1,0:T(8,128)(2,1)S(1)} %fusion.31), channel_id=1, source_target_pairs={{0,4},{4,8},{8,12},{12,16},{16,20},{20,24},{24,28},{28,0},{1,5},{5... | collective-permute-start | bytes 786440 | tf_op jit(solution)/shard_map/ppermute | solution.py:47
  106.2 9.1 %collective-permute-start.23 = (bf16[128,1024]{1,0:T(8,128)(2,1)S(1)}, bf16[128,1024]{1,0:T(8,128)(2,1)S(1)}, u32[]{:S(2)}, u32[]{:S(2)}) collective-permute-start(bf16[128,1024]{1,0:T(8,128)(2,1)S(1)} %slice.661), channel_id=1, source_target_pairs={{0,96},{1,33},{2,98},{3,35},{32,64},{33,1},{34,66},{35,3},{64,32},... | collective-permute-start | bytes 786440 | tf_op jit(solution)/shard_map/ppermute | solution.py:34
  108.0 10.4 %collective-permute-start.24 = (bf16[128,1024]{1,0:T(8,128)(2,1)S(1)}, bf16[128,1024]{1,0:T(8,128)(2,1)S(1)}, u32[]{:S(2)}, u32[]{:S(2)}) collective-permute-start(bf16[128,1024]{1,0:T(8,128)(2,1)S(1)} %pad_maximum_fusion.30), channel_id=1, source_target_pairs={{0,130},{1,129},{2,128},{3,131},{32,162},{33,161},{34,160},{35,163... | collective-permute-start | bytes 786440 | tf_op jit(solution)/shard_map/ppermute | solution.py:34
  110.1 12.4 %collective-permute-start.30 = (bf16[64,1024]{1,0:T(8,128)(2,1)S(1)}, bf16[64,1024]{1,0:T(8,128)(2,1)S(1)}, u32[]{:S(2)}, u32[]{:S(2)}) collective-permute-start(bf16[64,1024]{1,0:T(8,128)(2,1)S(1)} %get-tuple-element.139), channel_id=1, source_target_pairs={{0,2},{1,3},{2,0},{3,1},{32,34},{33,35},{34,32},{35,33},{64,66},{6... | collective-permute-start | bytes 393224 | tf_op jit(solution)/shard_map/ppermute | solution.py:34
  118.4 7.0 %collective-permute-start.25 = (bf16[64,1024]{1,0:T(8,128)(2,1)S(1)}, bf16[64,1024]{1,0:T(8,128)(2,1)S(1)}, u32[]{:S(2)}, u32[]{:S(2)}) collective-permute-start(bf16[64,1024]{1,0:T(8,128)(2,1)S(1)} %fusion.37), channel_id=1, source_target_pairs={{0,32},{1,97},{2,34},{3,99},{32,0},{33,65},{34,2},{35,67},{64,96},... | collective-permute-start | bytes 393224 | tf_op jit(solution)/shard_map/ppermute | solution.py:34
  122.5 5.0 %collective-permute-start.26 = (bf16[64,1024]{1,0:T(8,128)(2,1)S(1)}, bf16[64,1024]{1,0:T(8,128)(2,1)S(1)}, u32[]{:S(2)}, u32[]{:S(2)}) collective-permute-start(bf16[64,1024]{1,0:T(8,128)(2,1)S(1)} %add_convert_fusion.1), channel_id=1, source_target_pairs={{0,128},{1,131},{2,130},{3,129},{32,160},{33,163},{34,162},{35,161... | collective-permute-start | bytes 393224 | tf_op jit(solution)/shard_map/ppermute | solution.py:34
  (1 other events, 10.8 us)
